TPU v7x, 32 devices: a whole 2x2x4 slice. The times are simulated.
32 devices in a mesh: dp: 2 (over core), seq: 16 (over z, y, x).
Axes of the slice: x: 2, y: 2, z: 4, core: 2. Of those that a mesh axis runs over, the one named last changes fastest.
Arguments:
- inputs: bfloat16 [2, 9216, 512], P('dp', 'seq'), may hold values from -6 to 6
- doc_bounds: int32 [2, 2], P('dp'), may hold values from 1 to 3071, as said below
- pool_weight: bfloat16 [1536, 512], replicated, may hold values from -0.15625 to 0.15625
- pool_bias: float32 [512], replicated, may hold values from -1.75 to 1.75
- ln1_gain: float32 [512], replicated, may hold values from 0.5 to 1.5
- ln1_bias: float32 [512], replicated, may hold values from -1.75 to 1.75
- query_weight: bfloat16 [512, 512], replicated, may hold values from -0.25 to 0.25
- key_weight: bfloat16 [512, 512], replicated, may hold values from -0.25 to 0.25
- value_weight: bfloat16 [512, 512], replicated, may hold values from -0.25 to 0.25
- out_weight: bfloat16 [512, 512], replicated, may hold values from -6 to 6
- pos_weight: bfloat16 [512, 512], replicated, may hold values from -0.25 to 0.25
- content_bias: float32 [512], replicated, may hold values from -6 to 6
- pos_bias: float32 [512], replicated, may hold values from -6 to 6
- ln2_gain: float32 [512], replicated, may hold values from 0.5 to 1.5
- ln2_bias: float32 [512], replicated, may hold values from -1.75 to 1.75
- ffn_in: bfloat16 [512, 2048], replicated, may hold values from -0.25 to 0.25
- ffn_in_bias: float32 [2048], replicated, may hold values from -1.75 to 1.75
- ffn_out: bfloat16 [2048, 512], replicated, may hold values from -0.125 to 0.125
- ffn_out_bias: float32 [512], replicated, may hold values from -1.75 to 1.75
- up_weight: bfloat16 [512, 1536], replicated, may hold values from -0.25 to 0.25
- up_bias: float32 [1536], replicated, may hold values from -1.75 to 1.75
- cotangent: bfloat16 [2, 9216, 512], P('dp', 'seq'), may hold values from -6 to 6
Outputs:
- outputs: bfloat16 [2, 9216, 512], P('dp', 'seq')
- input_grad: bfloat16 [2, 9216, 512], P('dp', 'seq')
- grad_pool_weight: float32 [1536, 512], replicated
- grad_pool_bias: float32 [512], replicated
- grad_ln1_gain: float32 [512], replicated
- grad_ln1_bias: float32 [512], replicated
- grad_query_weight: float32 [512, 512], replicated
- grad_key_weight: float32 [512, 512], replicated
- grad_value_weight: float32 [512, 512], replicated
- grad_out_weight: float32 [512, 512], replicated
- grad_pos_weight: float32 [512, 512], replicated
- grad_content_bias: float32 [512], replicated
- grad_pos_bias: float32 [512], replicated
- grad_ln2_gain: float32 [512], replicated
- grad_ln2_bias: float32 [512], replicated
- grad_ffn_in: float32 [512, 2048], replicated
- grad_ffn_in_bias: float32 [2048], replicated
- grad_ffn_out: float32 [2048, 512], replicated
- grad_ffn_out_bias: float32 [512], replicated
- grad_up_weight: float32 [512, 1536], replicated
- grad_up_bias: float32 [1536], replicated
Inputs may be any that keep to these rules, and one draw needn't show every extreme that they name: `doc_bounds`: each row holds three packed documents: the second begins inside the first 192 shortened positions and the third inside the last 192, so the second spans every block of the row.
All inputs are finite; a program needn't handle non-finite values.
Results may differ from a plain program's by a relative error of at most 0.015.
Values may be sent and summed in bfloat16 or wider, within the bound.
A program may use at most 320 MiB of HBM per device.

v0:
```python
import jax
import jax.numpy as jnp
from jax import lax
from jax.sharding import PartitionSpec as P

HEADS = 8


epsilon = 1e-05
masked_score = -1e30


def passed_along(value, axis, steps):
    count = lax.axis_size(axis)
    first, last = (max(0, -steps), min(count, count - steps))
    return lax.ppermute(value, axis, [(source, source + steps) for source in range(first, last)])


def doc_index(positions, bounds):
    return (positions >= bounds[:, 0:1]).astype(jnp.int32) + (positions >= bounds[:, 1:2]).astype(
        jnp.int32
    )


def angles(positions, model_width):
    half_width = model_width // 2
    rates = 10000.0 ** (-2.0 * jnp.arange(half_width, dtype=jnp.float32) / model_width)
    phase = positions.astype(jnp.float32)[:, None] * rates[None, :]
    return (jnp.sin(phase), jnp.cos(phase))


def skew(full, width):
    count = full.shape[-2]
    amounts = count - 1 - jnp.arange(count, dtype=jnp.int32)
    current = full
    for level in range(max(count - 1, 1).bit_length()):
        step_len = 1 << level
        moved = jnp.concatenate(
            [current[..., step_len:], jnp.zeros_like(current[..., :step_len])], -1
        )
        taken = amounts >> level & 1 == 1
        current = jnp.where(taken[:, None], moved, current)
    return current[..., :width]


def unskew(grad, span):
    lead = grad.shape[:-2]
    count, width = (grad.shape[-2], grad.shape[-1])
    amounts = count - 1 - jnp.arange(count, dtype=jnp.int32)
    current = jnp.pad(grad, [(0, 0)] * len(lead) + [(0, 0), (0, span - width)])
    for level in range(max(count - 1, 1).bit_length()):
        step_len = 1 << level
        moved = jnp.concatenate(
            [jnp.zeros_like(current[..., :step_len]), current[..., : span - step_len]], -1
        )
        taken = amounts >> level & 1 == 1
        current = jnp.where(taken[:, None], moved, current)
    return current


def layer_norm(hidden, gain, bias):
    average = jnp.mean(hidden, -1, keepdims=True)
    centred = hidden - average
    inverse = lax.rsqrt(jnp.mean(centred * centred, -1, keepdims=True) + epsilon)
    normed = centred * inverse
    return (normed * gain + bias, normed, inverse)


def norm_back(grad_out, normed, inverse, gain):
    scaled = grad_out * gain
    grad_in = inverse * (
        scaled
        - jnp.mean(scaled, -1, keepdims=True)
        - normed * jnp.mean(scaled * normed, -1, keepdims=True)
    )
    return (grad_in, jnp.sum(grad_out * normed, axis=(0, 1)), jnp.sum(grad_out, axis=(0, 1)))


def exact_gelu(value):
    return jax.nn.gelu(value, approximate=False)


def in_blocks(worker, running, arrays, dims):
    length = arrays[0].shape[dims[0]]
    block_len = 512
    block_count = length // block_len
    stacked = tuple(
        (
            jnp.moveaxis(
                array.reshape(
                    array.shape[:dim] + (block_count, block_len) + array.shape[dim + 1 :]
                ),
                dim,
                0,
            )
            for array, dim in zip(arrays, dims)
        )
    )

    def advance(state, element):
        return worker(state, element[0], element[1] * block_len)

    running, results = lax.scan(
        advance, running, (stacked, jnp.arange(block_count, dtype=jnp.int32))
    )
    results = jax.tree.map(
        lambda result: jnp.moveaxis(result, 0, 1).reshape(
            (result.shape[1], block_count * block_len) + result.shape[3:]
        ),
        results,
    )
    return (running, results)


def pair_scores(query_arrays, query_anchor, key_arrays, key_anchor, context):
    rev_table, bounds, score_scale, total_tokens = context
    query_u, query_v = (query_arrays[0], query_arrays[1])
    key_rows = key_arrays[0]
    rows_here, query_len, head_count, head_size = query_u.shape
    key_len = key_rows.shape[1]
    query_places = query_anchor + jnp.arange(query_len, dtype=jnp.int32)
    key_places = key_anchor + jnp.arange(key_len, dtype=jnp.int32)
    query_docs = doc_index(query_places[None, :], bounds)
    key_docs = doc_index(key_places[None, :], bounds)
    split_keys = key_rows.reshape(rows_here, key_len, head_count, head_size)
    content = jnp.einsum("rthe,rshe->rhts", query_u, split_keys, preferred_element_type=jnp.float32)
    span = query_len + key_len - 1
    start = total_tokens - query_len - query_anchor + key_anchor
    window = lax.dynamic_slice_in_dim(rev_table, start, span, 0)
    position = skew(
        jnp.einsum("rthe,khe->rhtk", query_v, window, preferred_element_type=jnp.float32), key_len
    )
    allowed = (key_places[None, None, :] <= query_places[None, :, None]) & (
        key_docs[:, None, :] == query_docs[:, :, None]
    )
    allowed = allowed[:, None, :, :]
    score = jnp.where(allowed, (content + position) * score_scale, masked_score)
    return (score, allowed, split_keys, window, start)


def pair_grads(query_arrays, query_anchor, key_arrays, key_anchor, context):
    score, allowed, split_keys, window, start = pair_scores(
        query_arrays, query_anchor, key_arrays, key_anchor, context
    )
    query_u, query_v, grad_attended, log_total, delta = query_arrays
    prob = jnp.where(allowed, jnp.exp(score - log_total[..., None]), 0.0)
    split_values = key_arrays[1].reshape(split_keys.shape)
    grad_prob = jnp.einsum(
        "rthe,rshe->rhts", grad_attended, split_values, preferred_element_type=jnp.float32
    )
    grad_score = (prob * (grad_prob - delta[..., None])).astype(jnp.bfloat16)
    query_terms = None
    key_terms = None
    content_add = jnp.einsum(
        "rhts,rshe->rthe", grad_score, split_keys, preferred_element_type=jnp.float32
    )
    spread = unskew(grad_score, window.shape[0])
    position_add = jnp.einsum("rhtk,khe->rthe", spread, window, preferred_element_type=jnp.float32)
    table_add = jnp.einsum("rhtk,rthe->khe", spread, query_v, preferred_element_type=jnp.float32)
    query_terms = (content_add, position_add, table_add, start)
    key_shape = key_arrays[0].shape
    grad_keys = jnp.einsum(
        "rhts,rthe->rshe", grad_score, query_u, preferred_element_type=jnp.float32
    ).reshape(key_shape)
    grad_values = jnp.einsum(
        "rhts,rthe->rshe",
        prob.astype(jnp.bfloat16),
        grad_attended,
        preferred_element_type=jnp.float32,
    ).reshape(key_shape)
    key_terms = (grad_keys, grad_values)
    return (query_terms, key_terms)


def forward_worker(query_arrays, query_anchor, context):

    def worker(running, pieces, anchor):
        score, allowed, split_keys, window, start = pair_scores(
            query_arrays, query_anchor, pieces, anchor, context
        )
        run_max, run_sum, run_acc = running
        new_max = jnp.maximum(run_max, jnp.max(score, -1))
        weight = jnp.where(allowed, jnp.exp(score - new_max[..., None]), 0.0)
        fade = jnp.exp(run_max - new_max)
        split_values = pieces[1].reshape(split_keys.shape)
        run_acc = run_acc * fade[..., None] + jnp.einsum(
            "rhts,rshe->rhte",
            weight.astype(jnp.bfloat16),
            split_values,
            preferred_element_type=jnp.float32,
        )
        return ((new_max, run_sum * fade + jnp.sum(weight, -1), run_acc), None)

    return worker


def add_table(table_acc, table_add, start):
    current = lax.dynamic_slice_in_dim(table_acc, start, table_add.shape[0], 0)
    return lax.dynamic_update_slice_in_dim(table_acc, current + table_add, start, 0)


def query_worker(query_arrays, query_anchor, context):

    def worker(running, pieces, anchor):
        query_terms, key_terms = pair_grads(query_arrays, query_anchor, pieces, anchor, context)
        content_add, position_add, table_add, start = query_terms
        content_acc, position_acc, table_acc = running
        return (
            (
                content_acc + content_add,
                position_acc + position_add,
                add_table(table_acc, table_add, start),
            ),
            key_terms,
        )

    return worker


def body(
    inputs,
    doc_bounds,
    pool_weight,
    pool_bias,
    ln1_gain,
    ln1_bias,
    query_weight,
    key_weight,
    value_weight,
    out_weight,
    pos_weight,
    content_bias,
    pos_bias,
    ln2_gain,
    ln2_bias,
    ffn_in,
    ffn_in_bias,
    ffn_out,
    ffn_out_bias,
    up_weight,
    up_bias,
    cotangent,
):
    rows_here, bytes_here, model_width = inputs.shape
    tokens_here = bytes_here // 3
    head_count = HEADS
    head_size = model_width // head_count
    score_scale = head_size ** (-0.5)
    total_tokens = tokens_here * lax.axis_size("seq")
    offset = lax.axis_index("seq") * tokens_here
    distances = total_tokens - 1 - jnp.arange(total_tokens, dtype=jnp.int32)
    sines, cosines = angles(distances, model_width)
    feats = jnp.concatenate([sines, cosines], -1).astype(jnp.bfloat16)
    rel_rows = jnp.dot(feats, pos_weight, preferred_element_type=jnp.float32).astype(jnp.bfloat16)
    rel_rows = rel_rows.reshape(total_tokens, head_count, head_size)
    rev_table = jnp.concatenate([rel_rows, jnp.zeros_like(rel_rows)], 0)
    context = (rev_table, doc_bounds, score_scale, total_tokens)
    rim = passed_along(inputs[:, bytes_here - 2 :, :], "seq", 1)
    shifted = jnp.concatenate([rim, inputs[:, : bytes_here - 2, :]], 1)
    pooled_in = shifted.reshape(rows_here, tokens_here, 3 * model_width)
    pooled = (
        jnp.einsum("rtc,cd->rtd", pooled_in, pool_weight, preferred_element_type=jnp.float32)
        + pool_bias
    )
    normed_one, plain_one, inverse_one = layer_norm(pooled, ln1_gain, ln1_bias)
    attn_in = normed_one.astype(jnp.bfloat16)
    query = jnp.einsum("rtc,cd->rtd", attn_in, query_weight, preferred_element_type=jnp.float32)
    key_rows = jnp.einsum(
        "rtc,cd->rtd", attn_in, key_weight, preferred_element_type=jnp.float32
    ).astype(jnp.bfloat16)
    value_rows = jnp.einsum(
        "rtc,cd->rtd", attn_in, value_weight, preferred_element_type=jnp.float32
    ).astype(jnp.bfloat16)
    split_shape = (rows_here, tokens_here, head_count, head_size)
    query_u = (query + content_bias).astype(jnp.bfloat16).reshape(split_shape)
    query_v = (query + pos_bias).astype(jnp.bfloat16).reshape(split_shape)
    stat_shape = (rows_here, head_count, tokens_here)
    start_state = (
        jnp.full(stat_shape, masked_score, jnp.float32),
        jnp.zeros(stat_shape, jnp.float32),
        jnp.zeros((rows_here, head_count, tokens_here, head_size), jnp.float32),
    )
    attend = forward_worker((query_u, query_v), offset, context)
    run_max, run_sum, run_acc = in_blocks(
        attend,
        start_state,
        (
            lax.all_gather(key_rows, "seq", axis=1, tiled=True),
            lax.all_gather(value_rows, "seq", axis=1, tiled=True),
        ),
        (1, 1),
    )[0]
    attended = run_acc / run_sum[..., None]
    log_total = run_max + jnp.log(run_sum)
    attended_split = jnp.transpose(attended, (0, 2, 1, 3))
    attended_low = attended_split.reshape(rows_here, tokens_here, model_width).astype(jnp.bfloat16)
    mixed = pooled + jnp.einsum(
        "rtc,cd->rtd", attended_low, out_weight, preferred_element_type=jnp.float32
    )
    normed_two, plain_two, inverse_two = layer_norm(mixed, ln2_gain, ln2_bias)
    ffn_input = normed_two.astype(jnp.bfloat16)
    pre_act = (
        jnp.einsum("rtc,cf->rtf", ffn_input, ffn_in, preferred_element_type=jnp.float32)
        + ffn_in_bias
    )
    activated, gelu_pull = jax.vjp(exact_gelu, pre_act)
    act_low = activated.astype(jnp.bfloat16)
    final = (
        mixed
        + jnp.einsum("rtf,fd->rtd", act_low, ffn_out, preferred_element_type=jnp.float32)
        + ffn_out_bias
    )
    final_low = final.astype(jnp.bfloat16)
    upsampled = (
        jnp.einsum("rtd,dc->rtc", final_low, up_weight, preferred_element_type=jnp.float32)
        + up_bias
    )
    outputs = (
        inputs.astype(jnp.float32) + upsampled.reshape(rows_here, bytes_here, model_width)
    ).astype(jnp.bfloat16)
    grad_up = cotangent.reshape(rows_here, tokens_here, 3 * model_width)
    grad_up_weight = jnp.einsum(
        "rtd,rtc->dc", final_low, grad_up, preferred_element_type=jnp.float32
    )
    grad_up_bias = jnp.sum(grad_up.astype(jnp.float32), axis=(0, 1))
    grad_final = jnp.einsum("rtc,dc->rtd", grad_up, up_weight, preferred_element_type=jnp.float32)
    grad_branch = grad_final.astype(jnp.bfloat16)
    grad_ffn_out = jnp.einsum(
        "rtf,rtd->fd", act_low, grad_branch, preferred_element_type=jnp.float32
    )
    grad_ffn_out_bias = jnp.sum(grad_branch.astype(jnp.float32), axis=(0, 1))
    grad_act = jnp.einsum("rtd,fd->rtf", grad_branch, ffn_out, preferred_element_type=jnp.float32)
    grad_pre = gelu_pull(grad_act)[0].astype(jnp.bfloat16)
    grad_ffn_in = jnp.einsum("rtc,rtf->cf", ffn_input, grad_pre, preferred_element_type=jnp.float32)
    grad_ffn_in_bias = jnp.sum(grad_pre.astype(jnp.float32), axis=(0, 1))
    grad_normed_two = jnp.einsum(
        "rtf,cf->rtc", grad_pre, ffn_in, preferred_element_type=jnp.float32
    )
    grad_from_two, grad_ln2_gain, grad_ln2_bias = norm_back(
        grad_normed_two, plain_two, inverse_two, ln2_gain
    )
    grad_mixed = grad_final + grad_from_two
    grad_attn_branch = grad_mixed.astype(jnp.bfloat16)
    grad_out_weight = jnp.einsum(
        "rtc,rtd->cd", attended_low, grad_attn_branch, preferred_element_type=jnp.float32
    )
    grad_attended = (
        jnp.einsum("rtd,cd->rtc", grad_attn_branch, out_weight, preferred_element_type=jnp.float32)
        .astype(jnp.bfloat16)
        .reshape(split_shape)
    )
    delta = jnp.sum(jnp.transpose(grad_attended.astype(jnp.float32), (0, 2, 1, 3)) * attended, -1)
    query_side = (query_u, query_v, grad_attended, log_total, delta)
    zero_query = (
        jnp.zeros(split_shape, jnp.float32),
        jnp.zeros(split_shape, jnp.float32),
        jnp.zeros((2 * total_tokens, head_count, head_size), jnp.float32),
    )
    both_worker = query_worker(query_side, offset, context)
    query_acc = zero_query
    query_acc, (grad_keys_part, grad_values_part) = in_blocks(
        both_worker,
        query_acc,
        (
            lax.all_gather(key_rows, "seq", axis=1, tiled=True),
            lax.all_gather(value_rows, "seq", axis=1, tiled=True),
        ),
        (1, 1),
    )
    query_acc, full_pair = (query_acc, (grad_keys_part, grad_values_part))
    grad_keys, grad_values = (
        lax.psum_scatter(full_pair[0], "seq", scatter_dimension=1, tiled=True),
        lax.psum_scatter(full_pair[1], "seq", scatter_dimension=1, tiled=True),
    )
    content_acc, position_acc, table_acc = query_acc
    grad_content = content_acc * score_scale
    grad_query_v = position_acc * score_scale
    grad_table = (table_acc[:total_tokens] * score_scale).reshape(total_tokens, model_width)
    grad_pos_weight = jnp.einsum(
        "kc,kd->cd", feats.astype(jnp.float32), grad_table, precision=lax.Precision.HIGHEST
    )
    grad_content_bias = jnp.sum(grad_content, axis=(0, 1)).reshape(model_width)
    grad_pos_bias = jnp.sum(grad_query_v, axis=(0, 1)).reshape(model_width)
    grad_query = (
        (grad_content + grad_query_v)
        .reshape(rows_here, tokens_here, model_width)
        .astype(jnp.bfloat16)
    )
    grad_key_low = (grad_keys * score_scale).astype(jnp.bfloat16)
    grad_value_low = grad_values.astype(jnp.bfloat16)
    grad_query_weight = jnp.einsum(
        "rtc,rtd->cd", attn_in, grad_query, preferred_element_type=jnp.float32
    )
    grad_key_weight = jnp.einsum(
        "rtc,rtd->cd", attn_in, grad_key_low, preferred_element_type=jnp.float32
    )
    grad_value_weight = jnp.einsum(
        "rtc,rtd->cd", attn_in, grad_value_low, preferred_element_type=jnp.float32
    )
    grad_normed_one = (
        jnp.einsum("rtd,cd->rtc", grad_query, query_weight, preferred_element_type=jnp.float32)
        + jnp.einsum("rtd,cd->rtc", grad_key_low, key_weight, preferred_element_type=jnp.float32)
        + jnp.einsum(
            "rtd,cd->rtc", grad_value_low, value_weight, preferred_element_type=jnp.float32
        )
    )
    grad_from_one, grad_ln1_gain, grad_ln1_bias = norm_back(
        grad_normed_one, plain_one, inverse_one, ln1_gain
    )
    grad_pooled = (grad_mixed + grad_from_one).astype(jnp.bfloat16)
    grad_pool_weight = jnp.einsum(
        "rtc,rtd->cd", pooled_in, grad_pooled, preferred_element_type=jnp.float32
    )
    grad_pool_bias = jnp.sum(grad_pooled.astype(jnp.float32), axis=(0, 1))
    grad_shifted = jnp.einsum(
        "rtd,cd->rtc", grad_pooled, pool_weight, preferred_element_type=jnp.float32
    ).reshape(rows_here, bytes_here, model_width)
    incoming = passed_along(grad_shifted[:, :2, :], "seq", -1)
    input_grad = (
        cotangent.astype(jnp.float32) + jnp.concatenate([grad_shifted[:, 2:, :], incoming], 1)
    ).astype(jnp.bfloat16)
    totals = lax.psum(
        (
            grad_pool_weight,
            grad_pool_bias,
            grad_ln1_gain,
            grad_ln1_bias,
            grad_query_weight,
            grad_key_weight,
            grad_value_weight,
            grad_out_weight,
            grad_pos_weight,
            grad_content_bias,
            grad_pos_bias,
            grad_ln2_gain,
            grad_ln2_bias,
            grad_ffn_in,
            grad_ffn_in_bias,
            grad_ffn_out,
            grad_ffn_out_bias,
            grad_up_weight,
            grad_up_bias,
        ),
        ("dp", "seq"),
    )
    return (
        outputs,
        input_grad,
        totals[0],
        totals[1],
        totals[2],
        totals[3],
        totals[4],
        totals[5],
        totals[6],
        totals[7],
        totals[8],
        totals[9],
        totals[10],
        totals[11],
        totals[12],
        totals[13],
        totals[14],
        totals[15],
        totals[16],
        totals[17],
        totals[18],
    )


def solution(mesh):
    placed = (
        P("dp", "seq", None),
        P("dp", None),
        P(),
        P(),
        P(),
        P(),
        P(),
        P(),
        P(),
        P(),
        P(),
        P(),
        P(),
        P(),
        P(),
        P(),
        P(),
        P(),
        P(),
        P(),
        P(),
        P("dp", "seq", None),
    )
    return jax.shard_map(
        body,
        mesh=mesh,
        in_specs=placed,
        out_specs=(
            P("dp", "seq", None),
            P("dp", "seq", None),
            P(),
            P(),
            P(),
            P(),
            P(),
            P(),
            P(),
            P(),
            P(),
            P(),
            P(),
            P(),
            P(),
            P(),
            P(),
            P(),
            P(),
            P(),
            P(),
        ),
        check_vma=False,
    )
```

profile of v0, /device:TPU:0, one launch (start us, length us, event | category | flops | bytes accessed | tf_op | source)
XLA Modules:
  0.0 1477.9 jit_solution(1519938352546041662)
XLA Ops:
  8.1 4.8 collective-permute-start
  22.5 12.7 fusion.67
  43.9 46.5 %all-gather.5.cloned.1.call-done = bf16[3072,512]{1,0:T(8,128)(2,1)} async-done(((bf16[192,512]{1,0:T(8,128)(2,1)}), bf16[3072,512]{1,0:T(8,128)(2,1)}) %all-gather.5.cloned.1.call-update) | async-done | bytes 3145744 | tf_op jit(solution)/shard_map/all_gather | solution.py:288
  90.4 4.6 copy.55
  95.0 65.4 %all-gather.7.cloned.1.call-done = bf16[3072,512]{1,0:T(8,128)(2,1)} async-done(((bf16[192,512]{1,0:T(8,128)(2,1)}), bf16[3072,512]{1,0:T(8,128)(2,1)}) %all-gather.7.cloned.1.call-update) | async-done | bytes 3145744 | tf_op jit(solution)/shard_map/all_gather | solution.py:289
  160.4 4.6 copy.56
  165.0 195.5 %while.37 = (s32[]{:T(128)}, f32[1,8,192]{2,1,0:T(8,128)S(1)}, f32[1,8,192]{2,1,0:T(8,128)S(1)}, f32[1,8,192,64]{2,3,1,0:T(8,128)}, s32[6]{0:T(128)S(1)}, /*inde...) while((s32[]{:T(128)}, f32[1,8,192]{2,1,0:T(8,128)S(1)}, ...), condition=%wide.region_5.6_spmd.clone, body=%wide.region_2.5_spmd.clone.sunk | while | flops 356360832 | bytes 194533680 | solution.py:103
  232.8 3.9 fusion.206
  263.3 3.9 fusion.206
  293.9 3.9 fusion.206
  324.5 3.9 fusion.206
  363.6 4.9 multiply_convert_fusion
  373.2 6.1 broadcast_in_dim.292
  379.3 442.7 %while.38 = (s32[]{:T(128)}, f32[1,192,8,64]{1,3,2,0:T(8,128)}, f32[1,192,8,64]{1,3,2,0:T(8,128)}, f32[6144,8,64]{0,2,1:T(8,128)}, f32[6,1,512,512]{3,2,0,1:T(8,...) while((s32[]{:T(128)}, f32[1,192,8,64]{1,3,2,0:T(8,128)}, ...), condition=%wide.region_12.13_spmd.clone, body=%wide.region_11.12_spmd.clone.sunk | while | flops 944163136 | bytes 304041728 | solution.py:103
  455.8 7.6 dynamic_update_slice.27
  463.4 4.5 fusion.228
  524.7 7.7 dynamic_update_slice.27
  532.4 4.6 fusion.228
  593.7 7.6 dynamic_update_slice.27
  601.3 4.6 fusion.228
  662.7 7.7 dynamic_update_slice.27
  670.4 4.6 fusion.228
  731.7 7.5 dynamic_update_slice.27
  739.2 4.6 fusion.228
  800.4 7.0 dynamic_update_slice.27
  807.4 4.5 fusion.228
  838.9 7.4 fusion.69
  846.2 121.3 %reduce-scatter.3.cloned.1.call-done = f32[1,192,512]{2,1,0:T(8,128)} async-done(((f32[1,3072,512]{2,1,0:T(8,128)}), f32[1,192,512]{2,1,0:T(8,128)}) %reduce-scatter.3.cloned.1.call-update) | async-done | bytes 393232 | tf_op jit(solution)/shard_map/reduce_scatter | solution.py:372
  969.1 149.0 %reduce-scatter.5.cloned.1.call-done = f32[1,192,512]{2,1,0:T(8,128)} async-done(((f32[1,3072,512]{2,1,0:T(8,128)}), f32[1,192,512]{2,1,0:T(8,128)}) %reduce-scatter.5.cloned.1.call-update) | async-done | bytes 393232 | tf_op jit(solution)/shard_map/reduce_scatter | solution.py:373
  1136.6 44.9 %all-reduce.26 = (f32[512]{0:T(512)}, f32[512]{0:T(512)}, f32[512]{0:T(512)}, f32[512]{0:T(512)}, f32[512]{0:T(512)}, /*index=5*/f32[512]{0:T(512)}, f32[512]{0:...) all-reduce(f32[512]{0:T(512)S(1)} %get-tuple-element.617, ...), channel_id=1, replica_groups=mesh['dp'=2,'seq'=16] {'dp','seq'}, use_global_device_ids=true, to_apply=%region_19.20 | all-reduce | flops 7680 | bytes 61440 | tf_op jit(solution)/shard_map/psum | solution.py:422
  1183.6 269.1 %all-reduce.30.cloned.1.call-done = (f32[1536,512]{1,0:T(8,128)}, f32[512,512]{1,0:T(8,128)}, f32[512,512]{1,0:T(8,128)}, f32[512,512]{1,0:T(8,128)}, f32[512,51...) async-done(((f32[1536,512]{1,0:T(8,128)}, f32[512,512]{1,0:T(8,128)}, f32[512,512]{1,0:T(8,128)}, ...) | async-done | bytes 19922960 | tf_op jit(solution)/shard_map/psum | solution.py:422
  1452.7 3.9 copy.131
  (891 shorter events, 577.1 us)
Async XLA Ops:
  7.2 356.3 %copy-start = (bf16[512,2048]{1,0:T(8,128)(2,1)S(1)}, bf16[512,2048]{1,0:T(8,128)(2,1)}, u32[]{:S(2)}) copy-start(bf16[512,2048]{1,0:T(8,128)(2,1)} %param.41) | copy-start | bytes 6291460
  7.2 8.5 copy-start.82
  7.2 83.1 %all-gather.5.cloned.1.call-start = ((), (), s32[]{:S(2)}) async-start(), calls=%async_computation.4 | async-start | bytes 3342336 | tf_op jit(solution)/shard_map/all_gather | solution.py:288
  8.1 6.1 collective-permute-start
  15.8 6.4 copy-start.33
  19.0 24.3 %copy-start.17 = (bf16[192,512]{1,0:T(8,128)(2,1)}, bf16[192,512]{1,0:T(8,128)(2,1)S(1)}, u32[]{:S(2)}) copy-start(bf16[192,512]{1,0:T(8,128)(2,1)S(1)} %add_convert_fusion.7) | copy-start | bytes 589828
  20.0 140.4 %all-gather.7.cloned.1.call-start = ((), (), s32[]{:S(2)}) async-start(), calls=%async_computation.5 | async-start | bytes 3342336 | tf_op jit(solution)/shard_map/all_gather | solution.py:289
  22.0 945.5 %reduce-scatter.3.cloned.1.call-start = ((), (), s32[]{:S(2)}) async-start(), calls=%async_computation.2 | async-start | bytes 6684672 | tf_op jit(solution)/shard_map/reduce_scatter | solution.py:372
  22.4 17.9 %copy-start.19 = (bf16[192,1536]{1,0:T(8,128)(2,1)}, bf16[192,1536]{1,0:T(8,128)(2,1)S(1)}, u32[]{:S(2)}) copy-start(bf16[192,1536]{1,0:T(8,128)(2,1)S(1)} %reshape.891) | copy-start | bytes 1769476
  22.5 12.7 copy-start.83
  361.6 6.8 copy-start.34
  363.3 8.4 copy-start.15
  363.3 8.4 copy-start.65
  363.6 8.1 copy-start.71
  372.5 6.8 copy-start.22
  400.5 26.2 %copy-start.6 = (bf16[1,192,8,64]{1,3,2,0:T(8,128)(2,1)}, bf16[1,192,8,64]{1,3,2,0:T(8,128)(2,1)S(1)}, u32[]{:S(2)}) copy-start(bf16[1,192,8,64]{1,3,2,0:T(8,128)(2,1)S(1)} %get-tuple-element.980) | copy-start | bytes 589828 | tf_op jit(solution)/shard_map/while
  469.4 26.2 %copy-start.6 = (bf16[1,192,8,64]{1,3,2,0:T(8,128)(2,1)}, bf16[1,192,8,64]{1,3,2,0:T(8,128)(2,1)S(1)}, u32[]{:S(2)}) copy-start(bf16[1,192,8,64]{1,3,2,0:T(8,128)(2,1)S(1)} %get-tuple-element.980) | copy-start | bytes 589828 | tf_op jit(solution)/shard_map/while
  538.4 26.2 %copy-start.6 = (bf16[1,192,8,64]{1,3,2,0:T(8,128)(2,1)}, bf16[1,192,8,64]{1,3,2,0:T(8,128)(2,1)S(1)}, u32[]{:S(2)}) copy-start(bf16[1,192,8,64]{1,3,2,0:T(8,128)(2,1)S(1)} %get-tuple-element.980) | copy-start | bytes 589828 | tf_op jit(solution)/shard_map/while
  607.3 26.2 %copy-start.6 = (bf16[1,192,8,64]{1,3,2,0:T(8,128)(2,1)}, bf16[1,192,8,64]{1,3,2,0:T(8,128)(2,1)S(1)}, u32[]{:S(2)}) copy-start(bf16[1,192,8,64]{1,3,2,0:T(8,128)(2,1)S(1)} %get-tuple-element.980) | copy-start | bytes 589828 | tf_op jit(solution)/shard_map/while
  676.4 26.2 %copy-start.6 = (bf16[1,192,8,64]{1,3,2,0:T(8,128)(2,1)}, bf16[1,192,8,64]{1,3,2,0:T(8,128)(2,1)S(1)}, u32[]{:S(2)}) copy-start(bf16[1,192,8,64]{1,3,2,0:T(8,128)(2,1)S(1)} %get-tuple-element.980) | copy-start | bytes 589828 | tf_op jit(solution)/shard_map/while
  745.3 26.1 %copy-start.6 = (bf16[1,192,8,64]{1,3,2,0:T(8,128)(2,1)}, bf16[1,192,8,64]{1,3,2,0:T(8,128)(2,1)S(1)}, u32[]{:S(2)}) copy-start(bf16[1,192,8,64]{1,3,2,0:T(8,128)(2,1)S(1)} %get-tuple-element.980) | copy-start | bytes 589828 | tf_op jit(solution)/shard_map/while
  822.0 296.1 %reduce-scatter.5.cloned.1.call-start = ((), (), s32[]{:S(2)}) async-start(), calls=%async_computation.3 | async-start | bytes 6684672 | tf_op jit(solution)/shard_map/reduce_scatter | solution.py:373
  822.6 630.1 %all-reduce.30.cloned.1.call-start = ((), (), s32[]{:S(2)}) async-start(), calls=%async_computation.6 | async-start | bytes 39845888 | tf_op jit(solution)/shard_map/psum | solution.py:422
  825.6 11.3 slice-start
  828.8 8.1 slice-start.1
  838.9 279.2 %copy-start.14 = (f32[192,512]{1,0:T(8,128)S(1)}, f32[192,512]{1,0:T(8,128)}, u32[]{:S(2)}) copy-start(f32[192,512]{1,0:T(8,128)} %copy-done.13) | copy-start | bytes 1179652
  838.9 279.2 %copy-start.36 = (bf16[512,512]{1,0:T(8,128)(2,1)S(1)}, bf16[512,512]{1,0:T(8,128)(2,1)}, u32[]{:S(2)}) copy-start(bf16[512,512]{1,0:T(8,128)(2,1)} %param.34) | copy-start | bytes 1572868
  838.9 279.2 %copy-start.64 = (f32[192]{0:T(256)S(1)}, f32[192]{0:T(256)}, u32[]{:S(2)}) copy-start(f32[192]{0:T(256)} %copy-done.63) | copy-start | bytes 2308
  838.9 279.3 %copy-start.68 = (f32[512]{0:T(512)S(1)}, f32[512]{0:T(512)}, u32[]{:S(2)}) copy-start(f32[512]{0:T(512)} %param.30) | copy-start | bytes 6148
  838.9 279.3 %copy-start.70 = (f32[192]{0:T(256)S(1)}, f32[192]{0:T(256)}, u32[]{:S(2)}) copy-start(f32[192]{0:T(256)} %copy-done.69) | copy-start | bytes 2308
  846.2 273.6 %copy-start.25 = (bf16[192,1536]{1,0:T(8,128)(2,1)S(1)}, bf16[192,1536]{1,0:T(8,128)(2,1)}, u32[]{:S(2)}) copy-start(bf16[192,1536]{1,0:T(8,128)(2,1)} %copy-done.24) | copy-start | bytes 1769476
  1133.8 47.7 %collective-permute-start.1 = (f32[1,2,512]{2,1,0:T(2,128)S(1)}, f32[1,2,512]{2,1,0:T(2,128)S(1)}, u32[]{:S(2)}, u32[]{:S(2)}) collective-permute-start(f32[1,2,512]{2,1,0:T(2,128)S(1)} %slice.238), channel_id=1, source_target_pairs={{1,0},{2,1},{3,2},{4,3},{5,4},{6,5},{7,6},{8,7},{9,8},{10,9},{11,1... | collective-permute-start | bytes 12296 | tf_op jit(solution)/shard_map/ppermute | solution.py:16
  (113 other events, 314.8 us)
Sparse Core Ops, SparseCore 0:
  20.1 70.2 all-gather.4
  93.7 66.6 all-gather.6
  822.1 145.3 reduce-scatter.2
  972.6 145.4 reduce-scatter.4
  1126.1 326.5 all-reduce.29
where the time goes:
time: 1490 us; the launch traced here: 1480 us
  waiting for transfers between devices  653 us (44%)
  local copies, waits for them, and re-layouts  301 us (20%)
  matrix products  217 us (15%)
  other arithmetic  188 us (13%)
  loops' own time  52.8 us (4%)
  blocking collectives  44.9 us (3%)
  between operations  15 us (1%)
    psum x1, waiting for transfers between devices, body(): lax.psum((grad_pool_weight, grad_pool_bias, grad_ln1_gain, grad_ln1_bias,...  269 us
    reduce_scatter x1, waiting for transfers between devices, body(): lax.psum_scatter(full_pair[1], 'seq', scatter_dimension=1, tiled=True)  149 us
    reduce_scatter x1, waiting for transfers between devices, body(): lax.psum_scatter(full_pair[0], 'seq', scatter_dimension=1, tiled=True)  121 us
    slice x96, local copies, waits for them, and re-layouts, skew(): current[..., step_len:]  108 us
    select_n x42, other arithmetic, unskew(): current = jnp.where(taken[:, None], moved, current)  69.1 us
    all_gather x1, waiting for transfers between devices, body(): lax.all_gather(value_rows, 'seq', axis=1, tiled=True)  65.4 us
    select_n x84, other arithmetic, skew(): current = jnp.where(taken[:, None], moved, current)  55.4 us
    another operation x2, loops' own time, in_blocks(): lax.scan(advance, running, (stacked, jnp.arange(block_count, dtype=jnp.in...  52.8 us
  transfers between devices with their start and end apart: 7, of which 6 were waited for; matrix products, arithmetic and copies ran while one was open for 4% of the time, Pallas kernels for 0%

commit v1 on v0

v1 whole, which is shorter than its diff:
```python
import functools

import jax
import jax.numpy as jnp
import numpy as np
from jax import lax
from jax.experimental import pallas as pl
from jax.experimental.pallas import tpu as pltpu
from jax.sharding import PartitionSpec as P

HEADS = 8
ROWS = 2
HEAD = 64
PAIR = 2 * HEAD
MESH = pl.DeviceIdType.MESH
F32 = jnp.float32
BF16 = jnp.bfloat16

epsilon = 1e-05
masked_score = -1e30


def dot(left, right, dims=((1,), (0,))):
    return lax.dot_general(left, right, (dims, ((), ())), preferred_element_type=F32)


def passed_along(value, axis, steps):
    count = lax.axis_size(axis)
    first, last = (max(0, -steps), min(count, count - steps))
    return lax.ppermute(value, axis, [(source, source + steps) for source in range(first, last)])


def place_of(block, group):
    turn, spot = block // group, block % group
    return turn, jnp.where(turn % 2 == 0, spot, group - 1 - spot)


def block_of(turn, member, group):
    return turn * group + jnp.where(turn % 2 == 0, member, group - 1 - member)


def whereabouts(group):
    core, chip = lax.axis_index("dp"), lax.axis_index("seq")
    chips = group // 2
    unit = chip // chips
    member = (chip % chips) * 2 + core
    return core, chip, unit // HEADS, unit % HEADS, member


def chip_of(row, head, member, group):
    return (row * HEADS + head) * (group // 2) + member // 2, member % 2


def meet(n, group, to_units):
    core, chip, row, head, member = whereabouts(group)
    barrier = pltpu.get_barrier_semaphore()

    def greet(row_or_core, chip_at):
        away = jnp.logical_or(row_or_core != core, chip_at != chip)

        @pl.when(away)
        def _():
            pl.semaphore_signal(
                barrier, inc=1, device_id=(row_or_core, chip_at), device_id_type=MESH
            )

        return away.astype(jnp.int32)

    own_row = row == core
    if to_units:
        for s in range(n):
            greet(row, jnp.int32(s))
        mine = jnp.logical_and(chip // (HEADS * (group // 2)) == core, True)
        pl.semaphore_wait(barrier, HEADS * group - mine.astype(jnp.int32))
    else:
        for h in range(HEADS):
            for g in range(group):
                c, k = chip_of(core, h, g, group)
                greet(jnp.int32(k), c)
        pl.semaphore_wait(barrier, n - own_row.astype(jnp.int32))


def send(source, target, sems, core, chip):
    here_core, here_chip = lax.axis_index("dp"), lax.axis_index("seq")
    here = jnp.logical_and(core == here_core, chip == here_chip)

    @pl.when(here)
    def _():
        pltpu.make_async_copy(source, target, sems[1]).start()

    @pl.when(jnp.logical_not(here))
    def _():
        pltpu.make_async_remote_copy(
            source, target, sems[0], sems[1], device_id=(core, chip), device_id_type=MESH
        ).start()


def sent(source, sem, core, chip):
    here_core, here_chip = lax.axis_index("dp"), lax.axis_index("seq")
    here = jnp.logical_and(core == here_core, chip == here_chip)

    @pl.when(jnp.logical_not(here))
    def _():
        pltpu.make_async_copy(source, source, sem).wait()


def arrived(whole, sem):
    pltpu.make_async_copy(whole, whole, sem).wait()


def to_units_kernel(n, group, *refs):
    count = len(refs) - 2
    arrays, outs = refs[: count // 2], refs[count // 2 : count]
    send_sem, recv_sem = refs[count:]
    core, chip, row, head, member = whereabouts(group)
    turn, spot = place_of(chip, group)
    meet(n, group, True)
    jobs = []
    for h in range(HEADS):
        for index, (array, out) in enumerate(zip(arrays, outs)):
            sems = (send_sem.at[index], recv_sem.at[index])
            if index == 0:
                to_chip, to_core = chip_of(core, h, spot, group)
                jobs.append((array.at[h], out.at[turn], sems, to_core, to_chip))
            else:
                for g in range(group):
                    to_chip, to_core = chip_of(core, h, g, group)
                    jobs.append((array.at[h], out.at[chip], sems, jnp.int32(to_core), to_chip))
    for job in jobs:
        send(*job)
    for source, _, sems, to_core, to_chip in jobs:
        sent(source, sems[0], to_core, to_chip)
    for index, out in enumerate(outs):
        arrived(out, recv_sem.at[index])


def to_owners_kernel(n, group, *refs):
    count = len(refs) - 2
    arrays, outs = refs[: count // 2], refs[count // 2 : count]
    send_sem, recv_sem = refs[count:]
    core, chip, row, head, member = whereabouts(group)
    meet(n, group, False)
    jobs = []
    for turn in range(n // group):
        block = block_of(jnp.int32(turn), member, group)
        sems = (send_sem.at[0], recv_sem.at[0])
        jobs.append((arrays[0].at[turn], outs[0].at[head], sems, row, block))
    if len(arrays) > 1:
        for block in range(n):
            sems = (send_sem.at[1], recv_sem.at[1])
            jobs.append((arrays[1].at[block], outs[1].at[member, head], sems, row, jnp.int32(block)))
    for job in jobs:
        send(*job)
    for source, _, sems, to_core, to_chip in jobs:
        sent(source, sems[0], to_core, to_chip)
    for index, out in enumerate(outs):
        arrived(out, recv_sem.at[index])


def exchange(kernel, n, group, arrays, shapes, ident):
    vmem = pl.BlockSpec(memory_space=pltpu.VMEM)
    return pl.pallas_call(
        functools.partial(kernel, n, group),
        out_shape=[jax.ShapeDtypeStruct(shape, array.dtype) for shape, array in zip(shapes, arrays)],
        in_specs=[vmem] * len(arrays),
        out_specs=[vmem] * len(arrays),
        scratch_shapes=[
            pltpu.SemaphoreType.DMA((len(arrays),)),
            pltpu.SemaphoreType.DMA((len(arrays),)),
        ],
        compiler_params=pltpu.CompilerParams(
            collective_id=ident, has_side_effects=True, vmem_limit_bytes=48 * 2**20
        ),
    )(*arrays)


def unpacked(pair):
    return jnp.concatenate([pair[:, :HEAD], pair[:, HEAD:]], 0)


def packed(block):
    half = block.shape[0] // 2
    return jnp.concatenate([block[:half], block[half:]], 1)


def query_parts(q_pair, content_bias, pos_bias, pos_weight, turn_sin, turn_cos):
    query = unpacked(q_pair.astype(F32))
    query_u = (query + content_bias).astype(BF16)
    query_v = (query + pos_bias).astype(BF16)
    spread = dot(query_v, pos_weight, ((1,), (1,)))
    half = turn_sin.shape[1]
    lift, rest = spread[:, :half], spread[:, half:]
    on_sin = rest * turn_sin - lift * turn_cos
    on_cos = lift * turn_sin + rest * turn_cos
    turned = jnp.concatenate([on_sin, on_cos], 1)
    return query_u, query_v, turned


def attend_kernel(
    n, group, tile, q_ref, kv_ref, table_ref, sin_ref, cos_ref, weight_ref, cb_ref, pb_ref, bounds_ref,
    att_ref, low_ref, total_ref, keep_ref, score_ref, extra_ref,
):
    turn = pl.program_id(0)
    member = whereabouts(group)[4]
    block = block_of(turn, member, group)
    length = sin_ref.shape[0]
    tokens = n * length
    query_u, _, turned = query_parts(
        q_ref[...], cb_ref[...], pb_ref[...], weight_ref[...], sin_ref[...], cos_ref[...]
    )
    scale = HEAD**-0.5
    head_part = (query_u.astype(F32) * scale).astype(BF16)
    extra_ref[:, :HEAD] = head_part
    extra_ref[:, HEAD:PAIR] = jnp.zeros_like(head_part)
    extra_ref[:, PAIR:] = (turned * scale).astype(BF16)
    first = block * length
    tiles = (first + length + tile - 1) // tile
    low_bound, high_bound = bounds_ref[0], bounds_ref[1]
    places = first + lax.broadcasted_iota(jnp.int32, (length, 1), 0)
    opening = jnp.where(
        places >= high_bound, high_bound, jnp.where(places >= low_bound, low_bound, 0)
    )
    lanes = lax.broadcasted_iota(jnp.int32, (length, tile), 1)

    def score_step(step, top):
        start = pl.multiple_of(step * tile, tile)
        keys = kv_ref[pl.ds(start, tile), :]
        waves = table_ref[pl.ds(pl.multiple_of((n - 1 - block) * length + start, length), tile), :]
        score = dot(extra_ref[:, :PAIR], keys, ((1,), (1,))) + dot(
            extra_ref[:, PAIR:], waves, ((1,), (1,))
        )
        at = lanes + start
        allowed = jnp.logical_and(at <= places, at >= opening)
        score = jnp.where(allowed, score, masked_score)
        score_ref[:, pl.ds(start, tile)] = score
        for part in range(tile // 128):
            top = jnp.maximum(top, score[:, part * 128 : (part + 1) * 128])
        return top

    top = lax.fori_loop(0, tiles, score_step, jnp.full((length, 128), masked_score, F32))
    top = jnp.max(top, 1, keepdims=True)

    def value_step(step, state):
        total, summed = state
        start = pl.multiple_of(step * tile, tile)
        weight = jnp.exp(score_ref[:, pl.ds(start, tile)] - top)
        for part in range(tile // 128):
            total = total + weight[:, part * 128 : (part + 1) * 128]
        low = weight.astype(BF16)
        keep_ref[:, pl.ds(start, tile)] = low
        return total, summed + dot(low, kv_ref[pl.ds(start, tile), :])

    total, summed = lax.fori_loop(
        0, tiles, value_step, (jnp.zeros((length, 128), F32), jnp.zeros((length, PAIR), F32))
    )
    total = jnp.sum(total, 1, keepdims=True)
    attended = summed[:, HEAD:] / total
    att_ref[...] = attended
    total_ref[...] = jnp.broadcast_to(total, (length, 128))
    low_ref[...] = packed(attended).astype(BF16)


def back_kernel(
    n, group, tile, q_ref, kv_ref, table_ref, sin_ref, cos_ref, weight_ref, cb_ref, pb_ref,
    att_ref, total_ref, keep_ref, grad_ref,
    dq_ref, dkv_ref, dweight_ref, dcb_ref, dpb_ref, dkv_acc,
):
    turn = pl.program_id(0)
    member = whereabouts(group)[4]
    block = block_of(turn, member, group)
    length = sin_ref.shape[0]
    scale = HEAD**-0.5

    @pl.when(turn == 0)
    def _():
        dkv_acc[...] = jnp.zeros_like(dkv_acc)
        dweight_ref[...] = jnp.zeros_like(dweight_ref)
        dcb_ref[...] = jnp.zeros_like(dcb_ref)
        dpb_ref[...] = jnp.zeros_like(dpb_ref)

    query_u, query_v, _ = query_parts(
        q_ref[...], cb_ref[...], pb_ref[...], weight_ref[...], sin_ref[...], cos_ref[...]
    )
    head_part = (query_u.astype(F32) * scale).astype(BF16)
    grad = unpacked(grad_ref[...].astype(F32))
    inverse = 1.0 / total_ref[:, :1]
    delta = jnp.sum(grad * att_ref[...], 1, keepdims=True) * inverse
    grad_low = (grad * inverse).astype(BF16)
    nothing = jnp.zeros_like(grad_low)
    grad_wide = jnp.concatenate([nothing, grad_low], 1)
    query_wide = jnp.concatenate([head_part, nothing], 1)
    tiles = (block * length + length + tile - 1) // tile

    def step_over(step, state):
        near, far = state
        start = pl.multiple_of(step * tile, tile)
        keys = kv_ref[pl.ds(start, tile), :]
        waves = table_ref[pl.ds(pl.multiple_of((n - 1 - block) * length + start, length), tile), :]
        weight = keep_ref[:, pl.ds(start, tile)]
        grad_weight = dot(grad_wide, keys, ((1,), (1,)))
        grad_score = (weight.astype(F32) * (grad_weight - delta)).astype(BF16)
        near = near + dot(grad_score, keys)
        far = far + dot(grad_score, waves)
        dkv_acc[pl.ds(start, tile), :] += dot(grad_score, query_wide, ((0,), (0,))) + dot(
            weight, grad_wide, ((0,), (0,))
        )
        return near, far

    near, far = lax.fori_loop(
        0,
        tiles,
        step_over,
        (jnp.zeros((length, PAIR), F32), jnp.zeros((length, table_ref.shape[1]), F32)),
    )
    grad_u = near[:, :HEAD] * scale
    half = sin_ref.shape[1]
    turn_sin, turn_cos = sin_ref[...], cos_ref[...]
    on_sin, on_cos = far[:, :half] * scale, far[:, half:] * scale
    lift = on_cos * turn_sin - on_sin * turn_cos
    rest = on_cos * turn_cos + on_sin * turn_sin
    spread = jnp.concatenate([lift, rest], 1).astype(BF16)
    grad_v = dot(spread, weight_ref[...])
    dweight_ref[...] += dot(spread, query_v, ((0,), (0,)))
    dcb_ref[...] += jnp.sum(grad_u, 0, keepdims=True)
    dpb_ref[...] += jnp.sum(grad_v, 0, keepdims=True)
    dq_ref[...] = packed(grad_u + grad_v).astype(BF16)

    @pl.when(turn == pl.num_programs(0) - 1)
    def _():
        dkv_ref[...] = dkv_acc[...].astype(BF16)


def wave_tables(tokens, length, width):
    rates = 10000.0 ** (-2.0 * np.arange(width // 2, dtype=np.float64) / width)
    far = (np.arange(tokens + length, dtype=np.float64) - (tokens - length))[:, None] * rates
    near = np.arange(length, dtype=np.float64)[:, None] * rates
    table = np.concatenate([np.sin(far), np.cos(far)], 1)
    return (
        jnp.asarray(table, dtype=BF16),
        jnp.asarray(np.sin(near), dtype=F32),
        jnp.asarray(np.cos(near), dtype=F32),
    )


def whole_spec(shape):
    return pl.BlockSpec(shape, lambda turn: (0,) * len(shape))


def turn_spec(shape):
    return pl.BlockSpec((None,) + shape, lambda turn: (turn,) + (0,) * len(shape))


def layer_norm(hidden, gain, bias):
    average = jnp.mean(hidden, -1, keepdims=True)
    centred = hidden - average
    inverse = lax.rsqrt(jnp.mean(centred * centred, -1, keepdims=True) + epsilon)
    normed = centred * inverse
    return (normed * gain + bias, normed, inverse)


def norm_back(grad_out, normed, inverse, gain):
    scaled = grad_out * gain
    grad_in = inverse * (
        scaled
        - jnp.mean(scaled, -1, keepdims=True)
        - normed * jnp.mean(scaled * normed, -1, keepdims=True)
    )
    return (grad_in, jnp.sum(grad_out * normed, axis=0), jnp.sum(grad_out, axis=0))


def exact_gelu(value):
    return jax.nn.gelu(value, approximate=False)


def heads_packed(array):
    length = array.shape[0]
    split = array.reshape(2, length // 2, HEADS, HEAD)
    return jnp.transpose(split, (2, 1, 0, 3)).reshape(HEADS, length // 2, PAIR)


def heads_unpacked(array):
    half = array.shape[1]
    split = array.reshape(HEADS, half, 2, HEAD)
    return jnp.transpose(split, (2, 1, 0, 3)).reshape(2 * half, HEADS * HEAD)


def body(
    inputs, doc_bounds, pool_weight, pool_bias, ln1_gain, ln1_bias, query_weight, key_weight,
    value_weight, out_weight, pos_weight, content_bias, pos_bias, ln2_gain, ln2_bias, ffn_in,
    ffn_in_bias, ffn_out, ffn_out_bias, up_weight, up_bias, cotangent,
):
    _, bytes_here, width = inputs.shape
    length = bytes_here // 3
    n = lax.axis_size("seq")
    tokens = n * length
    group = 2 * n // (ROWS * HEADS)
    rounds = n // group
    tile = 2 * length
    row, head, member = whereabouts(group)[2:]

    all_bounds = lax.all_gather(doc_bounds, "dp", axis=0, tiled=True)
    bounds = lax.dynamic_slice(all_bounds, (row, 0), (1, 2))[0]
    table, turn_sin, turn_cos = wave_tables(tokens, length, width)
    head_weight = lax.dynamic_slice(pos_weight, (0, head * HEAD), (width, HEAD))
    head_cb = lax.dynamic_slice(content_bias, (head * HEAD,), (HEAD,))[None]
    head_pb = lax.dynamic_slice(pos_bias, (head * HEAD,), (HEAD,))[None]

    rim = passed_along(inputs[:, bytes_here - 2 :, :], "seq", 1)
    shifted = jnp.concatenate([rim, inputs[:, : bytes_here - 2, :]], 1)
    pooled_in = shifted.reshape(length, 3 * width)
    pooled = dot(pooled_in, pool_weight) + pool_bias
    normed_one, plain_one, inverse_one = layer_norm(pooled, ln1_gain, ln1_bias)
    attn_in = normed_one.astype(BF16)
    query = dot(attn_in, query_weight).astype(BF16)
    keys = dot(attn_in, key_weight).astype(BF16).reshape(length, HEADS, HEAD)
    values = dot(attn_in, value_weight).astype(BF16).reshape(length, HEADS, HEAD)
    q_out = heads_packed(query)
    kv_out = jnp.transpose(jnp.concatenate([keys, values], 2), (1, 0, 2))

    q_in, kv_in = exchange(
        to_units_kernel, n, group, (q_out, kv_out),
        ((rounds, length // 2, PAIR), (n, length, PAIR)), 0,
    )
    kv_in = kv_in.reshape(tokens, PAIR)

    common_specs = [
        turn_spec((length // 2, PAIR)),
        whole_spec((tokens, PAIR)),
        whole_spec(table.shape),
        whole_spec(turn_sin.shape),
        whole_spec(turn_cos.shape),
        whole_spec(head_weight.shape),
        whole_spec((1, HEAD)),
        whole_spec((1, HEAD)),
    ]
    common = (q_in, kv_in, table, turn_sin, turn_cos, head_weight, head_cb, head_pb)
    attended, att_low, total, keep = pl.pallas_call(
        functools.partial(attend_kernel, n, group, tile),
        grid=(rounds,),
        in_specs=common_specs + [pl.BlockSpec(memory_space=pltpu.SMEM)],
        out_specs=[
            turn_spec((length, HEAD)),
            turn_spec((length // 2, PAIR)),
            turn_spec((length, 128)),
            turn_spec((length, tokens)),
        ],
        out_shape=[
            jax.ShapeDtypeStruct((rounds, length, HEAD), F32),
            jax.ShapeDtypeStruct((rounds, length // 2, PAIR), BF16),
            jax.ShapeDtypeStruct((rounds, length, 128), F32),
            jax.ShapeDtypeStruct((rounds, length, tokens), BF16),
        ],
        scratch_shapes=[
            pltpu.VMEM((length, tokens), F32),
            pltpu.VMEM((length, PAIR + width), BF16),
        ],
        compiler_params=pltpu.CompilerParams(vmem_limit_bytes=56 * 2**20),
    )(*common, bounds)

    (att_back,) = exchange(
        to_owners_kernel, n, group, (att_low,), ((HEADS, length // 2, PAIR),), 1
    )
    attended_low = heads_unpacked(att_back)

    mixed = pooled + dot(attended_low, out_weight)
    normed_two, plain_two, inverse_two = layer_norm(mixed, ln2_gain, ln2_bias)
    ffn_input = normed_two.astype(BF16)
    pre_act = dot(ffn_input, ffn_in) + ffn_in_bias
    activated, gelu_pull = jax.vjp(exact_gelu, pre_act)
    act_low = activated.astype(BF16)
    final = mixed + dot(act_low, ffn_out) + ffn_out_bias
    final_low = final.astype(BF16)
    upsampled = dot(final_low, up_weight) + up_bias
    outputs = (inputs.astype(F32) + upsampled.reshape(1, bytes_here, width)).astype(BF16)
    grad_up = cotangent.reshape(length, 3 * width)
    over_rows = ((0,), (0,))
    over_columns = ((1,), (1,))
    grad_up_weight = dot(final_low, grad_up, over_rows)
    grad_up_bias = jnp.sum(grad_up.astype(F32), axis=0)
    grad_final = dot(grad_up, up_weight, over_columns)
    grad_branch = grad_final.astype(BF16)
    grad_ffn_out = dot(act_low, grad_branch, over_rows)
    grad_ffn_out_bias = jnp.sum(grad_branch.astype(F32), axis=0)
    grad_act = dot(grad_branch, ffn_out, over_columns)
    grad_pre = gelu_pull(grad_act)[0].astype(BF16)
    grad_ffn_in = dot(ffn_input, grad_pre, over_rows)
    grad_ffn_in_bias = jnp.sum(grad_pre.astype(F32), axis=0)
    grad_normed_two = dot(grad_pre, ffn_in, over_columns)
    grad_from_two, grad_ln2_gain, grad_ln2_bias = norm_back(
        grad_normed_two, plain_two, inverse_two, ln2_gain
    )
    grad_mixed = grad_final + grad_from_two
    grad_attn_branch = grad_mixed.astype(BF16)
    grad_out_weight = dot(attended_low, grad_attn_branch, over_rows)
    grad_attended = dot(grad_attn_branch, out_weight, over_columns).astype(BF16)

    early = lax.psum(
        tuple(
            grad.astype(BF16) for grad in (grad_ffn_in, grad_ffn_out, grad_up_weight, grad_out_weight)
        ),
        ("dp", "seq"),
    )

    (grad_in,) = exchange(
        to_units_kernel, n, group, (heads_packed(grad_attended),), ((rounds, length // 2, PAIR),), 2
    )
    dq_out, dkv_out, grad_head_weight, grad_head_cb, grad_head_pb = pl.pallas_call(
        functools.partial(back_kernel, n, group, tile),
        grid=(rounds,),
        in_specs=common_specs
        + [
            turn_spec((length, HEAD)),
            turn_spec((length, 128)),
            turn_spec((length, tokens)),
            turn_spec((length // 2, PAIR)),
        ],
        out_specs=[
            turn_spec((length // 2, PAIR)),
            whole_spec((tokens, PAIR)),
            whole_spec((width, HEAD)),
            whole_spec((1, HEAD)),
            whole_spec((1, HEAD)),
        ],
        out_shape=[
            jax.ShapeDtypeStruct((rounds, length // 2, PAIR), BF16),
            jax.ShapeDtypeStruct((tokens, PAIR), BF16),
            jax.ShapeDtypeStruct((width, HEAD), F32),
            jax.ShapeDtypeStruct((1, HEAD), F32),
            jax.ShapeDtypeStruct((1, HEAD), F32),
        ],
        scratch_shapes=[pltpu.VMEM((tokens, PAIR), F32)],
        compiler_params=pltpu.CompilerParams(vmem_limit_bytes=56 * 2**20),
    )(*common, attended, total, keep, grad_in)
    dq_back, dkv_back = exchange(
        to_owners_kernel, n, group, (dq_out, dkv_out.reshape(n, length, PAIR)),
        ((HEADS, length // 2, PAIR), (group, HEADS, length, PAIR)), 3,
    )
    grad_query = heads_unpacked(dq_back)
    dkv_back = jnp.transpose(jnp.sum(dkv_back.astype(F32), 0), (1, 0, 2)).astype(BF16)
    grad_key_low = dkv_back[:, :, :HEAD].reshape(length, width)
    grad_value_low = dkv_back[:, :, HEAD:].reshape(length, width)

    def at_head(part, shape):
        return lax.dynamic_update_slice(
            jnp.zeros(shape, F32), part.reshape(shape[:-1] + (HEAD,)), (0,) * (len(shape) - 1) + (head * HEAD,)
        )

    grad_pos_weight = at_head(grad_head_weight, (width, width))
    grad_content_bias = at_head(grad_head_cb, (width,))
    grad_pos_bias = at_head(grad_head_pb, (width,))
    grad_query_weight = dot(attn_in, grad_query, over_rows)
    grad_key_weight = dot(attn_in, grad_key_low, over_rows)
    grad_value_weight = dot(attn_in, grad_value_low, over_rows)
    grad_normed_one = (
        dot(grad_query, query_weight, over_columns)
        + dot(grad_key_low, key_weight, over_columns)
        + dot(grad_value_low, value_weight, over_columns)
    )
    grad_from_one, grad_ln1_gain, grad_ln1_bias = norm_back(
        grad_normed_one, plain_one, inverse_one, ln1_gain
    )
    grad_pooled = (grad_mixed + grad_from_one).astype(BF16)
    grad_pool_weight = dot(pooled_in, grad_pooled, over_rows)
    grad_pool_bias = jnp.sum(grad_pooled.astype(F32), axis=0)
    grad_shifted = dot(grad_pooled, pool_weight, over_columns).reshape(1, bytes_here, width)
    incoming = passed_along(grad_shifted[:, :2, :], "seq", -1)
    input_grad = (
        cotangent.astype(F32) + jnp.concatenate([grad_shifted[:, 2:, :], incoming], 1)
    ).astype(BF16)
    late = lax.psum(
        tuple(
            grad.astype(BF16)
            for grad in (
                grad_pool_weight, grad_query_weight, grad_key_weight, grad_value_weight, grad_pos_weight,
            )
        ),
        ("dp", "seq"),
    )
    small_parts = (
        grad_pool_bias, grad_ln1_gain, grad_ln1_bias, grad_content_bias, grad_pos_bias,
        grad_ln2_gain, grad_ln2_bias, grad_ffn_in_bias, grad_ffn_out_bias, grad_up_bias,
    )
    small = lax.psum(jnp.concatenate(small_parts), ("dp", "seq"))
    cuts = np.cumsum([part.shape[0] for part in small_parts])[:-1].tolist()
    (
        sum_pool_bias, sum_ln1_gain, sum_ln1_bias, sum_content, sum_pos,
        sum_ln2_gain, sum_ln2_bias, sum_in_bias, sum_out_bias, sum_up_bias,
    ) = jnp.split(small, cuts)
    sum_in, sum_out, sum_up, sum_mix = (grad.astype(F32) for grad in early)
    sum_pool, sum_q, sum_k, sum_v, sum_p = (grad.astype(F32) for grad in late)
    return (
        outputs, input_grad, sum_pool, sum_pool_bias, sum_ln1_gain, sum_ln1_bias, sum_q, sum_k, sum_v,
        sum_mix, sum_p, sum_content, sum_pos, sum_ln2_gain, sum_ln2_bias, sum_in, sum_in_bias,
        sum_out, sum_out_bias, sum_up, sum_up_bias,
    )


def solution(mesh):
    split = P("dp", "seq", None)
    return jax.shard_map(
        body,
        mesh=mesh,
        in_specs=(split, P("dp", None)) + (P(),) * 19 + (split,),
        out_specs=(split, split) + (P(),) * 19,
        check_vma=False,
    )
```

time: 1490 us -> 445 us (0.30)
  waiting for transfers between devices: 653 us -> 147 us
  local copies, waits for them, and re-layouts: 301 us -> 35.1 us
  matrix products: 217 us -> 39.5 us
  other arithmetic: 188 us -> 21.9 us
  Pallas kernels: 0 us -> 130 us
  loops' own time: 52.8 us -> 0 us
    reduce_scatter x2 -> x0, waiting for transfers between devices: 270 us -> none  [the longest x1 149 us: body(): lax.psum_scatter(full_pair[1], 'seq', scatter_dimension=1, tiled=True)]
    dot_general x92 -> x24, matrix products: 217 us -> 39.5 us  [dot(): lax.dot_general(left, right, (dims, ((), ())), preferred_element_type=F32)]
    pallas_call x0 -> x6, Pallas kernels: none -> 130 us  [the longest x4 70.7 us: exchange(): pl.pallas_call(functools.partial(kernel, n, group), out_shape=[jax.ShapeD...]
    select_n x126 -> x0, other arithmetic: 125 us -> none  [the longest x42 69.1 us: unskew(): current = jnp.where(taken[:, None], moved, current)]
    psum x1, waiting for transfers between devices: 269 us -> 147 us  [body(): lax.psum(tuple((grad.astype(BF16) for grad in (grad_pool_weight, grad_que...]
    slice x126 -> x3, local copies, waits for them, and re-layouts: 118 us -> 2.36 us  [the longest x2 2.17 us: body(): grad_value_low = dkv_back[:, :, HEAD:].reshape(length, width)]
    all_gather x2 -> x0, waiting for transfers between devices: 112 us -> none  [the longest x1 65.4 us: body(): lax.all_gather(value_rows, 'seq', axis=1, tiled=True)]
    dynamic_update_slice x24 -> x3, local copies, waits for them, and re-layouts: 86 us -> 0.61 us  [at_head(): lax.dynamic_update_slice(jnp.zeros(shape, F32), part.reshape(shape[:-1] +...]
  transfers between devices with their start and end apart: 7 -> 3, of which waited for: 6 -> 1; matrix products, arithmetic and copies ran while one was open for 4% -> 5% of each run, Pallas kernels for 0% -> 0%
where the time goes in v1:
time: 445 us; the launch traced here: 444 us
  waiting for transfers between devices  147 us (33%)
  Pallas kernels  130 us (29%)
  blocking collectives  49.8 us (11%)
  matrix products  39.5 us (9%)
  local copies, waits for them, and re-layouts  35.1 us (8%)
  other arithmetic  21.9 us (5%)
  between operations  14.8 us (3%)
  starting transfers between devices  6.16 us (1%)
    psum x1, waiting for transfers between devices, body(): lax.psum(tuple((grad.astype(BF16) for grad in (grad_pool_weight, grad_que...  147 us
    pallas_call x4, Pallas kernels, exchange(): pl.pallas_call(functools.partial(kernel, n, group), out_shape=[jax.ShapeD...  70.7 us
    psum x1, blocking collectives, body(): small = lax.psum(jnp.concatenate(small_parts), ('dp', 'seq'))  47.9 us
    dot_general x24, matrix products, dot(): lax.dot_general(left, right, (dims, ((), ())), preferred_element_type=F32)  39.5 us
    pallas_call x1, Pallas kernels, body(): pl.pallas_call(functools.partial(back_kernel, n, group, tile), grid=(roun...  31.4 us
    pallas_call x1, Pallas kernels, body(): pl.pallas_call(functools.partial(attend_kernel, n, group, tile), grid=(ro...  27.7 us
  transfers between devices with their start and end apart: 3, of which 1 were waited for; matrix products, arithmetic and copies ran while one was open for 5% of the time, Pallas kernels for 0%

profile of v1, /device:TPU:0, one launch (start us, length us, event | category | flops | bytes accessed | tf_op | source)
XLA Modules:
  0.0 443.7 jit_solution(16151195737273746981)
XLA Ops:
  8.1 4.8 %collective-permute-start = (bf16[1,2,512]{2,1,0:T(2,128)(2,1)S(1)}, bf16[1,2,512]{2,1,0:T(2,128)(2,1)S(1)}, u32[]{:S(2)}, u32[]{:S(2)}) collective-permute-start(bf16[1,2,512]{2,1,0:T(2,128)(2,1)S(1)} %slice.18), channel_id=1, source_target_pairs={{0,1},{1,2},{2,3},{3,4},{4,5},{5,6},{6,7},{7,8},{8,9},{9,10},{10,1... | collective-permute-start | bytes 6152 | tf_op jit(solution)/shard_map/ppermute | solution.py:30
  13.0 1.9 all-gather
  16.3 1.9 constant_dynamic-slice_fusion.weight_ref
  19.5 2.8 fusion.21
  25.2 2.2 fusion.19
  29.1 1.8 copy.63
  32.0 2.0 convolution_convert_fusion.9
  33.9 1.8 copy.65
  35.7 1.9 copy.67
  41.1 15.3 %shard_map.400 = (bf16[8,96,128]{2,1,0:T(8,128)(2,1)S(1)}, bf16[16,192,128]{2,1,0:T(8,128)(2,1)S(1)}) custom-call(bf16[8,96,128]{2,1,0:T(8,128)(2,1)S(1)} %copy.68.refs_0_, bf16[8,192,128]{2,1,0:T(8,128)(2,1)S(1)} %maximum_bitcast_fusion.refs_1_), custom_call_target="tpu_custom_call" | custom-call | tf_op jit(solution)/shard_map/pallas_call | solution.py:162
  57.9 27.7 %shard_map.401 = (f32[8,192,64]{2,1,0:T(8,128)}, bf16[8,96,128]{2,1,0:T(8,128)(2,1)}, f32[8,192,128]{2,1,0:T(8,128)}, bf16[8,192,3072]{2,1,0:T(8,128)(2,1)}) custom-call(bf16[8,96,128]{2,1,0:T(8,128)(2,1)} %copy-done.3, bf16[3072,128]{1,0:T(8,128)(2,1)} %bitcast.81, bf16[3264,512]{1,0:T(8,128)(2,1)} %constant.131.clone.table_ref, ...), custom_call_target="tpu_custom_call" | custom-call | tf_op jit(solution)/shard_map/pallas_call | solution.py:437
  86.5 23.1 %shard_map.402 = bf16[8,96,128]{2,1,0:T(8,128)(2,1)S(1)} custom-call(bf16[8,96,128]{2,1,0:T(8,128)(2,1)S(1)} %copy-done.6), custom_call_target="tpu_custom_call" | custom-call | tf_op jit(solution)/shard_map/pallas_call | solution.py:162
  113.8 4.9 %multiply_convert_fusion = (bf16[192,2048]{1,0:T(8,128)(2,1)}, f32[192,2048]{1,0:T(8,128)S(1)}, f32[192,2048]{1,0:T(8,128)S(1)}) fusion(f32[2048]{0:T(1024)S(1)} %copy-done.47, bf16[512,2048]{1,0:T(8,128)(2,1)S(1)} %copy-done, f32[192,512]{1,0:T(8,128)S(1)} %get-tuple-element.83, f32[512]{0:T(512)S(1)} %copy-done.46, f32[512]{0:T(512)S(1)} %copy-done.42, ...), kind=kOutput, calls=%fused_computation.10 | convolution fusion | flops 429096960 | bytes 6436352 | tf_op jit(solution)/shard_map/dot_general | solution.py:24
  122.7 8.3 %shard_map.403.grad_ref = bf16[8,96,128]{2,1,0:T(8,128)(2,1)S(1)} custom-call(bf16[8,96,128]{2,1,0:T(8,128)(2,1)S(1)} %copy.73.refs_0_), custom_call_target="tpu_custom_call" | custom-call | tf_op jit(solution)/shard_map/pallas_call | solution.py:162
  131.7 31.4 %shard_map.404 = (bf16[8,96,128]{2,1,0:T(8,128)(2,1)}, bf16[3072,128]{1,0:T(8,128)(2,1)}, f32[512,64]{1,0:T(8,128)}, f32[1,64]{1,0:T(1,128)}, f32[1,64]{1,0:T(1,128)}) custom-call(bf16[8,96,128]{2,1,0:T(8,128)(2,1)} %copy-done.3, bf16[3072,128]{1,0:T(8,128)(2,1)} %bitcast.82, bf16[3264,512]{1,0:T(8,128)(2,1)} %constant.131.clone.table_ref, ...), custom_call_target="tpu_custom_call" | custom-call | tf_op jit(solution)/shard_map/pallas_call | solution.py:507
  165.1 24.1 %shard_map.405 = (bf16[8,96,128]{2,1,0:T(8,128)(2,1)S(1)}, bf16[2,8,192,128]{3,2,1,0:T(8,128)(2,1)S(1)}) custom-call(bf16[8,96,128]{2,1,0:T(8,128)(2,1)S(1)} %copy-done.7, bf16[16,192,128]{2,1,0:T(8,128)(2,1)S(1)} %bitcast.83), custom_call_target="tpu_custom_call" | custom-call | tf_op jit(solution)/shard_map/pallas_call | solution.py:162
  189.9 2.2 fusion.22
  194.3 2.2 convolution_convert_fusion.1
  196.5 2.1 convolution_convert_fusion
  201.7 2.1 convolution_add_fusion.4
  207.3 1.7 convolution_convert_fusion.3
  209.0 1.7 convolution_convert_fusion.2
  212.2 3.0 convolution_add_fusion
  215.2 1.7 reshape.158
  216.9 1.8 fusion.23
  218.7 1.6 reshape.167
  222.0 47.9 %psum.71 = f32[7680]{0:T(1024)S(1)} all-reduce(f32[7680]{0:T(1024)S(1)} %constant_dynamic-update-slice_fusion), channel_id=1, replica_groups=mesh['dp'=2,'seq'=16] {'dp','seq'}, use_global_device_ids=true, to_apply=%region_18.19 | all-reduce | flops 7680 | bytes 61440 | tf_op jit(solution)/shard_map/psum | solution.py:583
  273.8 146.6 %all-reduce.3.cloned.1.call-done = (bf16[1536,512]{1,0:T(8,128)(2,1)}, bf16[512,512]{1,0:T(8,128)(2,1)}, bf16[512,512]{1,0:T(8,128)(2,1)}, bf16[512,512]{1,0:T(8...) async-done(((bf16[1536,512]{1,0:T(8,128)(2,1)}, ...) | async-done | bytes 9961488 | tf_op jit(solution)/shard_map/psum | solution.py:570
  420.4 3.6 convert_element_type.141
  429.6 2.5 convert_element_type.157
  432.1 2.6 convert_element_type.159
  434.7 2.1 convert_element_type.161
  (186 shorter events, 47.8 us)
Async XLA Ops:
  7.2 106.5 %copy-start = (bf16[512,2048]{1,0:T(8,128)(2,1)S(1)}, bf16[512,2048]{1,0:T(8,128)(2,1)}, u32[]{:S(2)}) copy-start(bf16[512,2048]{1,0:T(8,128)(2,1)} %param.40) | copy-start | bytes 6291460
  7.2 413.2 %all-reduce.3.cloned.1.call-start = ((), (), s32[]{:S(2)}) async-start(), calls=%async_computation | async-start | bytes 19922944 | tf_op jit(solution)/shard_map/psum | solution.py:570
  8.1 14.7 %collective-permute-start = (bf16[1,2,512]{2,1,0:T(2,128)(2,1)S(1)}, bf16[1,2,512]{2,1,0:T(2,128)(2,1)S(1)}, u32[]{:S(2)}, u32[]{:S(2)}) collective-permute-start(bf16[1,2,512]{2,1,0:T(2,128)(2,1)S(1)} %slice.18), channel_id=1, source_target_pairs={{0,1},{1,2},{2,3},{3,4},{4,5},{5,6},{6,7},{7,8},{8,9},{9,10},{10,1... | collective-permute-start | bytes 6152 | tf_op jit(solution)/shard_map/ppermute | solution.py:30
  16.2 7.5 %copy-start.8 = (bf16[192,1536]{1,0:T(8,128)(2,1)}, bf16[192,1536]{1,0:T(8,128)(2,1)S(1)}, u32[]{:S(2)}) copy-start(bf16[192,1536]{1,0:T(8,128)(2,1)S(1)} %reshape.159) | copy-start | bytes 1769476
  16.3 6.5 %copy-start.15 = (bf16[1,576,512]{2,1,0:T(8,128)(2,1)S(1)}, bf16[1,576,512]{2,1,0:T(8,128)(2,1)}, u32[]{:S(2)}) copy-start(bf16[1,576,512]{2,1,0:T(8,128)(2,1)} %param.25) | copy-start | bytes 1769476
  22.3 2.9 copy-start.45
  25.1 2.7 copy-start.11
  25.1 2.5 copy-start.40
  25.2 2.5 copy-start.43
  25.2 2.6 copy-start.26
  29.1 8.5 %copy-start.22 = (bf16[512,512]{1,0:T(8,128)(2,1)S(1)}, bf16[512,512]{1,0:T(8,128)(2,1)}, u32[]{:S(2)}) copy-start(bf16[512,512]{1,0:T(8,128)(2,1)} %param.32) | copy-start | bytes 1572868
  109.8 3.9 copy-start.42
  109.8 3.9 copy-start.46
  109.8 3.9 copy-start.47
  113.8 4.9 %copy-start.13 = (f32[192,512]{1,0:T(8,128)S(1)}, f32[192,512]{1,0:T(8,128)}, u32[]{:S(2)}) copy-start(f32[192,512]{1,0:T(8,128)} %fusion.21) | copy-start | bytes 1179652
  113.8 4.9 %copy-start.27 = (bf16[2048,512]{1,0:T(8,128)(2,1)S(1)}, bf16[2048,512]{1,0:T(8,128)(2,1)}, u32[]{:S(2)}) copy-start(bf16[2048,512]{1,0:T(8,128)(2,1)} %param.42) | copy-start | bytes 6291460
  189.4 3.8 copy-start.19
  189.8 4.4 %copy-start.33 = (bf16[192,2048]{1,0:T(8,128)(2,1)S(1)}, bf16[192,2048]{1,0:T(8,128)(2,1)}, u32[]{:S(2)}) copy-start(bf16[192,2048]{1,0:T(8,128)(2,1)} %copy-done.32) | copy-start | bytes 2359300
  199.4 2.3 copy-start.23
  201.7 4.5 %copy-start.24 = (bf16[512,512]{1,0:T(8,128)(2,1)S(1)}, bf16[512,512]{1,0:T(8,128)(2,1)}, u32[]{:S(2)}) copy-start(bf16[512,512]{1,0:T(8,128)(2,1)} %param.33) | copy-start | bytes 1572868
  203.8 2.4 copy-start.31
  206.8 2.3 copy-start.9
  218.7 3.0 copy-start.49
  218.7 3.1 copy-start.48
  218.7 51.1 %copy-start.16 = (bf16[1,576,512]{2,1,0:T(8,128)(2,1)S(1)}, bf16[1,576,512]{2,1,0:T(8,128)(2,1)}, u32[]{:S(2)}) copy-start(bf16[1,576,512]{2,1,0:T(8,128)(2,1)} %param.25) | copy-start | bytes 1769476
  220.3 52.5 %collective-permute-start.1 = (f32[1,2,512]{2,1,0:T(2,128)S(1)}, f32[1,2,512]{2,1,0:T(2,128)S(1)}, u32[]{:S(2)}, u32[]{:S(2)}) collective-permute-start(f32[1,2,512]{2,1,0:T(2,128)S(1)} %slice.27), channel_id=1, source_target_pairs={{1,0},{2,1},{3,2},{4,3},{5,4},{6,5},{7,6},{8,7},{9,8},{10,9},{11,1... | collective-permute-start | bytes 12296 | tf_op jit(solution)/shard_map/ppermute | solution.py:30
  420.4 3.6 copy-start.38
  424.0 2.2 copy-start.36
  425.1 2.2 copy-start.35
  426.2 2.2 copy-start.34
  429.6 2.5 copy-start.20
  432.1 2.6 copy-start.30
  (21 other events, 29.1 us)
Sparse Core Ops, SparseCore 0:
  212.2 208.2 all-reduce.2

commit v2 on v1

--- a/solution.py
+++ b/solution.py
@@ -1,4 +1,5 @@
 import functools
+import types
 
 import jax
 import jax.numpy as jnp
@@ -595,10 +596,792 @@
     )
 
 
+EARLY_ROWS, LATE_ROWS = 6144, 3584
+SMALL_ROWS = 16
+FAR_SHARE = {EARLY_ROWS: 768, LATE_ROWS: 512}
+OVER_ROWS = ((0,), (0,))
+OVER_COLUMNS = ((1,), (1,))
+
+
+class Reduction:
+    def __init__(self, buffer, bufs, sems, free, small=None):
+        self.buffer, self.sems, self.free = buffer, sems, free
+        (self.from_core, self.near_one, self.near_two, self.near_z, self.far_z, self.far_one, self.far_two) = bufs
+        self.small = small
+        rows = buffer.shape[0]
+        self.half = rows // 2
+        self.far_size = FAR_SHARE[rows]
+        self.near_size = self.half - self.far_size
+        core, chip = lax.axis_index("dp"), lax.axis_index("seq")
+        self.core, self.chip = core, chip
+        self.z = chip // 4
+        bit_x, bit_y = chip % 2, (chip // 2) % 2
+        first_x = core == 0
+        self.peer_x, self.peer_y = chip + 1 - 2 * bit_x, chip + 2 - 4 * bit_y
+        self.bit_one = jnp.where(first_x, bit_x, bit_y)
+        self.bit_two = jnp.where(first_x, bit_y, bit_x)
+        step_one = jnp.where(first_x, 1, 2)
+        step_two = 3 - step_one
+        self.peer_one = chip + jnp.where(self.bit_one == 0, step_one, -step_one)
+        self.peer_two = chip + jnp.where(self.bit_two == 0, step_two, -step_two)
+        base = core * self.half
+        near, far = self.near_size, self.far_size
+        self.near_at = base
+        self.near_one_at = base + self.bit_one * (near // 2)
+        self.near_one_out = base + (1 - self.bit_one) * (near // 2)
+        self.near_two_at = self.near_one_at + self.bit_two * (near // 4)
+        self.near_two_out = self.near_one_at + (1 - self.bit_two) * (near // 4)
+        self.near_z_at = self.near_two_at + self.z * (near // 16)
+        self.far_at = base + near
+        self.far_z_at = self.far_at + self.z * (far // 4)
+        self.far_one_at = self.far_z_at + self.bit_one * (far // 8)
+        self.far_one_out = self.far_z_at + (1 - self.bit_one) * (far // 8)
+        self.far_two_at = self.far_one_at + self.bit_two * (far // 16)
+        self.far_two_out = self.far_one_at + (1 - self.bit_two) * (far // 16)
+
+    def rows(self, start, size):
+        return self.buffer.at[pl.ds(pl.multiple_of(start, 16), size)]
+
+    def copy(self, index, source, target, core, chip):
+        return pltpu.make_async_remote_copy(
+            source, target, self.sems.at[0, index], self.sems.at[1, index],
+            device_id=(core, chip), device_id_type=MESH,
+        )
+
+    def go(self, index, source, target, core, chip):
+        self.copy(index, source, target, core, chip).start()
+
+    def done(self, index, source):
+        copy = self.copy(index, source, source, self.core, self.peer_one)
+        copy.wait_send()
+        copy.wait_recv()
+
+
+    def freed(self, index, *devices):
+        for core, chip in devices:
+            pl.semaphore_signal(self.free.at[index], inc=1, device_id=(core, chip), device_id_type=MESH)
+
+    def z_peers(self):
+        return [(self.core, self.z_chip(away)[1]) for away in range(3)]
+
+    def is_free(self, index, count=1):
+        pl.semaphore_wait(self.free.at[index], count)
+
+    def add(self, start, size, parts):
+        chunk = min(size, 256)
+        while size % chunk:
+            chunk -= 16
+
+        def one(step, carry):
+            at = pl.ds(pl.multiple_of(start + step * chunk, 16), chunk)
+            here = pl.ds(pl.multiple_of(step * chunk, 16), chunk)
+            total = self.buffer[at].astype(F32)
+            for part in parts:
+                total = total + part[here].astype(F32)
+            self.buffer[at] = total.astype(BF16)
+            return carry
+
+        lax.fori_loop(0, size // chunk, one, 0)
+
+    def z_chip(self, away):
+        there = (self.z + 1 + away) % 4
+        return there, self.chip + (there - self.z) * 4
+
+    def small_go(self, stage, core, chip):
+        if self.small is not None:
+            own, taken = self.small
+            self.go(18 + stage, own, taken.at[stage], core, chip)
+
+    def small_done(self, stage):
+        if self.small is not None:
+            own, taken = self.small
+            self.done(18 + stage, own)
+            own[...] = own[...] + taken[stage]
+
+    def small_z_go(self):
+        if self.small is not None:
+            own, taken = self.small
+            taken[3 + self.z] = own[...]
+            for away in range(3):
+                peer = self.z_chip(away)[1]
+                self.go(21 + away, own, taken.at[3 + self.z], self.core, peer)
+
+    def small_z_done(self):
+        if self.small is not None:
+            own, taken = self.small
+            for away in range(3):
+                self.done(21 + away, own)
+            own[...] = (taken[3] + taken[4]) + (taken[5] + taken[6])
+
+    def step(self, number):
+        near, far = self.near_size, self.far_size
+        core, chip = self.core, self.chip
+        if number == 0:
+            self.go(0, self.rows((1 - core) * self.half, self.half), self.from_core, 1 - core, chip)
+            self.small_go(0, 1 - core, chip)
+        if number == 1:
+            self.done(0, self.from_core)
+            self.freed(0, (1 - core, chip))
+            self.add(core * self.half, self.half, (self.from_core,))
+            self.go(1, self.rows(self.near_one_out, near // 2), self.near_one, core, self.peer_one)
+            for away in range(3):
+                there, peer = self.z_chip(away)
+                self.go(3 + away, self.rows(self.far_at + there * (far // 4), far // 4), self.far_z.at[away], core, peer)
+            self.small_done(0)
+            self.small_go(1, core, self.peer_x)
+        if number == 2:
+            self.done(1, self.near_one)
+            self.freed(1, (core, self.peer_one))
+            self.add(self.near_one_at, near // 2, (self.near_one,))
+            self.go(2, self.rows(self.near_two_out, near // 4), self.near_two, core, self.peer_two)
+            for away in range(3):
+                self.done(3 + away, self.far_z.at[away])
+            self.freed(4, *self.z_peers())
+            self.add(self.far_z_at, far // 4, tuple(self.far_z.at[away] for away in range(3)))
+            self.go(6, self.rows(self.far_one_out, far // 8), self.far_one, core, self.peer_one)
+            self.small_done(1)
+            self.small_go(2, core, self.peer_y)
+        if number == 3:
+            self.done(2, self.near_two)
+            self.freed(2, (core, self.peer_two))
+            self.add(self.near_two_at, near // 4, (self.near_two,))
+            for away in range(3):
+                there, peer = self.z_chip(away)
+                self.go(
+                    7 + away, self.rows(self.near_two_at + there * (near // 16), near // 16),
+                    self.near_z.at[away], core, peer,
+                )
+            self.done(6, self.far_one)
+            self.freed(5, (core, self.peer_one))
+            self.add(self.far_one_at, far // 8, (self.far_one,))
+            self.go(10, self.rows(self.far_two_out, far // 16), self.far_two, core, self.peer_two)
+            self.small_done(2)
+            self.small_z_go()
+        if number == 4:
+            for away in range(3):
+                self.done(7 + away, self.near_z.at[away])
+            self.freed(3, *self.z_peers())
+            self.add(self.near_z_at, near // 16, tuple(self.near_z.at[away] for away in range(3)))
+            own = self.rows(self.near_z_at, near // 16)
+            self.is_free(3, 3)
+            for away in range(3):
+                self.go(11 + away, own, own, core, self.z_chip(away)[1])
+            self.done(10, self.far_two)
+            self.freed(6, (core, self.peer_two))
+            self.add(self.far_two_at, far // 16, (self.far_two,))
+            own = self.rows(self.far_two_at, far // 16)
+            self.is_free(6)
+            self.go(14, own, own, core, self.peer_two)
+            self.small_z_done()
+        if number == 5:
+            for away in range(3):
+                self.done(11 + away, self.rows(self.near_z_at, near // 16))
+            own = self.rows(self.near_two_at, near // 4)
+            self.is_free(2)
+            self.go(15, own, own, core, self.peer_two)
+            self.done(14, self.rows(self.far_two_at, far // 16))
+            own = self.rows(self.far_one_at, far // 8)
+            self.is_free(5)
+            self.go(16, own, own, core, self.peer_one)
+        if number == 6:
+            self.done(15, self.rows(self.near_two_at, near // 4))
+            own = self.rows(self.near_one_at, near // 2)
+            self.is_free(1)
+            self.go(17, own, own, core, self.peer_one)
+            self.done(16, self.rows(self.far_one_at, far // 8))
+            own = self.rows(self.far_z_at, far // 4)
+            self.is_free(4, 3)
+            for away in range(3):
+                self.go(24 + away, own, own, core, self.z_chip(away)[1])
+        if number == 7:
+            self.done(17, self.rows(self.near_one_at, near // 2))
+            own = self.rows(self.near_at, near)
+            self.is_free(0)
+            self.go(27, own, own, 1 - core, chip)
+            for away in range(3):
+                self.done(24 + away, self.rows(self.far_z_at, far // 4))
+            own = self.rows(self.far_at, far)
+            self.go(28, own, own, 1 - core, chip)
+        if number == 8:
+            self.done(27, self.rows(self.near_at, near))
+            self.done(28, self.rows(self.far_at, far))
+
+
+REDUCTION_SEMS = 29
+
+
+def reduction_scratch(rows):
+    far = FAR_SHARE[rows]
+    near = rows // 2 - far
+    return [
+        pltpu.VMEM(shape + (512,), BF16)
+        for shape in (
+            (rows // 2,), (near // 2,), (near // 4,), (3, near // 16), (3, far // 4), (far // 8,), (far // 16,),
+        )
+    ]
+
+
+def gelu_pair(value):
+    falling = jnp.exp(value * value * -0.5)
+    turn = 1.0 / (1.0 + 0.3275911 * 0.7071067811865476 * jnp.abs(value))
+    series = turn * (
+        0.254829592
+        + turn * (-0.284496736 + turn * (1.421413741 + turn * (-1.453152027 + turn * 1.061405429)))
+    )
+    tail = 0.5 * series * falling
+    share = jnp.where(value >= 0, 1.0 - tail, tail)
+    return value * share, share + value * falling * 0.3989422804014327
+
+
+def norm_parts(hidden):
+    average = jnp.mean(hidden, -1, keepdims=True)
+    centred = hidden - average
+    inverse = lax.rsqrt(jnp.mean(centred * centred, -1, keepdims=True) + epsilon)
+    return centred * inverse, inverse
+
+
+def norm_grad(grad_out, normed, inverse, gain):
+    scaled = grad_out * gain
+    return inverse * (
+        scaled
+        - jnp.mean(scaled, -1, keepdims=True)
+        - normed * jnp.mean(scaled * normed, -1, keepdims=True)
+    )
+
+
+def column_sum(value):
+    return jnp.sum(value, 0, keepdims=True)
+
+
+def layer_kernel(n, length, layout, *refs):
+    taken = iter(refs)
+    given, vectors, outs, scratch = ({name: next(taken) for name in part} for part in layout)
+    r = types.SimpleNamespace(**vectors, **outs, **scratch)
+    group = 2
+    rounds = n // group
+    tile = 2 * length
+    half_len = length // 2
+    width = 512
+    scale = HEAD**-0.5
+    core, chip, row, head, member = whereabouts(group)
+    count = 2 * n
+    me = core * n + chip
+
+    loads = {}
+    r.early_parts, r.late_parts = refs[-14:-7], refs[-7:]
+    for index, (name, source) in enumerate(given.items()):
+        loads[name] = pltpu.make_async_copy(source, scratch[name], r.load_sem.at[index])
+        loads[name].start()
+
+    def ready(*which):
+        for ref in which:
+            next(loads[name] for name in given if scratch[name] is ref).wait()
+
+    barrier = pltpu.get_barrier_semaphore()
+
+    def greet(step, carry):
+        other = (me + step) % count
+        pl.semaphore_signal(barrier, inc=1, device_id=(other // n, other % n), device_id_type=MESH)
+        return carry
+
+    lax.fori_loop(1, count, greet, 0)
+
+    low_bound, high_bound = r.bounds[0, 0], r.bounds[0, 1]
+    r.edges[core, :8] = jnp.full((8, 128), low_bound, jnp.int32)
+    r.edges[core, 8:] = jnp.full((8, 128), high_bound, jnp.int32)
+    ready(r.x3, r.pool_w)
+    own = dot(r.x3[:, :width], r.pool_w[2 * width :])
+    before = dot(r.x3[:, width:], r.pool_w[: 2 * width])
+    pl.semaphore_wait(barrier, count - 1)
+
+    def edge_copy():
+        return pltpu.make_async_remote_copy(
+            r.edges.at[core], r.edges.at[core], r.side_sem.at[0], r.side_sem.at[1],
+            device_id=(1 - core, chip), device_id_type=MESH,
+        )
+
+    def rim_copy():
+        return pltpu.make_async_remote_copy(
+            r.x3.at[length - 16 :, width:], r.rim, r.side_sem.at[2], r.side_sem.at[3],
+            device_id=(core, (chip + 1) % n), device_id_type=MESH,
+        )
+
+    edge_copy().start()
+
+    @pl.when(chip < n - 1)
+    def _():
+        rim_copy().start()
+
+    @pl.when(chip == 0)
+    def _():
+        r.rim[...] = jnp.zeros_like(r.rim)
+
+    @pl.when(chip > 0)
+    def _():
+        rim_copy().wait_recv()
+
+    rim_sum = dot(r.rim[...], r.pool_w[: 2 * width])
+    at_row = lax.broadcasted_iota(jnp.int32, (length, width), 0)
+    before = jnp.where(at_row == 0, rim_sum[15:16], pltpu.roll(before, 1, 0))
+    pooled = own + before + r.pool_b[...]
+    r.pooled[...] = pooled
+    plain, _ = norm_parts(pooled)
+    attn_in = (plain * r.ln1_g[...] + r.ln1_b[...]).astype(BF16)
+    r.attn_in[...] = attn_in
+    ready(r.q_w, r.k_w, r.v_w)
+    query = dot(attn_in, r.q_w[...])
+    keys = dot(attn_in, r.k_w[...])
+    values = dot(attn_in, r.v_w[...])
+    for h in range(HEADS):
+        at = slice(h * HEAD, (h + 1) * HEAD)
+        r.q_out[h] = packed(query[:, at]).astype(BF16)
+        r.kv_out[h] = jnp.concatenate([keys[:, at], values[:, at]], 1).astype(BF16)
+    turn_to, spot_to = place_of(chip, group)
+
+    def q_jobs(array, out, sem, recv):
+        jobs = []
+        for h in range(HEADS):
+            to_chip, to_core = chip_of(core, h, spot_to, group)
+            jobs.append((array.at[h], out.at[turn_to], (sem, recv.at[turn_to]), to_core, to_chip))
+        return jobs
+
+    kv_jobs = []
+    for h in range(HEADS):
+        for g in range(group):
+            to_chip, to_core = chip_of(core, h, g, group)
+            kv_jobs.append(
+                (r.kv_out.at[h], r.kv.at[chip], (r.send_sem.at[1], r.kv_sem.at[chip]), jnp.int32(to_core), to_chip)
+            )
+    first_jobs = q_jobs(r.q_out, r.q, r.send_sem.at[0], r.q_sem) + kv_jobs
+    for job in first_jobs:
+        send(*job)
+
+    ready(r.ct3, r.up_w, r.ffn_out)
+    grad_final = dot(r.ct3[...], r.up_w[...], OVER_COLUMNS)
+    r.grad_final[...] = grad_final
+    grad_branch = grad_final.astype(BF16)
+    r.grad_branch[...] = grad_branch
+    for part in range(4):
+        at = slice(part * width, (part + 1) * width)
+        r.grad_act[:, at] = dot(grad_branch, r.ffn_out[at], OVER_COLUMNS)
+    small = r.small
+    small[...] = jnp.zeros_like(small)
+    small[11:12] = column_sum(grad_branch.astype(F32))
+    for part in range(3):
+        at = slice(part * width, (part + 1) * width)
+        small[12 + part : 13 + part] = column_sum(r.ct3[:, at].astype(F32))
+
+    ready(r.pos_w, r.table)
+    odd = head % 2 == 1
+    pair_at = pl.ds(pl.multiple_of((head // 2) * PAIR, PAIR), PAIR)
+
+    def of_head(ref):
+        both = ref[:, pair_at].astype(F32)
+        return jnp.where(odd, both[:, HEAD:], both[:, :HEAD])
+
+    r.head_w[...] = of_head(r.pos_w).astype(BF16)
+    content_bias, pos_bias = of_head(r.content), of_head(r.pos)
+    edge_copy().wait_send()
+    edge_copy().wait_recv()
+    low_edge = r.edges[row, 0:1, 0:1]
+    high_edge = r.edges[row, 8:9, 0:1]
+    half = width // 2
+    lanes = lax.broadcasted_iota(jnp.int32, (length, tile), 1)
+
+    def rows_of(array):
+        return pl.ds(pl.multiple_of(array, length), tile)
+
+    def attend(turn, carry):
+        block = block_of(turn, member, group)
+        arrived(r.q.at[turn], r.q_sem.at[turn])
+        for other in range(group):
+            arrived(r.kv.at[turn * group + other], r.kv_sem.at[turn * group + other])
+        query_u, _, turned = query_parts(
+            r.q[turn], content_bias, pos_bias, r.head_w[...], r.sines[...], r.cosines[...]
+        )
+        head_part = (query_u.astype(F32) * scale).astype(BF16)
+        r.extra[:, :PAIR] = jnp.concatenate([head_part, jnp.zeros_like(head_part)], 1)
+        r.extra[:, PAIR:] = (turned * scale).astype(BF16)
+        places = block * length + lax.broadcasted_iota(jnp.int32, (length, 1), 0)
+        opening = jnp.where(places >= high_edge, high_edge, jnp.where(places >= low_edge, low_edge, 0))
+
+        def score_step(step, top):
+            pair = r.kv[pl.ds(step * group, group)].reshape(tile, PAIR)
+            waves = r.table[rows_of((n - 1 - block) * length + step * tile), :]
+            score = dot(r.extra[:, :PAIR], pair, OVER_COLUMNS) + dot(r.extra[:, PAIR:], waves, OVER_COLUMNS)
+            at = lanes + step * tile
+            allowed = jnp.logical_and(at <= places, at >= opening)
+            score = jnp.where(allowed, score, masked_score)
+            r.score[step] = score
+            for part in range(tile // 128):
+                top = jnp.maximum(top, score[:, part * 128 : (part + 1) * 128])
+            return top
+
+        top = lax.fori_loop(0, turn + 1, score_step, jnp.full((length, 128), masked_score, F32))
+        top = jnp.max(top, 1, keepdims=True)
+
+        def value_step(step, state):
+            total, summed = state
+            weight = jnp.exp(r.score[step] - top)
+            for part in range(tile // 128):
+                total = total + weight[:, part * 128 : (part + 1) * 128]
+            low = weight.astype(BF16)
+            r.keep[turn * (turn + 1) // 2 + step] = low
+            pair = r.kv[pl.ds(step * group, group)].reshape(tile, PAIR)
+            return total, summed + dot(low, pair)
+
+        total, summed = lax.fori_loop(
+            0, turn + 1, value_step, (jnp.zeros((length, 128), F32), jnp.zeros((length, PAIR), F32))
+        )
+        inverse = 1.0 / jnp.sum(total, 1, keepdims=True)
+        attended = summed[:, HEAD:] * inverse
+        r.att[turn] = jnp.concatenate([jnp.broadcast_to(inverse, (length, HEAD)), attended], 1)
+        r.att_out[turn] = packed(attended).astype(BF16)
+        send(
+            r.att_out.at[turn], r.att_in.at[head], (r.send_sem.at[2], r.att_sem.at[0]), row, block
+        )
+        return carry
+
+    lax.fori_loop(0, rounds, attend, 0)
+    for source, _, sems, to_core, to_chip in first_jobs:
+        sent(source, sems[0], to_core, to_chip)
+
+    def joined(get):
+        parts = [get(h) for h in range(HEADS)]
+        upper = jnp.concatenate([part[:, :HEAD] for part in parts], 1)
+        lower = jnp.concatenate([part[:, HEAD:] for part in parts], 1)
+        return jnp.concatenate([upper, lower], 0)
+
+    arrived(r.att_in, r.att_sem.at[0])
+    ready(r.out_w, r.ffn_in)
+    att_low = joined(lambda h: r.att_in[h].astype(F32)).astype(BF16)
+    r.att_low[...] = att_low
+    mixed = r.pooled[...] + dot(att_low, r.out_w[...])
+    r.mixed[...] = mixed
+    plain_two, inverse_two = norm_parts(mixed)
+    ffn_input = (plain_two * r.ln2_g[...] + r.ln2_b[...]).astype(BF16)
+    r.ffn_input[...] = ffn_input
+    grad_normed = jnp.zeros((length, width), F32)
+    for part in range(4):
+        at = slice(part * width, (part + 1) * width)
+        pre_act = dot(ffn_input, r.ffn_in[:, at]) + r.ffn_in_b[:, at]
+        act, slope = gelu_pair(pre_act)
+        r.act_low[:, at] = act.astype(BF16)
+        grad_pre = (r.grad_act[:, at] * slope).astype(BF16)
+        r.grad_pre[:, at] = grad_pre
+        small[7 + part : 8 + part] = column_sum(grad_pre.astype(F32))
+        grad_normed = grad_normed + dot(grad_pre, r.ffn_in[:, at], OVER_COLUMNS)
+    small[5:6] = column_sum(grad_normed * plain_two)
+    small[6:7] = column_sum(grad_normed)
+    grad_mixed = r.grad_final[...] + norm_grad(grad_normed, plain_two, inverse_two, r.ln2_g[...])
+    r.grad_final[...] = grad_mixed
+    grad_mixed_low = grad_mixed.astype(BF16)
+    grad_att = dot(grad_mixed_low, r.out_w[...], OVER_COLUMNS)
+    for h in range(HEADS):
+        r.q_out[h] = packed(grad_att[:, h * HEAD : (h + 1) * HEAD]).astype(BF16)
+    second_jobs = q_jobs(r.q_out, r.grad, r.send_sem.at[3], r.grad_sem)
+    for job in second_jobs:
+        send(*job)
+
+    early, late = r.early, r.late
+    for part in range(4):
+        at = slice(part * width, (part + 1) * width)
+        early[at] = dot(r.ffn_input[...], r.grad_pre[:, at], OVER_ROWS).astype(BF16)
+        early[2048 + part * width : 2048 + (part + 1) * width] = dot(
+            r.act_low[:, at], r.grad_branch[...], OVER_ROWS
+        ).astype(BF16)
+    early[5632:] = dot(r.att_low[...], grad_mixed_low, OVER_ROWS).astype(BF16)
+    final_low = (r.mixed[...] + dot(r.act_low[...], r.ffn_out[...]) + r.ffn_out_b[...]).astype(BF16)
+    for part in range(3):
+        at = slice(part * width, (part + 1) * width)
+        early[4096 + part * width : 4096 + (part + 1) * width] = dot(final_low, r.ct3[:, at], OVER_ROWS).astype(BF16)
+    first_sum = Reduction(early, r.early_parts, r.early_sem, r.early_free)
+    first_sum.step(0)
+    for part in range(3):
+        at = slice(part * width, (part + 1) * width)
+        lifted = dot(final_low, r.up_w[:, at]) + r.up_b[:, at]
+        r.out3[:, at] = (r.x3[:, at].astype(F32) + lifted).astype(BF16)
+
+    r.dkv[...] = jnp.zeros_like(r.dkv)
+    r.dhead[...] = jnp.zeros_like(r.dhead)
+    r.dbias[...] = jnp.zeros_like(r.dbias)
+
+    def back(index, carry):
+        turn = rounds - 1 - index
+        block = block_of(turn, member, group)
+        arrived(r.grad.at[turn], r.grad_sem.at[turn])
+        query = unpacked(r.q[turn].astype(F32))
+        query_u = ((query + content_bias).astype(BF16).astype(F32) * scale).astype(BF16)
+        query_v = (query + pos_bias).astype(BF16)
+        grad = unpacked(r.grad[turn].astype(F32))
+        inverse = r.att[turn][:, :HEAD]
+        grad_part = grad * inverse
+        delta = jnp.sum(grad_part * r.att[turn][:, HEAD:], 1, keepdims=True)
+        nothing = jnp.zeros((length, HEAD), F32)
+        r.extra[:, :PAIR] = jnp.concatenate([nothing, grad_part], 1).astype(BF16)
+        r.extra[:, PAIR : 2 * PAIR] = jnp.concatenate([query_u.astype(F32), nothing], 1).astype(BF16)
+        r.near[...] = jnp.zeros_like(r.near)
+        r.far[...] = jnp.zeros_like(r.far)
+
+        def step_over(step, inner):
+            pair = r.kv[pl.ds(step * group, group)].reshape(tile, PAIR)
+            waves = r.table[rows_of((n - 1 - block) * length + step * tile), :]
+            weight = r.keep[turn * (turn + 1) // 2 + step]
+            grad_weight = dot(r.extra[:, :PAIR], pair, OVER_COLUMNS)
+            grad_score = (weight.astype(F32) * (grad_weight - delta)).astype(BF16)
+            r.near[...] += dot(grad_score, pair)
+            r.far[...] += dot(grad_score, waves)
+            at = pl.ds(pl.multiple_of(step * tile, tile), tile)
+            r.dkv[at] += dot(grad_score, r.extra[:, PAIR : 2 * PAIR], OVER_ROWS) + dot(
+                weight, r.extra[:, :PAIR], OVER_ROWS
+            )
+            return inner
+
+        lax.fori_loop(0, turn + 1, step_over, 0)
+        at = pl.ds(pl.multiple_of(turn * tile, tile), tile)
+        r.dkv_out[pl.ds(turn * group, group)] = r.dkv[at].astype(BF16).reshape(group, length, PAIR)
+        for other in range(group):
+            key_block = turn * group + other
+            send(
+                r.dkv_out.at[key_block], r.dkv_in.at[member, head],
+                (r.send_sem.at[4], r.dkv_sem.at[0]), row, key_block,
+            )
+        grad_u = r.near[:, :HEAD] * scale
+        turn_sin, turn_cos = r.sines[...], r.cosines[...]
+        on_sin, on_cos = r.far[:, :half] * scale, r.far[:, half:] * scale
+        lift = on_cos * turn_sin - on_sin * turn_cos
+        rest = on_cos * turn_cos + on_sin * turn_sin
+        spread = jnp.concatenate([lift, rest], 1).astype(BF16)
+        grad_v = dot(spread, r.head_w[...])
+        r.dhead[...] += dot(spread, query_v, OVER_ROWS)
+        r.dbias[0:1] += column_sum(grad_u)
+        r.dbias[1:2] += column_sum(grad_v)
+        r.dq_out[turn] = packed(grad_u + grad_v).astype(BF16)
+        send(r.dq_out.at[turn], r.dq_in.at[head], (r.send_sem.at[5], r.dq_sem.at[0]), row, block)
+        for when, number in EARLY_STEPS:
+
+            @pl.when(index == when)
+            def _(number=number):
+                first_sum.step(number)
+
+        return carry
+
+    lax.fori_loop(0, rounds, back, 0)
+    first_left = [number for number in range(1, 9) if number not in [number for _, number in EARLY_STEPS]]
+
+    late[2048 + 1024 :] = jnp.zeros((512, 512), BF16)
+    dhead = r.dhead[...]
+    nothing = jnp.zeros_like(dhead)
+    late[3072:, pair_at] = jnp.where(
+        odd, jnp.concatenate([nothing, dhead], 1), jnp.concatenate([dhead, nothing], 1)
+    ).astype(BF16)
+    nothing = jnp.zeros((2, HEAD), F32)
+    dbias = r.dbias[...][:2]
+    small[3:5, pair_at] = jnp.where(
+        odd, jnp.concatenate([nothing, dbias], 1), jnp.concatenate([dbias, nothing], 1)
+    )
+    for source, _, sems, to_core, to_chip in second_jobs:
+        sent(source, sems[0], to_core, to_chip)
+    for turn in range(rounds):
+        block = block_of(jnp.int32(turn), member, group)
+        sent(r.att_out.at[turn], r.send_sem.at[2], row, block)
+        sent(r.dq_out.at[turn], r.send_sem.at[5], row, block)
+    for block in range(n):
+        sent(r.dkv_out.at[block], r.send_sem.at[4], row, jnp.int32(block))
+    arrived(r.dq_in, r.dq_sem.at[0])
+    arrived(r.dkv_in, r.dkv_sem.at[0])
+    grad_query = joined(lambda h: r.dq_in[h].astype(F32)).astype(BF16)
+    both = [r.dkv_in[0, h].astype(F32) + r.dkv_in[1, h].astype(F32) for h in range(HEADS)]
+    grad_keys = jnp.concatenate([part[:, :HEAD] for part in both], 1).astype(BF16)
+    grad_values = jnp.concatenate([part[:, HEAD:] for part in both], 1).astype(BF16)
+    attn_in = r.attn_in[...]
+    late[1536:2048] = dot(attn_in, grad_query, OVER_ROWS).astype(BF16)
+    late[2048:2560] = dot(attn_in, grad_keys, OVER_ROWS).astype(BF16)
+    late[2560:3072] = dot(attn_in, grad_values, OVER_ROWS).astype(BF16)
+    grad_normed = (
+        dot(grad_query, r.q_w[...], OVER_COLUMNS)
+        + dot(grad_keys, r.k_w[...], OVER_COLUMNS)
+        + dot(grad_values, r.v_w[...], OVER_COLUMNS)
+    )
+    plain, inverse = norm_parts(r.pooled[...])
+    small[1:2] = column_sum(grad_normed * plain)
+    small[2:3] = column_sum(grad_normed)
+    grad_pooled = (r.grad_final[...] + norm_grad(grad_normed, plain, inverse, r.ln1_g[...])).astype(BF16)
+    r.grad_pooled[...] = grad_pooled
+    grad_pooled_wide = grad_pooled.astype(F32)
+    small[0:1] = column_sum(grad_pooled_wide)
+
+    def back_rim_copy():
+        return pltpu.make_async_remote_copy(
+            r.grad_pooled.at[:16], r.back_rim, r.side_sem.at[4], r.side_sem.at[5],
+            device_id=(core, (chip + n - 1) % n), device_id_type=MESH,
+        )
+
+    @pl.when(chip > 0)
+    def _():
+        back_rim_copy().start()
+
+    late[1024:1536] = dot(r.x3[:, :width], grad_pooled, OVER_ROWS).astype(BF16)
+    follow = pltpu.roll(grad_pooled_wide, length - 1, 0)
+    within = jnp.where(at_row == length - 1, 0.0, follow).astype(BF16)
+    at_rim = lax.broadcasted_iota(jnp.int32, (16, width), 0)
+    rim_row = jnp.where(at_rim == 15, jnp.broadcast_to(grad_pooled_wide[:1], (16, width)), 0.0).astype(BF16)
+    late[:1024] = (
+        dot(r.x3[:, width:], within, OVER_ROWS) + dot(r.rim[...], rim_row, OVER_ROWS)
+    ).astype(BF16)
+    second_sum = Reduction(late, r.late_parts, r.late_sem, r.late_free, (small, r.small_in))
+    second_sum.step(0)
+    if first_left:
+        first_sum.step(first_left.pop(0))
+
+    @pl.when(chip == n - 1)
+    def _():
+        r.back_rim[...] = jnp.zeros_like(r.back_rim)
+
+    @pl.when(chip < n - 1)
+    def _():
+        back_rim_copy().wait_recv()
+
+    next_row = r.back_rim[...].astype(F32)[:1]
+    follow = jnp.where(at_row == length - 1, next_row, follow).astype(BF16)
+    first_part = r.ct3[:, :width].astype(F32) + dot(grad_pooled, r.pool_w[2 * width :], OVER_COLUMNS)
+    r.grad3[:, :width] = first_part.astype(BF16)
+    other_part = r.ct3[:, width:].astype(F32) + dot(follow, r.pool_w[: 2 * width], OVER_COLUMNS)
+    r.grad3[:, width:] = other_part.astype(BF16)
+
+    @pl.when(chip < n - 1)
+    def _():
+        rim_copy().wait_send()
+
+    @pl.when(chip > 0)
+    def _():
+        back_rim_copy().wait_send()
+
+    for number in range(1, 9):
+        second_sum.step(number)
+        if first_left:
+            first_sum.step(first_left.pop(0))
+
+
+EARLY_STEPS = ((0, 1), (3, 2), (5, 3), (7, 4))
+
+
+def widen_kernel(early_ref, late_ref, *outs):
+    at = pl.program_id(0)
+    wide = jnp.where(at < EARLY_ROWS // 512, early_ref[...].astype(F32), late_ref[...].astype(F32))
+    for out, (start, blocks) in zip(outs, WIDENED):
+
+        @pl.when(jnp.logical_and(at >= start, at < start + blocks))
+        def _(out=out):
+            out[...] = wide
+
+
+WIDENED = ((0, 4), (4, 4), (8, 3), (11, 1), (12, 3), (15, 1), (16, 1), (17, 1), (18, 1))
+ACROSS = (True, False, True, False, False, False, False, False, False)
+
+
+def widened(early, late):
+    def out_spec(start, blocks, across):
+        def place(at):
+            block = jnp.clip(at - start, 0, blocks - 1)
+            return (0, block) if across else (block, 0)
+
+        return pl.BlockSpec((512, 512), place)
+
+    first = EARLY_ROWS // 512
+    return pl.pallas_call(
+        widen_kernel,
+        grid=(first + LATE_ROWS // 512,),
+        in_specs=[
+            pl.BlockSpec((512, 512), lambda at: (jnp.minimum(at, first - 1), 0)),
+            pl.BlockSpec((512, 512), lambda at: (jnp.maximum(at - first, 0), 0)),
+        ],
+        out_specs=[out_spec(*cut, across) for cut, across in zip(WIDENED, ACROSS)],
+        out_shape=[
+            jax.ShapeDtypeStruct((512, 512 * blocks) if across else (512 * blocks, 512), F32)
+            for (_, blocks), across in zip(WIDENED, ACROSS)
+        ],
+        compiler_params=pltpu.CompilerParams(vmem_limit_bytes=48 * 2**20),
+    )(early, late)
+
+
+def fused_body(
+    inputs, doc_bounds, pool_weight, pool_bias, ln1_gain, ln1_bias, query_weight, key_weight,
+    value_weight, out_weight, pos_weight, content_bias, pos_bias, ln2_gain, ln2_bias, ffn_in,
+    ffn_in_bias, ffn_out, ffn_out_bias, up_weight, up_bias, cotangent,
+):
+    _, bytes_here, width = inputs.shape
+    length = bytes_here // 3
+    n = lax.axis_size("seq")
+    tokens = n * length
+    rounds = n // 2
+    table, sines, cosines = wave_tables(tokens, length, width)
+    given = dict(
+        x3=inputs.reshape(length, 3 * width), pool_w=pool_weight, q_w=query_weight, k_w=key_weight, v_w=value_weight,
+        ct3=cotangent.reshape(length, 3 * width), up_w=up_weight, ffn_out=ffn_out, pos_w=pos_weight, table=table,
+        out_w=out_weight, ffn_in=ffn_in,
+    )
+    vectors = dict(
+        pool_b=pool_bias, ln1_g=ln1_gain, ln1_b=ln1_bias, content=content_bias, pos=pos_bias, ln2_g=ln2_gain,
+        ln2_b=ln2_bias, ffn_in_b=ffn_in_bias, ffn_out_b=ffn_out_bias, up_b=up_bias,
+    )
+    vectors = {name: vector[None] for name, vector in vectors.items()} | dict(sines=sines, cosines=cosines)
+    vmem = pl.BlockSpec(memory_space=pltpu.VMEM)
+    outs = dict(
+        out3=((length, 3 * width), BF16), grad3=((length, 3 * width), BF16), early=((EARLY_ROWS, 512), BF16),
+        late=((LATE_ROWS, 512), BF16), small=((SMALL_ROWS, 512), F32),
+    )
+    pair_half = (length // 2, PAIR)
+    block, wide = (length, width), (length, 4 * width)
+    dma, signal = pltpu.SemaphoreType.DMA, pltpu.SemaphoreType.REGULAR
+    scratch = {name: pltpu.VMEM(array.shape, array.dtype) for name, array in given.items()}
+    low = dict(
+        rim=(16, 2 * width), back_rim=(16, width), attn_in=block, q_out=(HEADS,) + pair_half,
+        kv_out=(HEADS, length, PAIR), q=(rounds,) + pair_half, kv=(n, length, PAIR), grad_branch=block,
+        head_w=(width, HEAD), extra=(length, PAIR + width), keep=(rounds * (rounds + 1) // 2, length, 2 * length),
+        att_out=(rounds,) + pair_half, att_in=(HEADS,) + pair_half, att_low=block, ffn_input=block, act_low=wide,
+        grad_pre=wide, grad=(rounds,) + pair_half, dkv_out=(n, length, PAIR), dkv_in=(2, HEADS, length, PAIR),
+        dq_out=(rounds,) + pair_half, dq_in=(HEADS,) + pair_half, grad_pooled=block,
+    )
+    full = dict(
+        pooled=block, grad_final=block, grad_act=wide, score=(rounds, length, 2 * length), att=(rounds, length, PAIR),
+        mixed=block, dkv=(tokens, PAIR), dhead=(width, HEAD), dbias=(8, HEAD), near=(length, PAIR), far=block,
+        small_in=(7, SMALL_ROWS, 512),
+    )
+    scratch |= {name: pltpu.VMEM(shape, BF16) for name, shape in low.items()}
+    scratch |= {name: pltpu.VMEM(shape, F32) for name, shape in full.items()}
+    scratch |= dict(
+        edges=pltpu.VMEM((2, 16, 128), jnp.int32), load_sem=dma((len(given),)), side_sem=dma((6,)), send_sem=dma((6,)),
+        q_sem=dma((rounds,)), kv_sem=dma((n,)), att_sem=dma((1,)), grad_sem=dma((rounds,)), dkv_sem=dma((1,)),
+        dq_sem=dma((1,)), early_sem=dma((2, REDUCTION_SEMS)), late_sem=dma((2, REDUCTION_SEMS)),
+        early_free=signal((7,)), late_free=signal((7,)),
+    )
+    layout = (list(given), list(vectors) + ["bounds"], list(outs), list(scratch))
+    out3, grad3, early, late, small = pl.pallas_call(
+        functools.partial(layer_kernel, n, length, layout),
+        in_specs=[pl.BlockSpec(memory_space=pl.ANY)] * len(given)
+        + [vmem] * len(vectors)
+        + [pl.BlockSpec(memory_space=pltpu.SMEM)],
+        out_specs=[vmem] * len(outs),
+        out_shape=[jax.ShapeDtypeStruct(*out) for out in outs.values()],
+        scratch_shapes=list(scratch.values()) + reduction_scratch(EARLY_ROWS) + reduction_scratch(LATE_ROWS),
+        compiler_params=pltpu.CompilerParams(
+            collective_id=0, has_side_effects=True, vmem_limit_bytes=60 * 2**20
+        ),
+    )(*given.values(), *vectors.values(), doc_bounds)
+    sum_in, sum_out, sum_up, sum_mix, sum_pool, sum_q, sum_k, sum_v, sum_p = widened(early, late)
+    return (
+        out3.reshape(inputs.shape), grad3.reshape(inputs.shape), sum_pool, small[0], small[1], small[2],
+        sum_q, sum_k, sum_v, sum_mix, sum_p, small[3], small[4], small[5], small[6], sum_in,
+        small[7:11].reshape(-1), sum_out, small[11], sum_up, small[12:15].reshape(-1),
+    )
+
+
 def solution(mesh):
     split = P("dp", "seq", None)
+    fits = mesh.shape["seq"] == 16
     return jax.shard_map(
-        body,
+        fused_body if fits else body,
         mesh=mesh,
         in_specs=(split, P("dp", None)) + (P(),) * 19 + (split,),
         out_specs=(split, split) + (P(),) * 19,

time: 445 us -> 267 us (0.60)
  waiting for transfers between devices: 147 us -> 0 us
  Pallas kernels: 130 us -> 250 us
  blocking collectives: 49.8 us -> 0 us
  matrix products: 39.5 us -> 0 us
  other arithmetic: 21.9 us -> 0 us
  local copies, waits for them, and re-layouts: 35.1 us -> 16 us
  between operations: 14.8 us -> 0.67 us
  starting transfers between devices: 6.16 us -> 0 us
    psum x1 -> x0, waiting for transfers between devices: 147 us -> none  [body(): lax.psum(tuple((grad.astype(BF16) for grad in (grad_pool_weight, grad_que...]
    pallas_call x6 -> x2, Pallas kernels: 130 us -> 250 us  [the longest x1 232 us: fused_body(): pl.pallas_call(functools.partial(layer_kernel, n, length, layout), in_spe...]
    psum x1 -> x0, blocking collectives: 47.9 us -> none  [body(): small = lax.psum(jnp.concatenate(small_parts), ('dp', 'seq'))]
    dot_general x24 -> x0, matrix products: 39.5 us -> none  [dot(): lax.dot_general(left, right, (dims, ((), ())), preferred_element_type=F32)]
    convert_element_type x12 -> x0, other arithmetic: 18.5 us -> none  [the longest x4 8.33 us: body(): sum_in, sum_out, sum_up, sum_mix = (grad.astype(F32) for grad in early)]
    ppermute x2 -> x0, starting transfers between devices: 6.12 us -> none  [passed_along(): lax.ppermute(value, axis, [(source, source + steps) for source in range(f...]
    reshape x12 -> x5, local copies, waits for them, and re-layouts: 11.7 us -> 9.04 us  [the longest x1 2.11 us: fused_body(): out3.reshape(inputs.shape)]
  transfers between devices with their start and end apart: 3 -> 0, of which waited for: 1 -> 0; matrix products, arithmetic and copies ran while one was open for 5% -> 0% of each run, Pallas kernels for 0% -> 0%
where the time goes in v2:
time: 267 us
  Pallas kernels  250 us (94%)
  local copies, waits for them, and re-layouts  16 us (6%)
    pallas_call x1, Pallas kernels, fused_body(): pl.pallas_call(functools.partial(layer_kernel, n, length, layout), in_spe...  232 us
    pallas_call x1, Pallas kernels, widened(): pl.pallas_call(widen_kernel, grid=(first + LATE_ROWS // 512,), in_specs=[...  17.5 us

profile of v2, /device:TPU:0, one launch (start us, length us, event | category | flops | bytes accessed | tf_op | source)
XLA Modules:
  0.0 266.7 jit_solution(3948677925947990722)
XLA Ops:
  0.7 1.3 broadcast_in_dim.39.refs_21_
  2.0 2.1 reshape.60.refs_0_
  4.1 2.1 reshape.61.refs_5_
  6.2 232.4 %shard_map.400 = (bf16[192,1536]{1,0:T(8,128)(2,1)}, bf16[192,1536]{1,0:T(8,128)(2,1)}, bf16[6144,512]{1,0:T(8,128)(2,1)}, bf16[3584,512]{1,0:T(8,128)(2,1)}, f32[16,512]{1,0:T(8,128)}) custom-call(bf16[192,1536]{1,0:T(8,128)(2,1)} %reshape.60.refs_0_, bf16[1536,512]{1,0:T(8,128)(2,1)} %refs_1_.1, bf16[512,512]{1,0:T(8,128)(2,1)} %refs_2_.1, ...), custom_call_target="tpu_custom_call" | custom-call | tf_op jit(solution)/shard_map/pallas_call | solution.py:1360
  238.6 2.1 reshape.62
  240.7 0.8 slice_bitcast_fusion
  241.5 0.6 copy.46
  242.1 0.7 slice.39
  242.8 1.6 fusion
  244.4 0.6 reshape.65
  245.0 2.1 reshape.63
  247.1 0.0 copy-start
  247.1 2.0 copy-done
  249.2 17.5 %shard_map.401 = (f32[512,2048]{1,0:T(8,128)}, f32[2048,512]{1,0:T(8,128)}, f32[512,1536]{1,0:T(8,128)}, f32[512,512]{1,0:T(8,128)}, f32[1536,512]{1,0:T(8,128)}...) custom-call(bf16[6144,512]{1,0:T(8,128)(2,1)} %get-tuple-element.37.early_ref, ...), custom_call_target="tpu_custom_call" | custom-call | tf_op jit(solution)/shard_map/pallas_call | solution.py:1292
Async XLA Ops:
  247.1 2.0 copy-start

commit v3 on v2

--- a/solution.py
+++ b/solution.py
@@ -597,47 +597,34 @@
 
 
 EARLY_ROWS, LATE_ROWS = 6144, 3584
+EARLY_CHUNKS = ((0, 2048), (2048, 2048), (4096, 2048))
+LATE_CHUNKS = ((0, 1536), (1536, 1536), (3072, 512))
 SMALL_ROWS = 16
-FAR_SHARE = {EARLY_ROWS: 768, LATE_ROWS: 512}
 OVER_ROWS = ((0,), (0,))
 OVER_COLUMNS = ((1,), (1,))
 
 
 class Reduction:
-    def __init__(self, buffer, bufs, sems, free, small=None):
-        self.buffer, self.sems, self.free = buffer, sems, free
-        (self.from_core, self.near_one, self.near_two, self.near_z, self.far_z, self.far_one, self.far_two) = bufs
-        self.small = small
-        rows = buffer.shape[0]
-        self.half = rows // 2
-        self.far_size = FAR_SHARE[rows]
-        self.near_size = self.half - self.far_size
+    def __init__(self, buffer, start, rows, bufs, sems, free, small=None):
+        self.buffer, self.sems, self.free, self.small = buffer, sems, free, small
+        self.from_core, self.from_one, self.from_two, self.from_z = bufs
         core, chip = lax.axis_index("dp"), lax.axis_index("seq")
-        self.core, self.chip = core, chip
+        self.core, self.chip, self.size = core, chip, rows // 2
         self.z = chip // 4
         bit_x, bit_y = chip % 2, (chip // 2) % 2
         first_x = core == 0
         self.peer_x, self.peer_y = chip + 1 - 2 * bit_x, chip + 2 - 4 * bit_y
-        self.bit_one = jnp.where(first_x, bit_x, bit_y)
-        self.bit_two = jnp.where(first_x, bit_y, bit_x)
-        step_one = jnp.where(first_x, 1, 2)
-        step_two = 3 - step_one
-        self.peer_one = chip + jnp.where(self.bit_one == 0, step_one, -step_one)
-        self.peer_two = chip + jnp.where(self.bit_two == 0, step_two, -step_two)
-        base = core * self.half
-        near, far = self.near_size, self.far_size
-        self.near_at = base
-        self.near_one_at = base + self.bit_one * (near // 2)
-        self.near_one_out = base + (1 - self.bit_one) * (near // 2)
-        self.near_two_at = self.near_one_at + self.bit_two * (near // 4)
-        self.near_two_out = self.near_one_at + (1 - self.bit_two) * (near // 4)
-        self.near_z_at = self.near_two_at + self.z * (near // 16)
-        self.far_at = base + near
-        self.far_z_at = self.far_at + self.z * (far // 4)
-        self.far_one_at = self.far_z_at + self.bit_one * (far // 8)
-        self.far_one_out = self.far_z_at + (1 - self.bit_one) * (far // 8)
-        self.far_two_at = self.far_one_at + self.bit_two * (far // 16)
-        self.far_two_out = self.far_one_at + (1 - self.bit_two) * (far // 16)
+        bit_one, bit_two = jnp.where(first_x, bit_x, bit_y), jnp.where(first_x, bit_y, bit_x)
+        self.peer_one = jnp.where(first_x, self.peer_x, self.peer_y)
+        self.peer_two = jnp.where(first_x, self.peer_y, self.peer_x)
+        size = self.size
+        self.at = start + core * size
+        self.out = start + (1 - core) * size
+        self.one_at = self.at + bit_one * (size // 2)
+        self.one_out = self.at + (1 - bit_one) * (size // 2)
+        self.two_at = self.one_at + bit_two * (size // 4)
+        self.two_out = self.one_at + (1 - bit_two) * (size // 4)
+        self.z_at = self.two_at + self.z * (size // 16)
 
     def rows(self, start, size):
         return self.buffer.at[pl.ds(pl.multiple_of(start, 16), size)]
@@ -656,19 +643,22 @@
         copy.wait_send()
         copy.wait_recv()
 
-
     def freed(self, index, *devices):
         for core, chip in devices:
             pl.semaphore_signal(self.free.at[index], inc=1, device_id=(core, chip), device_id_type=MESH)
 
+    def is_free(self, index, count=1):
+        pl.semaphore_wait(self.free.at[index], count)
+
+    def z_chip(self, away):
+        there = (self.z + 1 + away) % 4
+        return there, self.chip + (there - self.z) * 4
+
     def z_peers(self):
         return [(self.core, self.z_chip(away)[1]) for away in range(3)]
 
-    def is_free(self, index, count=1):
-        pl.semaphore_wait(self.free.at[index], count)
-
     def add(self, start, size, parts):
-        chunk = min(size, 256)
+        chunk = min(size, 128)
         while size % chunk:
             chunk -= 16
 
@@ -683,19 +673,15 @@
 
         lax.fori_loop(0, size // chunk, one, 0)
 
-    def z_chip(self, away):
-        there = (self.z + 1 + away) % 4
-        return there, self.chip + (there - self.z) * 4
-
     def small_go(self, stage, core, chip):
         if self.small is not None:
             own, taken = self.small
-            self.go(18 + stage, own, taken.at[stage], core, chip)
+            self.go(12 + stage, own, taken.at[stage], core, chip)
 
     def small_done(self, stage):
         if self.small is not None:
             own, taken = self.small
-            self.done(18 + stage, own)
+            self.done(12 + stage, own)
             own[...] = own[...] + taken[stage]
 
     def small_z_go(self):
@@ -703,121 +689,84 @@
             own, taken = self.small
             taken[3 + self.z] = own[...]
             for away in range(3):
-                peer = self.z_chip(away)[1]
-                self.go(21 + away, own, taken.at[3 + self.z], self.core, peer)
+                self.go(15 + away, own, taken.at[3 + self.z], self.core, self.z_chip(away)[1])
 
     def small_z_done(self):
         if self.small is not None:
             own, taken = self.small
             for away in range(3):
-                self.done(21 + away, own)
+                self.done(15 + away, own)
             own[...] = (taken[3] + taken[4]) + (taken[5] + taken[6])
 
     def step(self, number):
-        near, far = self.near_size, self.far_size
-        core, chip = self.core, self.chip
+        size, core, chip = self.size, self.core, self.chip
         if number == 0:
-            self.go(0, self.rows((1 - core) * self.half, self.half), self.from_core, 1 - core, chip)
+            self.go(0, self.rows(self.out, size), self.from_core, 1 - core, chip)
             self.small_go(0, 1 - core, chip)
         if number == 1:
             self.done(0, self.from_core)
             self.freed(0, (1 - core, chip))
-            self.add(core * self.half, self.half, (self.from_core,))
-            self.go(1, self.rows(self.near_one_out, near // 2), self.near_one, core, self.peer_one)
-            for away in range(3):
-                there, peer = self.z_chip(away)
-                self.go(3 + away, self.rows(self.far_at + there * (far // 4), far // 4), self.far_z.at[away], core, peer)
+            self.add(self.one_out, size // 2, (self.part(self.from_core, self.one_out - self.at, size // 2),))
+            self.go(1, self.rows(self.one_out, size // 2), self.from_one, core, self.peer_one)
+            self.add(self.one_at, size // 2, (self.part(self.from_core, self.one_at - self.at, size // 2),))
             self.small_done(0)
             self.small_go(1, core, self.peer_x)
         if number == 2:
-            self.done(1, self.near_one)
+            self.done(1, self.from_one)
             self.freed(1, (core, self.peer_one))
-            self.add(self.near_one_at, near // 2, (self.near_one,))
-            self.go(2, self.rows(self.near_two_out, near // 4), self.near_two, core, self.peer_two)
-            for away in range(3):
-                self.done(3 + away, self.far_z.at[away])
-            self.freed(4, *self.z_peers())
-            self.add(self.far_z_at, far // 4, tuple(self.far_z.at[away] for away in range(3)))
-            self.go(6, self.rows(self.far_one_out, far // 8), self.far_one, core, self.peer_one)
+            self.add(self.two_out, size // 4, (self.part(self.from_one, self.two_out - self.one_at, size // 4),))
+            self.go(2, self.rows(self.two_out, size // 4), self.from_two, core, self.peer_two)
+            self.add(self.two_at, size // 4, (self.part(self.from_one, self.two_at - self.one_at, size // 4),))
             self.small_done(1)
             self.small_go(2, core, self.peer_y)
         if number == 3:
-            self.done(2, self.near_two)
+            self.done(2, self.from_two)
             self.freed(2, (core, self.peer_two))
-            self.add(self.near_two_at, near // 4, (self.near_two,))
+            self.add(self.two_at, size // 4, (self.from_two,))
             for away in range(3):
                 there, peer = self.z_chip(away)
-                self.go(
-                    7 + away, self.rows(self.near_two_at + there * (near // 16), near // 16),
-                    self.near_z.at[away], core, peer,
-                )
-            self.done(6, self.far_one)
-            self.freed(5, (core, self.peer_one))
-            self.add(self.far_one_at, far // 8, (self.far_one,))
-            self.go(10, self.rows(self.far_two_out, far // 16), self.far_two, core, self.peer_two)
+                self.go(3 + away, self.rows(self.two_at + there * (size // 16), size // 16), self.from_z.at[away], core, peer)
             self.small_done(2)
             self.small_z_go()
         if number == 4:
             for away in range(3):
-                self.done(7 + away, self.near_z.at[away])
+                self.done(3 + away, self.from_z.at[away])
             self.freed(3, *self.z_peers())
-            self.add(self.near_z_at, near // 16, tuple(self.near_z.at[away] for away in range(3)))
-            own = self.rows(self.near_z_at, near // 16)
+            self.add(self.z_at, size // 16, tuple(self.from_z.at[away] for away in range(3)))
+            own = self.rows(self.z_at, size // 16)
             self.is_free(3, 3)
             for away in range(3):
-                self.go(11 + away, own, own, core, self.z_chip(away)[1])
-            self.done(10, self.far_two)
-            self.freed(6, (core, self.peer_two))
-            self.add(self.far_two_at, far // 16, (self.far_two,))
-            own = self.rows(self.far_two_at, far // 16)
-            self.is_free(6)
-            self.go(14, own, own, core, self.peer_two)
+                self.go(6 + away, own, own, core, self.z_chip(away)[1])
             self.small_z_done()
         if number == 5:
             for away in range(3):
-                self.done(11 + away, self.rows(self.near_z_at, near // 16))
-            own = self.rows(self.near_two_at, near // 4)
+                self.done(6 + away, self.rows(self.z_at, size // 16))
+            own = self.rows(self.two_at, size // 4)
             self.is_free(2)
-            self.go(15, own, own, core, self.peer_two)
-            self.done(14, self.rows(self.far_two_at, far // 16))
-            own = self.rows(self.far_one_at, far // 8)
-            self.is_free(5)
-            self.go(16, own, own, core, self.peer_one)
+            self.go(9, own, own, core, self.peer_two)
         if number == 6:
-            self.done(15, self.rows(self.near_two_at, near // 4))
-            own = self.rows(self.near_one_at, near // 2)
+            self.done(9, self.rows(self.two_at, size // 4))
+            own = self.rows(self.one_at, size // 2)
             self.is_free(1)
-            self.go(17, own, own, core, self.peer_one)
-            self.done(16, self.rows(self.far_one_at, far // 8))
-            own = self.rows(self.far_z_at, far // 4)
-            self.is_free(4, 3)
-            for away in range(3):
-                self.go(24 + away, own, own, core, self.z_chip(away)[1])
+            self.go(10, own, own, core, self.peer_one)
         if number == 7:
-            self.done(17, self.rows(self.near_one_at, near // 2))
-            own = self.rows(self.near_at, near)
+            self.done(10, self.rows(self.one_at, size // 2))
+            own = self.rows(self.at, size)
             self.is_free(0)
-            self.go(27, own, own, 1 - core, chip)
-            for away in range(3):
-                self.done(24 + away, self.rows(self.far_z_at, far // 4))
-            own = self.rows(self.far_at, far)
-            self.go(28, own, own, 1 - core, chip)
+            self.go(11, own, own, 1 - core, chip)
         if number == 8:
-            self.done(27, self.rows(self.near_at, near))
-            self.done(28, self.rows(self.far_at, far))
-
-
-REDUCTION_SEMS = 29
+            self.done(11, self.rows(self.at, size))
+
+    def part(self, ref, start, size):
+        return ref.at[pl.ds(pl.multiple_of(start, 16), size)]
+
+
+REDUCTION_SEMS = 18
 
 
 def reduction_scratch(rows):
-    far = FAR_SHARE[rows]
-    near = rows // 2 - far
     return [
-        pltpu.VMEM(shape + (512,), BF16)
-        for shape in (
-            (rows // 2,), (near // 2,), (near // 4,), (3, near // 16), (3, far // 4), (far // 8,), (far // 16,),
-        )
+        pltpu.VMEM(shape + (512,), BF16) for shape in ((rows // 2,), (rows // 4,), (rows // 8,), (3, rows // 32))
     ]
 
 
@@ -868,7 +817,13 @@
     me = core * n + chip
 
     loads = {}
-    r.early_parts, r.late_parts = refs[-14:-7], refs[-7:]
+    count_early, count_late = len(EARLY_CHUNKS), len(LATE_CHUNKS)
+    chunk_refs = refs[-4 * (count_early + count_late) :]
+
+    def reduction(buffer, index, cut, small=None):
+        bufs = chunk_refs[4 * index : 4 * index + 4]
+        return Reduction(buffer, *cut, bufs, r.sum_sem.at[index], r.sum_free.at[index], small)
+
     for index, (name, source) in enumerate(given.items()):
         loads[name] = pltpu.make_async_copy(source, scratch[name], r.load_sem.at[index])
         loads[name].start()
@@ -889,7 +844,17 @@
     low_bound, high_bound = r.bounds[0, 0], r.bounds[0, 1]
     r.edges[core, :8] = jnp.full((8, 128), low_bound, jnp.int32)
     r.edges[core, 8:] = jnp.full((8, 128), high_bound, jnp.int32)
-    ready(r.x3, r.pool_w)
+
+    def tokens_of(source, target):
+        for block in range(width // 128):
+            r.mixing[block] = source[:, block * 128 : (block + 1) * 128].astype(F32)
+            for part in range(3):
+                every = r.mixing[block, pl.ds(part, length, stride=3), :]
+                start = part * width + block * 128
+                target[:, start : start + 128] = every.astype(BF16)
+
+    ready(r.x_bytes, r.pool_w)
+    tokens_of(r.x_bytes, r.x3)
     own = dot(r.x3[:, :width], r.pool_w[2 * width :])
     before = dot(r.x3[:, width:], r.pool_w[: 2 * width])
     pl.semaphore_wait(barrier, count - 1)
@@ -947,16 +912,15 @@
 
     kv_jobs = []
     for h in range(HEADS):
-        for g in range(group):
-            to_chip, to_core = chip_of(core, h, g, group)
-            kv_jobs.append(
-                (r.kv_out.at[h], r.kv.at[chip], (r.send_sem.at[1], r.kv_sem.at[chip]), jnp.int32(to_core), to_chip)
-            )
-    first_jobs = q_jobs(r.q_out, r.q, r.send_sem.at[0], r.q_sem) + kv_jobs
+        to_chip, _ = chip_of(core, h, 0, group)
+        sems = (r.send_sem.at[1], r.kv_sem.at[chip])
+        kv_jobs.append((r.kv_out.at[h], r.kv.at[chip], sems, chip % 2, to_chip))
+    first_jobs = kv_jobs + q_jobs(r.q_out, r.q, r.send_sem.at[0], r.q_sem)
     for job in first_jobs:
         send(*job)
 
-    ready(r.ct3, r.up_w, r.ffn_out)
+    ready(r.ct_bytes, r.up_w, r.ffn_out)
+    tokens_of(r.ct_bytes, r.ct3)
     grad_final = dot(r.ct3[...], r.up_w[...], OVER_COLUMNS)
     r.grad_final[...] = grad_final
     grad_branch = grad_final.astype(BF16)
@@ -991,11 +955,29 @@
     def rows_of(array):
         return pl.ds(pl.multiple_of(array, length), tile)
 
+    def forward(turn):
+        at = turn * group + core
+        return pltpu.make_async_remote_copy(
+            r.kv.at[at], r.kv.at[at], r.send_sem.at[6], r.kv_sem.at[at], device_id=(1 - core, chip), device_id_type=MESH
+        )
+
+    def pass_on(turn):
+        at = turn * group + core
+        arrived(r.kv.at[at], r.kv_sem.at[at])
+        forward(turn).start()
+
+    pass_on(0)
+
     def attend(turn, carry):
         block = block_of(turn, member, group)
+
+        @pl.when(turn < rounds - 1)
+        def _():
+            pass_on(turn + 1)
+
         arrived(r.q.at[turn], r.q_sem.at[turn])
-        for other in range(group):
-            arrived(r.kv.at[turn * group + other], r.kv_sem.at[turn * group + other])
+        other = turn * group + 1 - core
+        arrived(r.kv.at[other], r.kv_sem.at[other])
         query_u, _, turned = query_parts(
             r.q[turn], content_bias, pos_bias, r.head_w[...], r.sines[...], r.cosines[...]
         )
@@ -1045,6 +1027,8 @@
     lax.fori_loop(0, rounds, attend, 0)
     for source, _, sems, to_core, to_chip in first_jobs:
         sent(source, sems[0], to_core, to_chip)
+    for turn in range(rounds):
+        forward(turn).wait_send()
 
     def joined(get):
         parts = [get(h) for h in range(HEADS)]
@@ -1084,27 +1068,56 @@
         send(*job)
 
     early, late = r.early, r.late
+    sums = [reduction(early, index, cut) for index, cut in enumerate(EARLY_CHUNKS)]
+    for index, cut in enumerate(LATE_CHUNKS):
+        small_pair = (small, r.small_in) if index == 0 else None
+        sums.append(reduction(late, count_early + index, cut, small_pair))
+
+    def steps_at(moment):
+        for index, number in SCHEDULE.get(moment, ()):
+            sums[index].step(number)
+
     for part in range(4):
         at = slice(part * width, (part + 1) * width)
         early[at] = dot(r.ffn_input[...], r.grad_pre[:, at], OVER_ROWS).astype(BF16)
+    sums[0].step(0)
+    for part in range(4):
+        at = slice(part * width, (part + 1) * width)
         early[2048 + part * width : 2048 + (part + 1) * width] = dot(
             r.act_low[:, at], r.grad_branch[...], OVER_ROWS
         ).astype(BF16)
+    sums[1].step(0)
+    steps_at(-3)
     early[5632:] = dot(r.att_low[...], grad_mixed_low, OVER_ROWS).astype(BF16)
     final_low = (r.mixed[...] + dot(r.act_low[...], r.ffn_out[...]) + r.ffn_out_b[...]).astype(BF16)
     for part in range(3):
         at = slice(part * width, (part + 1) * width)
         early[4096 + part * width : 4096 + (part + 1) * width] = dot(final_low, r.ct3[:, at], OVER_ROWS).astype(BF16)
-    first_sum = Reduction(early, r.early_parts, r.early_sem, r.early_free)
-    first_sum.step(0)
+    sums[2].step(0)
+    steps_at(-2)
     for part in range(3):
         at = slice(part * width, (part + 1) * width)
         lifted = dot(final_low, r.up_w[:, at]) + r.up_b[:, at]
         r.out3[:, at] = (r.x3[:, at].astype(F32) + lifted).astype(BF16)
 
+    steps_at(-1)
+
     r.dkv[...] = jnp.zeros_like(r.dkv)
     r.dhead[...] = jnp.zeros_like(r.dhead)
     r.dbias[...] = jnp.zeros_like(r.dbias)
+
+    def give_over(turn):
+        return pltpu.make_async_remote_copy(
+            r.dkv_out.at[turn * group + 1 - core], r.dkv_other.at[turn], r.send_sem.at[7], r.other_sem.at[turn],
+            device_id=(1 - core, chip), device_id_type=MESH,
+        )
+
+    def hand_in(turn):
+        at = turn * group + core
+        give_over(turn).wait_recv()
+        total = r.dkv[pl.ds(pl.multiple_of(at * length, length), length)] + r.dkv_other[turn].astype(F32)
+        r.dkv_out[at] = total.astype(BF16)
+        send(r.dkv_out.at[at], r.dkv_in.at[head], (r.send_sem.at[4], r.dkv_sem.at[0]), row, at)
 
     def back(index, carry):
         turn = rounds - 1 - index
@@ -1138,14 +1151,14 @@
             return inner
 
         lax.fori_loop(0, turn + 1, step_over, 0)
-        at = pl.ds(pl.multiple_of(turn * tile, tile), tile)
-        r.dkv_out[pl.ds(turn * group, group)] = r.dkv[at].astype(BF16).reshape(group, length, PAIR)
-        for other in range(group):
-            key_block = turn * group + other
-            send(
-                r.dkv_out.at[key_block], r.dkv_in.at[member, head],
-                (r.send_sem.at[4], r.dkv_sem.at[0]), row, key_block,
-            )
+        give = turn * group + 1 - core
+        r.dkv_out[give] = r.dkv[pl.ds(pl.multiple_of(give * length, length), length)].astype(BF16)
+        give_over(turn).start()
+
+        @pl.when(index > 0)
+        def _():
+            hand_in(turn + 1)
+
         grad_u = r.near[:, :HEAD] * scale
         turn_sin, turn_cos = r.sines[...], r.cosines[...]
         on_sin, on_cos = r.far[:, :half] * scale, r.far[:, half:] * scale
@@ -1158,16 +1171,17 @@
         r.dbias[1:2] += column_sum(grad_v)
         r.dq_out[turn] = packed(grad_u + grad_v).astype(BF16)
         send(r.dq_out.at[turn], r.dq_in.at[head], (r.send_sem.at[5], r.dq_sem.at[0]), row, block)
-        for when, number in EARLY_STEPS:
-
-            @pl.when(index == when)
-            def _(number=number):
-                first_sum.step(number)
+        for when in range(rounds):
+            if when in SCHEDULE:
+
+                @pl.when(index == when)
+                def _(when=when):
+                    steps_at(when)
 
         return carry
 
     lax.fori_loop(0, rounds, back, 0)
-    first_left = [number for number in range(1, 9) if number not in [number for _, number in EARLY_STEPS]]
+    hand_in(0)
 
     late[2048 + 1024 :] = jnp.zeros((512, 512), BF16)
     dhead = r.dhead[...]
@@ -1180,24 +1194,30 @@
     small[3:5, pair_at] = jnp.where(
         odd, jnp.concatenate([nothing, dbias], 1), jnp.concatenate([dbias, nothing], 1)
     )
+    sums[5].step(0)
+    steps_at(8)
     for source, _, sems, to_core, to_chip in second_jobs:
         sent(source, sems[0], to_core, to_chip)
     for turn in range(rounds):
         block = block_of(jnp.int32(turn), member, group)
         sent(r.att_out.at[turn], r.send_sem.at[2], row, block)
         sent(r.dq_out.at[turn], r.send_sem.at[5], row, block)
-    for block in range(n):
-        sent(r.dkv_out.at[block], r.send_sem.at[4], row, jnp.int32(block))
+    for turn in range(rounds):
+        sent(r.dkv_out.at[turn * group + core], r.send_sem.at[4], row, turn * group + core)
+        give_over(turn).wait_send()
+    steps_at(9)
     arrived(r.dq_in, r.dq_sem.at[0])
     arrived(r.dkv_in, r.dkv_sem.at[0])
     grad_query = joined(lambda h: r.dq_in[h].astype(F32)).astype(BF16)
-    both = [r.dkv_in[0, h].astype(F32) + r.dkv_in[1, h].astype(F32) for h in range(HEADS)]
+    both = [r.dkv_in[h].astype(F32) for h in range(HEADS)]
     grad_keys = jnp.concatenate([part[:, :HEAD] for part in both], 1).astype(BF16)
     grad_values = jnp.concatenate([part[:, HEAD:] for part in both], 1).astype(BF16)
     attn_in = r.attn_in[...]
     late[1536:2048] = dot(attn_in, grad_query, OVER_ROWS).astype(BF16)
     late[2048:2560] = dot(attn_in, grad_keys, OVER_ROWS).astype(BF16)
     late[2560:3072] = dot(attn_in, grad_values, OVER_ROWS).astype(BF16)
+    sums[4].step(0)
+    steps_at(10)
     grad_normed = (
         dot(grad_query, r.q_w[...], OVER_COLUMNS)
         + dot(grad_keys, r.k_w[...], OVER_COLUMNS)
@@ -1229,10 +1249,8 @@
     late[:1024] = (
         dot(r.x3[:, width:], within, OVER_ROWS) + dot(r.rim[...], rim_row, OVER_ROWS)
     ).astype(BF16)
-    second_sum = Reduction(late, r.late_parts, r.late_sem, r.late_free, (small, r.small_in))
-    second_sum.step(0)
-    if first_left:
-        first_sum.step(first_left.pop(0))
+    sums[3].step(0)
+    steps_at(11)
 
     @pl.when(chip == n - 1)
     def _():
@@ -1257,52 +1275,91 @@
     def _():
         back_rim_copy().wait_send()
 
-    for number in range(1, 9):
-        second_sum.step(number)
-        if first_left:
-            first_sum.step(first_left.pop(0))
-
-
-EARLY_STEPS = ((0, 1), (3, 2), (5, 3), (7, 4))
-
-
-def widen_kernel(early_ref, late_ref, *outs):
-    at = pl.program_id(0)
-    wide = jnp.where(at < EARLY_ROWS // 512, early_ref[...].astype(F32), late_ref[...].astype(F32))
-    for out, (start, blocks) in zip(outs, WIDENED):
-
-        @pl.when(jnp.logical_and(at >= start, at < start + blocks))
-        def _(out=out):
-            out[...] = wide
-
-
-WIDENED = ((0, 4), (4, 4), (8, 3), (11, 1), (12, 3), (15, 1), (16, 1), (17, 1), (18, 1))
-ACROSS = (True, False, True, False, False, False, False, False, False)
-
-
-def widened(early, late):
-    def out_spec(start, blocks, across):
-        def place(at):
-            block = jnp.clip(at - start, 0, blocks - 1)
-            return (0, block) if across else (block, 0)
-
-        return pl.BlockSpec((512, 512), place)
-
-    first = EARLY_ROWS // 512
-    return pl.pallas_call(
-        widen_kernel,
-        grid=(first + LATE_ROWS // 512,),
-        in_specs=[
-            pl.BlockSpec((512, 512), lambda at: (jnp.minimum(at, first - 1), 0)),
-            pl.BlockSpec((512, 512), lambda at: (jnp.maximum(at - first, 0), 0)),
+    steps_at(12)
+
+
+SCHEDULE = {
+    -2: ((0, 1),),
+    -1: ((1, 1),),
+    0: ((0, 2), (2, 1)),
+    1: ((0, 3), (1, 2)),
+    2: ((1, 3), (2, 2)),
+    3: ((0, 4),),
+    4: ((2, 3), (1, 4)),
+    5: ((0, 5), (2, 4)),
+    7: ((1, 5), (0, 6)),
+    8: ((2, 5), (5, 1)),
+    9: ((1, 6),),
+    10: ((0, 7), (5, 2), (2, 6)),
+    11: ((4, 1), (1, 7), (5, 3)),
+    12: (
+        (3, 1), (4, 2), (2, 7), (5, 4), (3, 2), (4, 3), (5, 5), (3, 3), (4, 4), (5, 6), (3, 4), (4, 5), (5, 7),
+        (3, 5), (4, 6), (3, 6), (4, 7), (3, 7), (0, 8), (1, 8), (2, 8), (5, 8), (4, 8), (3, 8),
+    ),
+}
+
+
+WIDENED = (
+    (0, 4, True), (2048, 4, False), (4096, 3, True), (5632, 1, False),
+    (0, 3, False), (1536, 1, False), (2048, 1, False), (2560, 1, False), (3072, 1, False),
+)
+NARROW = ((0, 1), (1, 1), (2, 1), (3, 1), (4, 1), (5, 1), (6, 1), (7, 4), (11, 1), (12, 3))
+
+
+def last_kernel(*refs):
+    early, late, out3, grad3, small = refs[:5]
+    wide_outs, narrow_outs, byte_outs = refs[5:14], refs[14:24], refs[24:26]
+    staging, mixing, sems = refs[26:]
+    copies = []
+    for index, (out, (start, blocks, across)) in enumerate(zip(wide_outs, WIDENED)):
+        source = early if index < 4 else late
+        for block in range(blocks):
+            slot = len(copies)
+
+            def widen(step, carry, source=source, slot=slot, first=start + block * 512):
+                here = pl.ds(pl.multiple_of(step * 64, 64), 64)
+                staging[slot, here] = source[pl.ds(pl.multiple_of(first + step * 64, 64), 64)].astype(F32)
+                return carry
+
+            lax.fori_loop(0, 8, widen, 0)
+            at = slice(block * 512, (block + 1) * 512)
+            target = out.at[:, at] if across else out.at[at]
+            copy = pltpu.make_async_copy(staging.at[slot], target, sems.at[slot])
+            copy.start()
+            copies.append(copy)
+    for out, tokens in zip(byte_outs, (out3, grad3)):
+        length, width = out.shape[0] // 3, out.shape[1]
+        for block in range(width // 128):
+            for part in range(3):
+                start = part * width + block * 128
+                mixing[block, pl.ds(part, length, stride=3), :] = tokens[:, start : start + 128].astype(F32)
+            out[:, block * 128 : (block + 1) * 128] = mixing[block].astype(BF16)
+    for out, (start, blocks) in zip(narrow_outs, NARROW):
+        for block in range(blocks):
+            out[:, block * 512 : (block + 1) * 512] = small[start + block : start + block + 1]
+    for copy in copies:
+        copy.wait()
+
+
+def finished(early, late, out3, grad3, small):
+    length, width = out3.shape[0], out3.shape[1] // 3
+    vmem = pl.BlockSpec(memory_space=pltpu.VMEM)
+    shapes = [(512, 512 * blocks) if across else (512 * blocks, 512) for _, blocks, across in WIDENED]
+    narrow = [(1, 512 * blocks) for _, blocks in NARROW]
+    count = sum(blocks for _, blocks, _ in WIDENED)
+    outs = pl.pallas_call(
+        last_kernel,
+        in_specs=[vmem] * 5,
+        out_specs=[pl.BlockSpec(memory_space=pl.ANY)] * len(shapes) + [vmem] * (len(narrow) + 2),
+        out_shape=[jax.ShapeDtypeStruct(shape, F32) for shape in shapes + narrow]
+        + [jax.ShapeDtypeStruct((3 * length, width), BF16)] * 2,
+        scratch_shapes=[
+            pltpu.VMEM((count, 512, 512), F32), pltpu.VMEM((width // 128, 3 * length, 128), F32),
+            pltpu.SemaphoreType.DMA((count,)),
         ],
-        out_specs=[out_spec(*cut, across) for cut, across in zip(WIDENED, ACROSS)],
-        out_shape=[
-            jax.ShapeDtypeStruct((512, 512 * blocks) if across else (512 * blocks, 512), F32)
-            for (_, blocks), across in zip(WIDENED, ACROSS)
-        ],
-        compiler_params=pltpu.CompilerParams(vmem_limit_bytes=48 * 2**20),
-    )(early, late)
+        compiler_params=pltpu.CompilerParams(vmem_limit_bytes=56 * 2**20),
+    )(early, late, out3, grad3, small)
+    return outs[: len(shapes)], [out[0] for out in outs[len(shapes) : -2]], outs[-2:]
 
 
 def fused_body(
@@ -1317,8 +1374,8 @@
     rounds = n // 2
     table, sines, cosines = wave_tables(tokens, length, width)
     given = dict(
-        x3=inputs.reshape(length, 3 * width), pool_w=pool_weight, q_w=query_weight, k_w=key_weight, v_w=value_weight,
-        ct3=cotangent.reshape(length, 3 * width), up_w=up_weight, ffn_out=ffn_out, pos_w=pos_weight, table=table,
+        x_bytes=inputs[0], pool_w=pool_weight, q_w=query_weight, k_w=key_weight, v_w=value_weight,
+        ct_bytes=cotangent[0], up_w=up_weight, ffn_out=ffn_out, pos_w=pos_weight, table=table,
         out_w=out_weight, ffn_in=ffn_in,
     )
     vectors = dict(
@@ -1336,25 +1393,25 @@
     dma, signal = pltpu.SemaphoreType.DMA, pltpu.SemaphoreType.REGULAR
     scratch = {name: pltpu.VMEM(array.shape, array.dtype) for name, array in given.items()}
     low = dict(
-        rim=(16, 2 * width), back_rim=(16, width), attn_in=block, q_out=(HEADS,) + pair_half,
+        x3=(length, 3 * width), ct3=(length, 3 * width), rim=(16, 2 * width), back_rim=(16, width), attn_in=block, q_out=(HEADS,) + pair_half,
         kv_out=(HEADS, length, PAIR), q=(rounds,) + pair_half, kv=(n, length, PAIR), grad_branch=block,
         head_w=(width, HEAD), extra=(length, PAIR + width), keep=(rounds * (rounds + 1) // 2, length, 2 * length),
         att_out=(rounds,) + pair_half, att_in=(HEADS,) + pair_half, att_low=block, ffn_input=block, act_low=wide,
-        grad_pre=wide, grad=(rounds,) + pair_half, dkv_out=(n, length, PAIR), dkv_in=(2, HEADS, length, PAIR),
-        dq_out=(rounds,) + pair_half, dq_in=(HEADS,) + pair_half, grad_pooled=block,
+        grad_pre=wide, grad=(rounds,) + pair_half, dkv_out=(n, length, PAIR), dkv_in=(HEADS, length, PAIR),
+        dkv_other=(rounds, length, PAIR), dq_out=(rounds,) + pair_half, dq_in=(HEADS,) + pair_half, grad_pooled=block,
     )
     full = dict(
-        pooled=block, grad_final=block, grad_act=wide, score=(rounds, length, 2 * length), att=(rounds, length, PAIR),
+        mixing=(width // 128, 3 * length, 128), pooled=block, grad_final=block, grad_act=wide, score=(rounds, length, 2 * length), att=(rounds, length, PAIR),
         mixed=block, dkv=(tokens, PAIR), dhead=(width, HEAD), dbias=(8, HEAD), near=(length, PAIR), far=block,
         small_in=(7, SMALL_ROWS, 512),
     )
     scratch |= {name: pltpu.VMEM(shape, BF16) for name, shape in low.items()}
     scratch |= {name: pltpu.VMEM(shape, F32) for name, shape in full.items()}
     scratch |= dict(
-        edges=pltpu.VMEM((2, 16, 128), jnp.int32), load_sem=dma((len(given),)), side_sem=dma((6,)), send_sem=dma((6,)),
+        edges=pltpu.VMEM((2, 16, 128), jnp.int32), load_sem=dma((len(given),)), side_sem=dma((6,)), send_sem=dma((8,)), other_sem=dma((rounds,)),
+
         q_sem=dma((rounds,)), kv_sem=dma((n,)), att_sem=dma((1,)), grad_sem=dma((rounds,)), dkv_sem=dma((1,)),
-        dq_sem=dma((1,)), early_sem=dma((2, REDUCTION_SEMS)), late_sem=dma((2, REDUCTION_SEMS)),
-        early_free=signal((7,)), late_free=signal((7,)),
+        dq_sem=dma((1,)), sum_sem=dma((6, 2, REDUCTION_SEMS)), sum_free=signal((6, 4)),
     )
     layout = (list(given), list(vectors) + ["bounds"], list(outs), list(scratch))
     out3, grad3, early, late, small = pl.pallas_call(
@@ -1364,16 +1421,18 @@
         + [pl.BlockSpec(memory_space=pltpu.SMEM)],
         out_specs=[vmem] * len(outs),
         out_shape=[jax.ShapeDtypeStruct(*out) for out in outs.values()],
-        scratch_shapes=list(scratch.values()) + reduction_scratch(EARLY_ROWS) + reduction_scratch(LATE_ROWS),
+        scratch_shapes=list(scratch.values())
+        + sum((reduction_scratch(rows) for _, rows in EARLY_CHUNKS + LATE_CHUNKS), []),
         compiler_params=pltpu.CompilerParams(
             collective_id=0, has_side_effects=True, vmem_limit_bytes=60 * 2**20
         ),
     )(*given.values(), *vectors.values(), doc_bounds)
-    sum_in, sum_out, sum_up, sum_mix, sum_pool, sum_q, sum_k, sum_v, sum_p = widened(early, late)
+    wide, narrow, both = finished(early, late, out3, grad3, small)
+    sum_in, sum_out, sum_up, sum_mix, sum_pool, sum_q, sum_k, sum_v, sum_p = wide
+    pool_b, ln1_g, ln1_b, content, pos, ln2_g, ln2_b, in_b, out_b, up_b = narrow
     return (
-        out3.reshape(inputs.shape), grad3.reshape(inputs.shape), sum_pool, small[0], small[1], small[2],
-        sum_q, sum_k, sum_v, sum_mix, sum_p, small[3], small[4], small[5], small[6], sum_in,
-        small[7:11].reshape(-1), sum_out, small[11], sum_up, small[12:15].reshape(-1),
+        both[0][None], both[1][None], sum_pool, pool_b, ln1_g, ln1_b, sum_q, sum_k, sum_v, sum_mix, sum_p,
+        content, pos, ln2_g, ln2_b, sum_in, in_b, sum_out, out_b, sum_up, up_b,
     )
 
 

time: 267 us -> 218 us (0.82)
  Pallas kernels: 250 us -> 214 us
  local copies, waits for them, and re-layouts: 16 us -> 1.3 us
    pallas_call x1, Pallas kernels: 232 us -> 202 us  [fused_body(): pl.pallas_call(functools.partial(layer_kernel, n, length, layout), in_spe...]
    reshape x5 -> x0, local copies, waits for them, and re-layouts: 9.04 us -> none  [the longest x1 2.11 us: fused_body(): out3.reshape(inputs.shape)]
    pallas_call x1, Pallas kernels: 17.5 us -> 12.2 us  [finished(): pl.pallas_call(last_kernel, in_specs=[vmem] * 5, out_specs=[pl.BlockSpec(...]
    unnamed x4 -> x0, local copies, waits for them, and re-layouts: 3.4 us -> none
where the time goes in v3:
time: 218 us; the launch traced here: 217 us
  Pallas kernels  214 us (98%)
    pallas_call x1, Pallas kernels, fused_body(): pl.pallas_call(functools.partial(layer_kernel, n, length, layout), in_spe...  202 us
    pallas_call x1, Pallas kernels, finished(): pl.pallas_call(last_kernel, in_specs=[vmem] * 5, out_specs=[pl.BlockSpec(...  12.2 us

profile of v3, /device:TPU:0, one launch (start us, length us, event | category | flops | bytes accessed | tf_op | source)
XLA Modules:
  0.0 217.1 jit_solution(12235631658103288772)
XLA Ops:
  0.7 1.3 broadcast_in_dim.45.refs_21_
  2.0 201.6 %shard_map.400 = (bf16[192,1536]{1,0:T(8,128)(2,1)}, bf16[192,1536]{1,0:T(8,128)(2,1)}, bf16[6144,512]{1,0:T(8,128)(2,1)}, bf16[3584,512]{1,0:T(8,128)(2,1)}, f32[16,512]{1,0:T(8,128)}) custom-call(bf16[576,512]{1,0:T(8,128)(2,1)} %bitcast.22, bf16[1536,512]{1,0:T(8,128)(2,1)} %refs_1_.1, bf16[512,512]{1,0:T(8,128)(2,1)} %refs_2_.1, ...), custom_call_target="tpu_custom_call" | custom-call | tf_op jit(solution)/shard_map/pallas_call | solution.py:1417
  203.6 12.2 %shard_map.401 = (f32[512,2048]{1,0:T(8,128)}, f32[2048,512]{1,0:T(8,128)}, f32[512,1536]{1,0:T(8,128)}, f32[512,512]{1,0:T(8,128)}, f32[1536,512]{1,0:T(8,128)}...) custom-call(bf16[6144,512]{1,0:T(8,128)(2,1)} %get-tuple-element.47., ...), custom_call_target="tpu_custom_call" | custom-call | tf_op jit(solution)/shard_map/pallas_call | solution.py:1350
  215.8 1.3 reduce

commit v4 on v3

--- a/solution.py
+++ b/solution.py
@@ -597,34 +597,43 @@
 
 
 EARLY_ROWS, LATE_ROWS = 6144, 3584
-EARLY_CHUNKS = ((0, 2048), (2048, 2048), (4096, 2048))
-LATE_CHUNKS = ((0, 1536), (1536, 1536), (3072, 512))
+EARLY_CHUNKS = ((0, 2048, False), (2048, 2048, True), (4096, 2048, False))
+LATE_CHUNKS = ((3072, 512, False), (1536, 1536, False), (0, 1024, True), (1024, 512, False))
 SMALL_ROWS = 16
 OVER_ROWS = ((0,), (0,))
 OVER_COLUMNS = ((1,), (1,))
 
 
 class Reduction:
-    def __init__(self, buffer, start, rows, bufs, sems, free, small=None):
+    def __init__(self, buffer, start, rows, by_z, bufs, sems, free, small=None):
         self.buffer, self.sems, self.free, self.small = buffer, sems, free, small
-        self.from_core, self.from_one, self.from_two, self.from_z = bufs
         core, chip = lax.axis_index("dp"), lax.axis_index("seq")
-        self.core, self.chip, self.size = core, chip, rows // 2
-        self.z = chip // 4
-        bit_x, bit_y = chip % 2, (chip // 2) % 2
+        self.core, self.chip = core, chip
+        x, y, z = chip % 2, (chip // 2) % 2, chip // 4
         first_x = core == 0
-        self.peer_x, self.peer_y = chip + 1 - 2 * bit_x, chip + 2 - 4 * bit_y
-        bit_one, bit_two = jnp.where(first_x, bit_x, bit_y), jnp.where(first_x, bit_y, bit_x)
-        self.peer_one = jnp.where(first_x, self.peer_x, self.peer_y)
-        self.peer_two = jnp.where(first_x, self.peer_y, self.peer_x)
-        size = self.size
-        self.at = start + core * size
-        self.out = start + (1 - core) * size
-        self.one_at = self.at + bit_one * (size // 2)
-        self.one_out = self.at + (1 - bit_one) * (size // 2)
-        self.two_at = self.one_at + bit_two * (size // 4)
-        self.two_out = self.one_at + (1 - bit_two) * (size // 4)
-        self.z_at = self.two_at + self.z * (size // 16)
+        self.peer_x, self.peer_y = (core, chip + 1 - 2 * x), (core, chip + 2 - 4 * y)
+        self.z_peers = [(core, chip + ((z + away) % 4 - z) * 4) for away in (1, 2, 3)]
+        self.z = z
+
+        def pair(bit, peer_core, peer_chip):
+            return (bit, [(1 - bit, peer_core, peer_chip)])
+
+        one = pair(jnp.where(first_x, x, y), core, jnp.where(first_x, self.peer_x[1], self.peer_y[1]))
+        two = pair(jnp.where(first_x, y, x), core, jnp.where(first_x, self.peer_y[1], self.peer_x[1]))
+        stages = [pair(core, 1 - core, chip)]
+        if by_z:
+            low, high = z % 2, z // 2
+            stages += [pair(low, core, chip + 4 - 8 * low), one, two, pair(high, core, chip + 8 - 16 * high)]
+        else:
+            stages += [one, two, (z, [((z + away) % 4, core, self.z_peers[away - 1][1]) for away in (1, 2, 3)])]
+        self.stages = []
+        at, size, first = start, rows, 0
+        for buf, (own, others) in zip(bufs, stages):
+            ways = len(others) + 1
+            self.stages.append((at, size, size // ways, own, others, buf, first))
+            at, size, first = at + own * (size // ways), size // ways, first + len(others)
+        self.back = first
+        self.last = 2 * len(stages)
 
     def rows(self, start, size):
         return self.buffer.at[pl.ds(pl.multiple_of(start, 16), size)]
@@ -635,139 +644,95 @@
             device_id=(core, chip), device_id_type=MESH,
         )
 
-    def go(self, index, source, target, core, chip):
-        self.copy(index, source, target, core, chip).start()
-
     def done(self, index, source):
-        copy = self.copy(index, source, source, self.core, self.peer_one)
+        copy = self.copy(index, source, source, 1 - self.core, self.chip)
         copy.wait_send()
         copy.wait_recv()
 
-    def freed(self, index, *devices):
-        for core, chip in devices:
-            pl.semaphore_signal(self.free.at[index], inc=1, device_id=(core, chip), device_id_type=MESH)
-
-    def is_free(self, index, count=1):
-        pl.semaphore_wait(self.free.at[index], count)
-
-    def z_chip(self, away):
-        there = (self.z + 1 + away) % 4
-        return there, self.chip + (there - self.z) * 4
-
-    def z_peers(self):
-        return [(self.core, self.z_chip(away)[1]) for away in range(3)]
-
-    def add(self, start, size, parts):
+    def add(self, start, size, part_start, buf):
         chunk = min(size, 128)
         while size % chunk:
             chunk -= 16
 
         def one(step, carry):
             at = pl.ds(pl.multiple_of(start + step * chunk, 16), chunk)
-            here = pl.ds(pl.multiple_of(step * chunk, 16), chunk)
+            here = pl.ds(pl.multiple_of(part_start + step * chunk, 16), chunk)
             total = self.buffer[at].astype(F32)
-            for part in parts:
-                total = total + part[here].astype(F32)
+            for part in range(buf.shape[0]):
+                total = total + buf[part, here].astype(F32)
             self.buffer[at] = total.astype(BF16)
             return carry
 
         lax.fori_loop(0, size // chunk, one, 0)
 
-    def small_go(self, stage, core, chip):
+    def send_parts(self, number):
+        at, _, part, _, others, buf, first = self.stages[number]
+        for place, (other, core, chip) in enumerate(others):
+            self.copy(first + place, self.rows(at + other * part, part), buf.at[place], core, chip).start()
+
+    def send_back(self, number):
+        at, _, part, own, others, _, first = self.stages[number]
+        pl.semaphore_wait(self.free.at[number], len(others))
+        mine = self.rows(at + own * part, part)
+        for place, (_, core, chip) in enumerate(others):
+            self.copy(self.back + first + place, mine, mine, core, chip).start()
+
+    def step(self, number):
+        count = len(self.stages)
+        if number == 0:
+            self.send_parts(0)
+        elif number <= count:
+            at, _, part, own, others, buf, first = self.stages[number - 1]
+            for place, (_, core, chip) in enumerate(others):
+                self.done(first + place, buf.at[place])
+            for _, core, chip in others:
+                pl.semaphore_signal(self.free.at[number - 1], inc=1, device_id=(core, chip), device_id_type=MESH)
+            kept = at + own * part
+            if number < count:
+                _, _, next_part, next_own, next_others, _, _ = self.stages[number]
+                for other, _, _ in next_others:
+                    self.add(kept + other * next_part, next_part, other * next_part, buf)
+                self.send_parts(number)
+                self.add(kept + next_own * next_part, next_part, next_own * next_part, buf)
+            else:
+                self.add(kept, part, 0, buf)
+                self.send_back(count - 1)
+        else:
+            stage = 2 * count - number
+            at, _, part, own, others, _, first = self.stages[stage]
+            for place in range(len(others)):
+                self.done(self.back + first + place, self.rows(at + own * part, part))
+            if stage > 0:
+                self.send_back(stage - 1)
         if self.small is not None:
-            own, taken = self.small
-            self.go(12 + stage, own, taken.at[stage], core, chip)
-
-    def small_done(self, stage):
-        if self.small is not None:
-            own, taken = self.small
-            self.done(12 + stage, own)
-            own[...] = own[...] + taken[stage]
-
-    def small_z_go(self):
-        if self.small is not None:
-            own, taken = self.small
+            self.small_step(number)
+
+    def small_step(self, number):
+        own, taken = self.small
+        first = 2 * self.back
+        if number in (1, 2, 3):
+            self.done(first + number - 1, own)
+            own[...] = own[...] + taken[number - 1]
+        if number < 3:
+            core, chip = ((1 - self.core, self.chip), self.peer_x, self.peer_y)[number]
+            self.copy(first + number, own, taken.at[number], core, chip).start()
+        if number == 3:
             taken[3 + self.z] = own[...]
-            for away in range(3):
-                self.go(15 + away, own, taken.at[3 + self.z], self.core, self.z_chip(away)[1])
-
-    def small_z_done(self):
-        if self.small is not None:
-            own, taken = self.small
-            for away in range(3):
-                self.done(15 + away, own)
+            for place, (core, chip) in enumerate(self.z_peers):
+                self.copy(first + 3 + place, own, taken.at[3 + self.z], core, chip).start()
+        if number == 4:
+            for place in range(3):
+                self.done(first + 3 + place, own)
             own[...] = (taken[3] + taken[4]) + (taken[5] + taken[6])
 
-    def step(self, number):
-        size, core, chip = self.size, self.core, self.chip
-        if number == 0:
-            self.go(0, self.rows(self.out, size), self.from_core, 1 - core, chip)
-            self.small_go(0, 1 - core, chip)
-        if number == 1:
-            self.done(0, self.from_core)
-            self.freed(0, (1 - core, chip))
-            self.add(self.one_out, size // 2, (self.part(self.from_core, self.one_out - self.at, size // 2),))
-            self.go(1, self.rows(self.one_out, size // 2), self.from_one, core, self.peer_one)
-            self.add(self.one_at, size // 2, (self.part(self.from_core, self.one_at - self.at, size // 2),))
-            self.small_done(0)
-            self.small_go(1, core, self.peer_x)
-        if number == 2:
-            self.done(1, self.from_one)
-            self.freed(1, (core, self.peer_one))
-            self.add(self.two_out, size // 4, (self.part(self.from_one, self.two_out - self.one_at, size // 4),))
-            self.go(2, self.rows(self.two_out, size // 4), self.from_two, core, self.peer_two)
-            self.add(self.two_at, size // 4, (self.part(self.from_one, self.two_at - self.one_at, size // 4),))
-            self.small_done(1)
-            self.small_go(2, core, self.peer_y)
-        if number == 3:
-            self.done(2, self.from_two)
-            self.freed(2, (core, self.peer_two))
-            self.add(self.two_at, size // 4, (self.from_two,))
-            for away in range(3):
-                there, peer = self.z_chip(away)
-                self.go(3 + away, self.rows(self.two_at + there * (size // 16), size // 16), self.from_z.at[away], core, peer)
-            self.small_done(2)
-            self.small_z_go()
-        if number == 4:
-            for away in range(3):
-                self.done(3 + away, self.from_z.at[away])
-            self.freed(3, *self.z_peers())
-            self.add(self.z_at, size // 16, tuple(self.from_z.at[away] for away in range(3)))
-            own = self.rows(self.z_at, size // 16)
-            self.is_free(3, 3)
-            for away in range(3):
-                self.go(6 + away, own, own, core, self.z_chip(away)[1])
-            self.small_z_done()
-        if number == 5:
-            for away in range(3):
-                self.done(6 + away, self.rows(self.z_at, size // 16))
-            own = self.rows(self.two_at, size // 4)
-            self.is_free(2)
-            self.go(9, own, own, core, self.peer_two)
-        if number == 6:
-            self.done(9, self.rows(self.two_at, size // 4))
-            own = self.rows(self.one_at, size // 2)
-            self.is_free(1)
-            self.go(10, own, own, core, self.peer_one)
-        if number == 7:
-            self.done(10, self.rows(self.one_at, size // 2))
-            own = self.rows(self.at, size)
-            self.is_free(0)
-            self.go(11, own, own, 1 - core, chip)
-        if number == 8:
-            self.done(11, self.rows(self.at, size))
-
-    def part(self, ref, start, size):
-        return ref.at[pl.ds(pl.multiple_of(start, 16), size)]
-
 
 REDUCTION_SEMS = 18
 
 
-def reduction_scratch(rows):
-    return [
-        pltpu.VMEM(shape + (512,), BF16) for shape in ((rows // 2,), (rows // 4,), (rows // 8,), (3, rows // 32))
-    ]
+def reduction_scratch(rows, by_z):
+    shapes = [(1, rows // 2), (1, rows // 4), (1, rows // 8)]
+    shapes += [(1, rows // 16), (1, rows // 32)] if by_z else [(3, rows // 32)]
+    return [pltpu.VMEM(shape + (512,), BF16) for shape in shapes]
 
 
 def gelu_pair(value):
@@ -817,11 +782,10 @@
     me = core * n + chip
 
     loads = {}
-    count_early, count_late = len(EARLY_CHUNKS), len(LATE_CHUNKS)
-    chunk_refs = refs[-4 * (count_early + count_late) :]
+    chunk_refs = list(refs[len(refs) - sum(5 if cut[2] else 4 for cut in EARLY_CHUNKS + LATE_CHUNKS) :])
 
     def reduction(buffer, index, cut, small=None):
-        bufs = chunk_refs[4 * index : 4 * index + 4]
+        bufs = [chunk_refs.pop(0) for _ in range(5 if cut[2] else 4)]
         return Reduction(buffer, *cut, bufs, r.sum_sem.at[index], r.sum_free.at[index], small)
 
     for index, (name, source) in enumerate(given.items()):
@@ -1068,9 +1032,10 @@
         send(*job)
 
     early, late = r.early, r.late
+    count_early, count_late = len(EARLY_CHUNKS), len(LATE_CHUNKS)
     sums = [reduction(early, index, cut) for index, cut in enumerate(EARLY_CHUNKS)]
     for index, cut in enumerate(LATE_CHUNKS):
-        small_pair = (small, r.small_in) if index == 0 else None
+        small_pair = (small, r.small_in) if index == count_late - 1 else None
         sums.append(reduction(late, count_early + index, cut, small_pair))
 
     def steps_at(moment):
@@ -1081,6 +1046,7 @@
         at = slice(part * width, (part + 1) * width)
         early[at] = dot(r.ffn_input[...], r.grad_pre[:, at], OVER_ROWS).astype(BF16)
     sums[0].step(0)
+    steps_at(-4)
     for part in range(4):
         at = slice(part * width, (part + 1) * width)
         early[2048 + part * width : 2048 + (part + 1) * width] = dot(
@@ -1194,7 +1160,7 @@
     small[3:5, pair_at] = jnp.where(
         odd, jnp.concatenate([nothing, dbias], 1), jnp.concatenate([dbias, nothing], 1)
     )
-    sums[5].step(0)
+    sums[3].step(0)
     steps_at(8)
     for source, _, sems, to_core, to_chip in second_jobs:
         sent(source, sems[0], to_core, to_chip)
@@ -1205,13 +1171,13 @@
     for turn in range(rounds):
         sent(r.dkv_out.at[turn * group + core], r.send_sem.at[4], row, turn * group + core)
         give_over(turn).wait_send()
-    steps_at(9)
     arrived(r.dq_in, r.dq_sem.at[0])
     arrived(r.dkv_in, r.dkv_sem.at[0])
     grad_query = joined(lambda h: r.dq_in[h].astype(F32)).astype(BF16)
     both = [r.dkv_in[h].astype(F32) for h in range(HEADS)]
     grad_keys = jnp.concatenate([part[:, :HEAD] for part in both], 1).astype(BF16)
     grad_values = jnp.concatenate([part[:, HEAD:] for part in both], 1).astype(BF16)
+    steps_at(9)
     attn_in = r.attn_in[...]
     late[1536:2048] = dot(attn_in, grad_query, OVER_ROWS).astype(BF16)
     late[2048:2560] = dot(attn_in, grad_keys, OVER_ROWS).astype(BF16)
@@ -1229,6 +1195,7 @@
     grad_pooled = (r.grad_final[...] + norm_grad(grad_normed, plain, inverse, r.ln1_g[...])).astype(BF16)
     r.grad_pooled[...] = grad_pooled
     grad_pooled_wide = grad_pooled.astype(F32)
+    steps_at(11)
     small[0:1] = column_sum(grad_pooled_wide)
 
     def back_rim_copy():
@@ -1249,8 +1216,9 @@
     late[:1024] = (
         dot(r.x3[:, width:], within, OVER_ROWS) + dot(r.rim[...], rim_row, OVER_ROWS)
     ).astype(BF16)
-    sums[3].step(0)
-    steps_at(11)
+    for later in sums[5:]:
+        later.step(0)
+    steps_at(12)
 
     @pl.when(chip == n - 1)
     def _():
@@ -1275,26 +1243,24 @@
     def _():
         back_rim_copy().wait_send()
 
-    steps_at(12)
+    steps_at(13)
 
 
 SCHEDULE = {
     -2: ((0, 1),),
     -1: ((1, 1),),
-    0: ((0, 2), (2, 1)),
-    1: ((0, 3), (1, 2)),
-    2: ((1, 3), (2, 2)),
-    3: ((0, 4),),
-    4: ((2, 3), (1, 4)),
-    5: ((0, 5), (2, 4)),
-    7: ((1, 5), (0, 6)),
-    8: ((2, 5), (5, 1)),
-    9: ((1, 6),),
-    10: ((0, 7), (5, 2), (2, 6)),
-    11: ((4, 1), (1, 7), (5, 3)),
-    12: (
-        (3, 1), (4, 2), (2, 7), (5, 4), (3, 2), (4, 3), (5, 5), (3, 3), (4, 4), (5, 6), (3, 4), (4, 5), (5, 7),
-        (3, 5), (4, 6), (3, 6), (4, 7), (3, 7), (0, 8), (1, 8), (2, 8), (5, 8), (4, 8), (3, 8),
+    0: ((2, 1), (0, 2),),
+    2: ((0, 3), (1, 2),),
+    6: ((2, 2),),
+    8: ((3, 1), (0, 4), (1, 3),),
+    10: ((2, 3),),
+    11: ((4, 1),),
+    12: ((1, 4), (5, 1), (0, 5),),
+    13: (
+        (3, 2), (4, 2), (2, 4), (1, 5), (6, 1), (0, 6), (5, 2), (1, 6), (4, 3), (6, 2), (3, 3), (5, 3), (2, 5),
+        (6, 3), (3, 4), (1, 7), (5, 4), (4, 4), (0, 7), (2, 6), (6, 4), (5, 5), (3, 5), (1, 8), (0, 8), (3, 6),
+        (5, 6), (4, 5), (2, 7), (5, 7), (3, 7), (4, 6), (3, 8), (5, 8), (1, 9), (6, 5), (2, 8), (1, 10), (6, 6),
+        (4, 7), (5, 9), (6, 7), (5, 10), (4, 8), (6, 8),
     ),
 }
 
@@ -1411,7 +1377,8 @@
         edges=pltpu.VMEM((2, 16, 128), jnp.int32), load_sem=dma((len(given),)), side_sem=dma((6,)), send_sem=dma((8,)), other_sem=dma((rounds,)),
 
         q_sem=dma((rounds,)), kv_sem=dma((n,)), att_sem=dma((1,)), grad_sem=dma((rounds,)), dkv_sem=dma((1,)),
-        dq_sem=dma((1,)), sum_sem=dma((6, 2, REDUCTION_SEMS)), sum_free=signal((6, 4)),
+        dq_sem=dma((1,)), sum_sem=dma((len(EARLY_CHUNKS + LATE_CHUNKS), 2, REDUCTION_SEMS)),
+        sum_free=signal((len(EARLY_CHUNKS + LATE_CHUNKS), 5)),
     )
     layout = (list(given), list(vectors) + ["bounds"], list(outs), list(scratch))
     out3, grad3, early, late, small = pl.pallas_call(
@@ -1422,7 +1389,7 @@
         out_specs=[vmem] * len(outs),
         out_shape=[jax.ShapeDtypeStruct(*out) for out in outs.values()],
         scratch_shapes=list(scratch.values())
-        + sum((reduction_scratch(rows) for _, rows in EARLY_CHUNKS + LATE_CHUNKS), []),
+        + sum((reduction_scratch(*cut[1:]) for cut in EARLY_CHUNKS + LATE_CHUNKS), []),
         compiler_params=pltpu.CompilerParams(
             collective_id=0, has_side_effects=True, vmem_limit_bytes=60 * 2**20
         ),

time: 218 us -> 189 us (0.87)
  Pallas kernels: 214 us -> 186 us
    pallas_call x1, Pallas kernels: 202 us -> 173 us  [fused_body(): pl.pallas_call(functools.partial(layer_kernel, n, length, layout), in_spe...]
where the time goes in v4:
time: 189 us
  Pallas kernels  186 us (98%)
    pallas_call x1, Pallas kernels, fused_body(): pl.pallas_call(functools.partial(layer_kernel, n, length, layout), in_spe...  173 us
    pallas_call x1, Pallas kernels, finished(): pl.pallas_call(last_kernel, in_specs=[vmem] * 5, out_specs=[pl.BlockSpec(...  12.2 us

profile of v4, /device:TPU:0, one launch (start us, length us, event | category | flops | bytes accessed | tf_op | source)
XLA Modules:
  0.0 189.0 jit_solution(18443634829640551381)
XLA Ops:
  0.7 1.3 broadcast_in_dim.45.refs_21_
  2.0 173.5 %shard_map.400 = (bf16[192,1536]{1,0:T(8,128)(2,1)}, bf16[192,1536]{1,0:T(8,128)(2,1)}, bf16[6144,512]{1,0:T(8,128)(2,1)}, bf16[3584,512]{1,0:T(8,128)(2,1)}, f32[16,512]{1,0:T(8,128)}) custom-call(bf16[576,512]{1,0:T(8,128)(2,1)} %bitcast.22, bf16[1536,512]{1,0:T(8,128)(2,1)} %refs_1_.1, bf16[512,512]{1,0:T(8,128)(2,1)} %refs_2_.1, ...), custom_call_target="tpu_custom_call" | custom-call | tf_op jit(solution)/shard_map/pallas_call | solution.py:1384
  175.4 12.2 %shard_map.401 = (f32[512,2048]{1,0:T(8,128)}, f32[2048,512]{1,0:T(8,128)}, f32[512,1536]{1,0:T(8,128)}, f32[512,512]{1,0:T(8,128)}, f32[1536,512]{1,0:T(8,128)}...) custom-call(bf16[6144,512]{1,0:T(8,128)(2,1)} %get-tuple-element.47., ...), custom_call_target="tpu_custom_call" | custom-call | tf_op jit(solution)/shard_map/pallas_call | solution.py:1316
  187.7 1.3 reduce

commit v5 on v4

--- a/solution.py
+++ b/solution.py
@@ -331,9 +331,9 @@
         dkv_ref[...] = dkv_acc[...].astype(BF16)
 
 
-def wave_tables(tokens, length, width):
+def wave_tables(tokens, length, width, more=0):
     rates = 10000.0 ** (-2.0 * np.arange(width // 2, dtype=np.float64) / width)
-    far = (np.arange(tokens + length, dtype=np.float64) - (tokens - length))[:, None] * rates
+    far = (np.arange(tokens + max(length, more), dtype=np.float64) - (tokens - length))[:, None] * rates
     near = np.arange(length, dtype=np.float64)[:, None] * rates
     table = np.concatenate([np.sin(far), np.cos(far)], 1)
     return (
@@ -598,8 +598,10 @@
 
 EARLY_ROWS, LATE_ROWS = 6144, 3584
 EARLY_CHUNKS = ((0, 2048, False), (2048, 2048, True), (4096, 2048, False))
-LATE_CHUNKS = ((3072, 512, False), (1536, 1536, False), (0, 1024, True), (1024, 512, False))
+LATE_CHUNKS = ((3072, 512, False), (1536, 1024, False), (2560, 512, True), (0, 1024, False), (1024, 512, True))
+QKV_SUMS, POOL_SUMS = slice(4, 6), slice(6, None)
 SMALL_ROWS = 16
+TILE = 512
 OVER_ROWS = ((0,), (0,))
 OVER_COLUMNS = ((1,), (1,))
 
@@ -767,14 +769,17 @@
     return jnp.sum(value, 0, keepdims=True)
 
 
+def most_tiles(turn, length):
+    return ((2 * turn + 2) * length + TILE - 1) // TILE
+
+
 def layer_kernel(n, length, layout, *refs):
     taken = iter(refs)
     given, vectors, outs, scratch = ({name: next(taken) for name in part} for part in layout)
     r = types.SimpleNamespace(**vectors, **outs, **scratch)
     group = 2
     rounds = n // group
-    tile = 2 * length
-    half_len = length // 2
+    tile = TILE
     width = 512
     scale = HEAD**-0.5
     core, chip, row, head, member = whereabouts(group)
@@ -874,11 +879,14 @@
             jobs.append((array.at[h], out.at[turn_to], (sem, recv.at[turn_to]), to_core, to_chip))
         return jobs
 
+    def rows_in(block):
+        return pl.ds(pl.multiple_of(block * length, length), length)
+
     kv_jobs = []
     for h in range(HEADS):
         to_chip, _ = chip_of(core, h, 0, group)
         sems = (r.send_sem.at[1], r.kv_sem.at[chip])
-        kv_jobs.append((r.kv_out.at[h], r.kv.at[chip], sems, chip % 2, to_chip))
+        kv_jobs.append((r.kv_out.at[h], r.kv.at[rows_in(chip)], sems, chip % 2, to_chip))
     first_jobs = kv_jobs + q_jobs(r.q_out, r.q, r.send_sem.at[0], r.q_sem)
     for job in first_jobs:
         send(*job)
@@ -916,32 +924,43 @@
     half = width // 2
     lanes = lax.broadcasted_iota(jnp.int32, (length, tile), 1)
 
-    def rows_of(array):
-        return pl.ds(pl.multiple_of(array, length), tile)
+    def rows_of(start):
+        return pl.ds(pl.multiple_of(start, 64), tile)
+
+    def tiles_to(block):
+        return ((block + 1) * length + tile - 1) // tile
+
+    def kept_at(turn):
+        return sum(jnp.where(turn > before, most_tiles(before, length), 0) for before in range(rounds - 1))
 
     def forward(turn):
         at = turn * group + core
         return pltpu.make_async_remote_copy(
-            r.kv.at[at], r.kv.at[at], r.send_sem.at[6], r.kv_sem.at[at], device_id=(1 - core, chip), device_id_type=MESH
+            r.kv.at[rows_in(at)], r.kv.at[rows_in(at)], r.send_sem.at[6], r.kv_sem.at[at], device_id=(1 - core, chip), device_id_type=MESH
         )
 
     def pass_on(turn):
         at = turn * group + core
-        arrived(r.kv.at[at], r.kv_sem.at[at])
+        arrived(r.kv.at[rows_in(at)], r.kv_sem.at[at])
         forward(turn).start()
 
     pass_on(0)
+    pass_on(1)
+    arrived(r.kv.at[rows_in(1 - core)], r.kv_sem.at[1 - core])
 
     def attend(turn, carry):
         block = block_of(turn, member, group)
 
+        @pl.when(turn < rounds - 2)
+        def _():
+            pass_on(turn + 2)
+
         @pl.when(turn < rounds - 1)
         def _():
-            pass_on(turn + 1)
+            other = (turn + 1) * group + 1 - core
+            arrived(r.kv.at[rows_in(other)], r.kv_sem.at[other])
 
         arrived(r.q.at[turn], r.q_sem.at[turn])
-        other = turn * group + 1 - core
-        arrived(r.kv.at[other], r.kv_sem.at[other])
         query_u, _, turned = query_parts(
             r.q[turn], content_bias, pos_bias, r.head_w[...], r.sines[...], r.cosines[...]
         )
@@ -952,7 +971,7 @@
         opening = jnp.where(places >= high_edge, high_edge, jnp.where(places >= low_edge, low_edge, 0))
 
         def score_step(step, top):
-            pair = r.kv[pl.ds(step * group, group)].reshape(tile, PAIR)
+            pair = r.kv[rows_of(step * tile), :]
             waves = r.table[rows_of((n - 1 - block) * length + step * tile), :]
             score = dot(r.extra[:, :PAIR], pair, OVER_COLUMNS) + dot(r.extra[:, PAIR:], waves, OVER_COLUMNS)
             at = lanes + step * tile
@@ -963,7 +982,8 @@
                 top = jnp.maximum(top, score[:, part * 128 : (part + 1) * 128])
             return top
 
-        top = lax.fori_loop(0, turn + 1, score_step, jnp.full((length, 128), masked_score, F32))
+        kept, tiles = kept_at(turn), tiles_to(block)
+        top = lax.fori_loop(0, tiles, score_step, jnp.full((length, 128), masked_score, F32))
         top = jnp.max(top, 1, keepdims=True)
 
         def value_step(step, state):
@@ -972,12 +992,12 @@
             for part in range(tile // 128):
                 total = total + weight[:, part * 128 : (part + 1) * 128]
             low = weight.astype(BF16)
-            r.keep[turn * (turn + 1) // 2 + step] = low
-            pair = r.kv[pl.ds(step * group, group)].reshape(tile, PAIR)
+            r.keep[kept + step] = low
+            pair = r.kv[rows_of(step * tile), :]
             return total, summed + dot(low, pair)
 
         total, summed = lax.fori_loop(
-            0, turn + 1, value_step, (jnp.zeros((length, 128), F32), jnp.zeros((length, PAIR), F32))
+            0, tiles, value_step, (jnp.zeros((length, 128), F32), jnp.zeros((length, PAIR), F32))
         )
         inverse = 1.0 / jnp.sum(total, 1, keepdims=True)
         attended = summed[:, HEAD:] * inverse
@@ -1038,9 +1058,17 @@
         small_pair = (small, r.small_in) if index == count_late - 1 else None
         sums.append(reduction(late, count_early + index, cut, small_pair))
 
+    def leave(index):
+        cut = (EARLY_CHUNKS + LATE_CHUNKS)[index]
+        buffer, target = (early, r.early_o) if index < count_early else (late, r.late_o)
+        at = pl.ds(cut[0], cut[1])
+        return pltpu.make_async_copy(buffer.at[at], target.at[at], r.leave_sem.at[index])
+
     def steps_at(moment):
         for index, number in SCHEDULE.get(moment, ()):
             sums[index].step(number)
+            if number == sums[index].last:
+                leave(index).start()
 
     for part in range(4):
         at = slice(part * width, (part + 1) * width)
@@ -1103,9 +1131,9 @@
         r.far[...] = jnp.zeros_like(r.far)
 
         def step_over(step, inner):
-            pair = r.kv[pl.ds(step * group, group)].reshape(tile, PAIR)
+            pair = r.kv[rows_of(step * tile), :]
             waves = r.table[rows_of((n - 1 - block) * length + step * tile), :]
-            weight = r.keep[turn * (turn + 1) // 2 + step]
+            weight = r.keep[kept + step]
             grad_weight = dot(r.extra[:, :PAIR], pair, OVER_COLUMNS)
             grad_score = (weight.astype(F32) * (grad_weight - delta)).astype(BF16)
             r.near[...] += dot(grad_score, pair)
@@ -1116,7 +1144,8 @@
             )
             return inner
 
-        lax.fori_loop(0, turn + 1, step_over, 0)
+        kept = kept_at(turn)
+        lax.fori_loop(0, tiles_to(block), step_over, 0)
         give = turn * group + 1 - core
         r.dkv_out[give] = r.dkv[pl.ds(pl.multiple_of(give * length, length), length)].astype(BF16)
         give_over(turn).start()
@@ -1179,11 +1208,6 @@
     grad_values = jnp.concatenate([part[:, HEAD:] for part in both], 1).astype(BF16)
     steps_at(9)
     attn_in = r.attn_in[...]
-    late[1536:2048] = dot(attn_in, grad_query, OVER_ROWS).astype(BF16)
-    late[2048:2560] = dot(attn_in, grad_keys, OVER_ROWS).astype(BF16)
-    late[2560:3072] = dot(attn_in, grad_values, OVER_ROWS).astype(BF16)
-    sums[4].step(0)
-    steps_at(10)
     grad_normed = (
         dot(grad_query, r.q_w[...], OVER_COLUMNS)
         + dot(grad_keys, r.k_w[...], OVER_COLUMNS)
@@ -1195,7 +1219,7 @@
     grad_pooled = (r.grad_final[...] + norm_grad(grad_normed, plain, inverse, r.ln1_g[...])).astype(BF16)
     r.grad_pooled[...] = grad_pooled
     grad_pooled_wide = grad_pooled.astype(F32)
-    steps_at(11)
+    steps_at(10)
     small[0:1] = column_sum(grad_pooled_wide)
 
     def back_rim_copy():
@@ -1216,7 +1240,13 @@
     late[:1024] = (
         dot(r.x3[:, width:], within, OVER_ROWS) + dot(r.rim[...], rim_row, OVER_ROWS)
     ).astype(BF16)
-    for later in sums[5:]:
+    for later in sums[POOL_SUMS]:
+        later.step(0)
+    steps_at(11)
+    late[1536:2048] = dot(attn_in, grad_query, OVER_ROWS).astype(BF16)
+    late[2048:2560] = dot(attn_in, grad_keys, OVER_ROWS).astype(BF16)
+    late[2560:3072] = dot(attn_in, grad_values, OVER_ROWS).astype(BF16)
+    for later in sums[QKV_SUMS]:
         later.step(0)
     steps_at(12)
 
@@ -1244,23 +1274,24 @@
         back_rim_copy().wait_send()
 
     steps_at(13)
+    for index in range(len(sums)):
+        leave(index).wait()
 
 
 SCHEDULE = {
-    -2: ((0, 1),),
-    -1: ((1, 1),),
-    0: ((2, 1), (0, 2),),
-    2: ((0, 3), (1, 2),),
-    6: ((2, 2),),
-    8: ((3, 1), (0, 4), (1, 3),),
-    10: ((2, 3),),
-    11: ((4, 1),),
-    12: ((1, 4), (5, 1), (0, 5),),
+    -2: ((1, 1),),
+    -1: ((0, 1),),
+    1: ((0, 2),),
+    2: ((1, 2), (2, 1), (0, 3),),
+    8: ((2, 2), (1, 3), (0, 4), (3, 1),),
+    10: ((1, 4),),
+    11: ((2, 3),),
+    12: ((3, 2), (0, 5), (7, 1), (4, 1), (3, 3), (1, 5), (5, 1), (6, 1),),
     13: (
-        (3, 2), (4, 2), (2, 4), (1, 5), (6, 1), (0, 6), (5, 2), (1, 6), (4, 3), (6, 2), (3, 3), (5, 3), (2, 5),
-        (6, 3), (3, 4), (1, 7), (5, 4), (4, 4), (0, 7), (2, 6), (6, 4), (5, 5), (3, 5), (1, 8), (0, 8), (3, 6),
-        (5, 6), (4, 5), (2, 7), (5, 7), (3, 7), (4, 6), (3, 8), (5, 8), (1, 9), (6, 5), (2, 8), (1, 10), (6, 6),
-        (4, 7), (5, 9), (6, 7), (5, 10), (4, 8), (6, 8),
+        (7, 2), (2, 4), (4, 2), (1, 6), (6, 2), (3, 4), (5, 2), (7, 3), (0, 6), (4, 3), (1, 7), (5, 3), (6, 3),
+        (2, 5), (3, 5), (5, 4), (7, 4), (4, 4), (5, 5), (6, 4), (7, 5), (1, 8), (3, 6), (2, 6), (5, 6), (7, 6),
+        (4, 5), (0, 7), (7, 7), (3, 7), (6, 5), (0, 8), (5, 7), (3, 8), (7, 8), (4, 6), (6, 6), (5, 8), (1, 9),
+        (2, 7), (7, 9), (4, 7), (5, 9), (1, 10), (6, 7), (7, 10), (4, 8), (2, 8), (5, 10), (6, 8),
     ),
 }
 
@@ -1275,24 +1306,22 @@
 def last_kernel(*refs):
     early, late, out3, grad3, small = refs[:5]
     wide_outs, narrow_outs, byte_outs = refs[5:14], refs[14:24], refs[24:26]
-    staging, mixing, sems = refs[26:]
-    copies = []
-    for index, (out, (start, blocks, across)) in enumerate(zip(wide_outs, WIDENED)):
-        source = early if index < 4 else late
-        for block in range(blocks):
-            slot = len(copies)
-
-            def widen(step, carry, source=source, slot=slot, first=start + block * 512):
-                here = pl.ds(pl.multiple_of(step * 64, 64), 64)
-                staging[slot, here] = source[pl.ds(pl.multiple_of(first + step * 64, 64), 64)].astype(F32)
-                return carry
-
-            lax.fori_loop(0, 8, widen, 0)
+    loaded, staging, mixing, load_sems, sems = refs[26:]
+    blocks = []
+    for index, (out, (start, count, across)) in enumerate(zip(wide_outs, WIDENED)):
+        for block in range(count):
+            first = start + block * 512
             at = slice(block * 512, (block + 1) * 512)
-            target = out.at[:, at] if across else out.at[at]
-            copy = pltpu.make_async_copy(staging.at[slot], target, sems.at[slot])
-            copy.start()
-            copies.append(copy)
+            source = (early if index < 4 else late).at[first : first + 512]
+            blocks.append((source, out.at[:, at] if across else out.at[at]))
+    loads = [
+        pltpu.make_async_copy(source, loaded.at[slot], load_sems.at[slot]) for slot, (source, _) in enumerate(blocks)
+    ]
+    stores = [
+        pltpu.make_async_copy(staging.at[slot], target, sems.at[slot]) for slot, (_, target) in enumerate(blocks)
+    ]
+    for load in loads:
+        load.start()
     for out, tokens in zip(byte_outs, (out3, grad3)):
         length, width = out.shape[0] // 3, out.shape[1]
         for block in range(width // 128):
@@ -1300,11 +1329,21 @@
                 start = part * width + block * 128
                 mixing[block, pl.ds(part, length, stride=3), :] = tokens[:, start : start + 128].astype(F32)
             out[:, block * 128 : (block + 1) * 128] = mixing[block].astype(BF16)
-    for out, (start, blocks) in zip(narrow_outs, NARROW):
-        for block in range(blocks):
+    for slot in range(len(blocks)):
+        loads[slot].wait()
+
+        def widen(step, carry, slot=slot):
+            here = pl.ds(pl.multiple_of(step * 64, 64), 64)
+            staging[slot, here] = loaded[slot, here].astype(F32)
+            return carry
+
+        lax.fori_loop(0, 8, widen, 0)
+        stores[slot].start()
+    for out, (start, count) in zip(narrow_outs, NARROW):
+        for block in range(count):
             out[:, block * 512 : (block + 1) * 512] = small[start + block : start + block + 1]
-    for copy in copies:
-        copy.wait()
+    for store in stores:
+        store.wait()
 
 
 def finished(early, late, out3, grad3, small):
@@ -1315,13 +1354,13 @@
     count = sum(blocks for _, blocks, _ in WIDENED)
     outs = pl.pallas_call(
         last_kernel,
-        in_specs=[vmem] * 5,
+        in_specs=[pl.BlockSpec(memory_space=pl.ANY)] * 2 + [vmem] * 3,
         out_specs=[pl.BlockSpec(memory_space=pl.ANY)] * len(shapes) + [vmem] * (len(narrow) + 2),
         out_shape=[jax.ShapeDtypeStruct(shape, F32) for shape in shapes + narrow]
         + [jax.ShapeDtypeStruct((3 * length, width), BF16)] * 2,
         scratch_shapes=[
-            pltpu.VMEM((count, 512, 512), F32), pltpu.VMEM((width // 128, 3 * length, 128), F32),
-            pltpu.SemaphoreType.DMA((count,)),
+            pltpu.VMEM((count, 512, 512), BF16), pltpu.VMEM((count, 512, 512), F32), pltpu.VMEM((width // 128, 3 * length, 128), F32),
+            pltpu.SemaphoreType.DMA((count,)), pltpu.SemaphoreType.DMA((count,)),
         ],
         compiler_params=pltpu.CompilerParams(vmem_limit_bytes=56 * 2**20),
     )(early, late, out3, grad3, small)
@@ -1338,7 +1377,7 @@
     n = lax.axis_size("seq")
     tokens = n * length
     rounds = n // 2
-    table, sines, cosines = wave_tables(tokens, length, width)
+    table, sines, cosines = wave_tables(tokens, length, width, TILE)
     given = dict(
         x_bytes=inputs[0], pool_w=pool_weight, q_w=query_weight, k_w=key_weight, v_w=value_weight,
         ct_bytes=cotangent[0], up_w=up_weight, ffn_out=ffn_out, pos_w=pos_weight, table=table,
@@ -1351,8 +1390,8 @@
     vectors = {name: vector[None] for name, vector in vectors.items()} | dict(sines=sines, cosines=cosines)
     vmem = pl.BlockSpec(memory_space=pltpu.VMEM)
     outs = dict(
-        out3=((length, 3 * width), BF16), grad3=((length, 3 * width), BF16), early=((EARLY_ROWS, 512), BF16),
-        late=((LATE_ROWS, 512), BF16), small=((SMALL_ROWS, 512), F32),
+        out3=((length, 3 * width), BF16), grad3=((length, 3 * width), BF16), small=((SMALL_ROWS, 512), F32),
+        early_o=((EARLY_ROWS, 512), BF16), late_o=((LATE_ROWS, 512), BF16),
     )
     pair_half = (length // 2, PAIR)
     block, wide = (length, width), (length, 4 * width)
@@ -1360,14 +1399,14 @@
     scratch = {name: pltpu.VMEM(array.shape, array.dtype) for name, array in given.items()}
     low = dict(
         x3=(length, 3 * width), ct3=(length, 3 * width), rim=(16, 2 * width), back_rim=(16, width), attn_in=block, q_out=(HEADS,) + pair_half,
-        kv_out=(HEADS, length, PAIR), q=(rounds,) + pair_half, kv=(n, length, PAIR), grad_branch=block,
-        head_w=(width, HEAD), extra=(length, PAIR + width), keep=(rounds * (rounds + 1) // 2, length, 2 * length),
+        kv_out=(HEADS, length, PAIR), q=(rounds,) + pair_half, kv=(tokens, PAIR), grad_branch=block,
+        head_w=(width, HEAD), extra=(length, PAIR + width), keep=(sum(most_tiles(turn, length) for turn in range(rounds)), length, TILE),
         att_out=(rounds,) + pair_half, att_in=(HEADS,) + pair_half, att_low=block, ffn_input=block, act_low=wide,
         grad_pre=wide, grad=(rounds,) + pair_half, dkv_out=(n, length, PAIR), dkv_in=(HEADS, length, PAIR),
-        dkv_other=(rounds, length, PAIR), dq_out=(rounds,) + pair_half, dq_in=(HEADS,) + pair_half, grad_pooled=block,
+        dkv_other=(rounds, length, PAIR), dq_out=(rounds,) + pair_half, dq_in=(HEADS,) + pair_half, grad_pooled=block, early=(EARLY_ROWS, 512), late=(LATE_ROWS, 512),
     )
     full = dict(
-        mixing=(width // 128, 3 * length, 128), pooled=block, grad_final=block, grad_act=wide, score=(rounds, length, 2 * length), att=(rounds, length, PAIR),
+        mixing=(width // 128, 3 * length, 128), pooled=block, grad_final=block, grad_act=wide, score=(tokens // TILE, length, TILE), att=(rounds, length, PAIR),
         mixed=block, dkv=(tokens, PAIR), dhead=(width, HEAD), dbias=(8, HEAD), near=(length, PAIR), far=block,
         small_in=(7, SMALL_ROWS, 512),
     )
@@ -1378,20 +1417,20 @@
 
         q_sem=dma((rounds,)), kv_sem=dma((n,)), att_sem=dma((1,)), grad_sem=dma((rounds,)), dkv_sem=dma((1,)),
         dq_sem=dma((1,)), sum_sem=dma((len(EARLY_CHUNKS + LATE_CHUNKS), 2, REDUCTION_SEMS)),
-        sum_free=signal((len(EARLY_CHUNKS + LATE_CHUNKS), 5)),
+        sum_free=signal((len(EARLY_CHUNKS + LATE_CHUNKS), 5)), leave_sem=dma((len(EARLY_CHUNKS + LATE_CHUNKS),)),
     )
     layout = (list(given), list(vectors) + ["bounds"], list(outs), list(scratch))
-    out3, grad3, early, late, small = pl.pallas_call(
+    out3, grad3, small, early, late = pl.pallas_call(
         functools.partial(layer_kernel, n, length, layout),
         in_specs=[pl.BlockSpec(memory_space=pl.ANY)] * len(given)
         + [vmem] * len(vectors)
         + [pl.BlockSpec(memory_space=pltpu.SMEM)],
-        out_specs=[vmem] * len(outs),
+        out_specs=[vmem] * 3 + [pl.BlockSpec(memory_space=pl.ANY)] * 2,
         out_shape=[jax.ShapeDtypeStruct(*out) for out in outs.values()],
         scratch_shapes=list(scratch.values())
         + sum((reduction_scratch(*cut[1:]) for cut in EARLY_CHUNKS + LATE_CHUNKS), []),
         compiler_params=pltpu.CompilerParams(
-            collective_id=0, has_side_effects=True, vmem_limit_bytes=60 * 2**20
+            collective_id=0, has_side_effects=True, vmem_limit_bytes=62 * 2**20
         ),
     )(*given.values(), *vectors.values(), doc_bounds)
     wide, narrow, both = finished(early, late, out3, grad3, small)

time: 189 us -> 178 us (0.942)
  Pallas kernels: 186 us -> 174 us
    pallas_call x1, Pallas kernels: 173 us -> 162 us  [fused_body(): pl.pallas_call(functools.partial(layer_kernel, n, length, layout), in_spe...]
where the time goes in v5:
time: 178 us; the launch traced here: 177 us
  Pallas kernels  174 us (98%)
    pallas_call x1, Pallas kernels, fused_body(): pl.pallas_call(functools.partial(layer_kernel, n, length, layout), in_spe...  162 us
    pallas_call x1, Pallas kernels, finished(): pl.pallas_call(last_kernel, in_specs=[pl.BlockSpec(memory_space=pl.ANY)]...  12.1 us

profile of v5, /device:TPU:0, one launch (start us, length us, event | category | flops | bytes accessed | tf_op | source)
XLA Modules:
  0.0 177.4 jit_solution(9163369041957702753)
XLA Ops:
  0.7 1.3 broadcast_in_dim.45.refs_21_
  2.0 162.0 %shard_map.400 = (bf16[192,1536]{1,0:T(8,128)(2,1)}, bf16[192,1536]{1,0:T(8,128)(2,1)}, f32[16,512]{1,0:T(8,128)}, bf16[6144,512]{1,0:T(8,128)(2,1)}, bf16[3584,512]{1,0:T(8,128)(2,1)}) custom-call(bf16[576,512]{1,0:T(8,128)(2,1)} %bitcast.22, bf16[1536,512]{1,0:T(8,128)(2,1)} %refs_1_.1, bf16[512,512]{1,0:T(8,128)(2,1)} %refs_2_.1, ...), custom_call_target="tpu_custom_call" | custom-call | tf_op jit(solution)/shard_map/pallas_call | solution.py:1423
  164.0 12.1 %shard_map.401 = (f32[512,2048]{1,0:T(8,128)}, f32[2048,512]{1,0:T(8,128)}, f32[512,1536]{1,0:T(8,128)}, f32[512,512]{1,0:T(8,128)}, f32[1536,512]{1,0:T(8,128)}...) custom-call(bf16[6144,512]{1,0:T(8,128)(2,1)} %get-tuple-element.47., ...), custom_call_target="tpu_custom_call" | custom-call | tf_op jit(solution)/shard_map/pallas_call | solution.py:1355
  176.1 1.3 reduce

commit v6 on v5

--- a/solution.py
+++ b/solution.py
@@ -801,6 +801,8 @@
         for ref in which:
             next(loads[name] for name in given if scratch[name] is ref).wait()
 
+    r.up_b[...] = r.up_flat[...].reshape(1, 3 * width)
+
     barrier = pltpu.get_barrier_semaphore()
 
     def greet(step, carry):
@@ -1306,7 +1308,7 @@
 def last_kernel(*refs):
     early, late, out3, grad3, small = refs[:5]
     wide_outs, narrow_outs, byte_outs = refs[5:14], refs[14:24], refs[24:26]
-    loaded, staging, mixing, load_sems, sems = refs[26:]
+    loaded, staging, mixing, bytes_low, load_sems, sems = refs[26:]
     blocks = []
     for index, (out, (start, count, across)) in enumerate(zip(wide_outs, WIDENED)):
         for block in range(count):
@@ -1322,26 +1324,39 @@
     ]
     for load in loads:
         load.start()
-    for out, tokens in zip(byte_outs, (out3, grad3)):
+    for out, (start, count) in zip(narrow_outs, NARROW):
+        if count == 3:
+            out[...] = jnp.concatenate([small[start + block : start + block + 1] for block in range(count)], 1).reshape(-1)
+        else:
+            for block in range(count):
+                out[:, block * 512 : (block + 1) * 512] = small[start + block : start + block + 1]
+
+    def widen(slot):
+        loads[slot].wait()
+
+        def rows(step, carry):
+            here = pl.ds(pl.multiple_of(step * 128, 128), 128)
+            staging[slot, here] = loaded[slot, here].astype(F32)
+            return carry
+
+        lax.fori_loop(0, 4, rows, 0)
+        stores[slot].start()
+
+    some = len(blocks) // 2
+    for slot in range(some):
+        widen(slot)
+    for index, (out, tokens) in enumerate(zip(byte_outs, (out3, grad3))):
         length, width = out.shape[0] // 3, out.shape[1]
         for block in range(width // 128):
             for part in range(3):
                 start = part * width + block * 128
                 mixing[block, pl.ds(part, length, stride=3), :] = tokens[:, start : start + 128].astype(F32)
-            out[:, block * 128 : (block + 1) * 128] = mixing[block].astype(BF16)
-    for slot in range(len(blocks)):
-        loads[slot].wait()
-
-        def widen(step, carry, slot=slot):
-            here = pl.ds(pl.multiple_of(step * 64, 64), 64)
-            staging[slot, here] = loaded[slot, here].astype(F32)
-            return carry
-
-        lax.fori_loop(0, 8, widen, 0)
-        stores[slot].start()
-    for out, (start, count) in zip(narrow_outs, NARROW):
-        for block in range(count):
-            out[:, block * 512 : (block + 1) * 512] = small[start + block : start + block + 1]
+            bytes_low[index, :, block * 128 : (block + 1) * 128] = mixing[block].astype(BF16)
+        store = pltpu.make_async_copy(bytes_low.at[index], out, sems.at[len(blocks) + index])
+        store.start()
+        stores.append(store)
+    for slot in range(some, len(blocks)):
+        widen(slot)
     for store in stores:
         store.wait()
 
@@ -1350,21 +1365,23 @@
     length, width = out3.shape[0], out3.shape[1] // 3
     vmem = pl.BlockSpec(memory_space=pltpu.VMEM)
     shapes = [(512, 512 * blocks) if across else (512 * blocks, 512) for _, blocks, across in WIDENED]
-    narrow = [(1, 512 * blocks) for _, blocks in NARROW]
+    narrow = [(512 * blocks,) if blocks == 3 else (1, 512 * blocks) for _, blocks in NARROW]
     count = sum(blocks for _, blocks, _ in WIDENED)
     outs = pl.pallas_call(
         last_kernel,
         in_specs=[pl.BlockSpec(memory_space=pl.ANY)] * 2 + [vmem] * 3,
-        out_specs=[pl.BlockSpec(memory_space=pl.ANY)] * len(shapes) + [vmem] * (len(narrow) + 2),
+        out_specs=[pl.BlockSpec(memory_space=pl.ANY)] * len(shapes)
+        + [vmem] * len(narrow)
+        + [pl.BlockSpec(memory_space=pl.ANY)] * 2,
         out_shape=[jax.ShapeDtypeStruct(shape, F32) for shape in shapes + narrow]
         + [jax.ShapeDtypeStruct((3 * length, width), BF16)] * 2,
         scratch_shapes=[
             pltpu.VMEM((count, 512, 512), BF16), pltpu.VMEM((count, 512, 512), F32), pltpu.VMEM((width // 128, 3 * length, 128), F32),
-            pltpu.SemaphoreType.DMA((count,)), pltpu.SemaphoreType.DMA((count,)),
+            pltpu.VMEM((2, 3 * length, width), BF16), pltpu.SemaphoreType.DMA((count,)), pltpu.SemaphoreType.DMA((count + 2,)),
         ],
         compiler_params=pltpu.CompilerParams(vmem_limit_bytes=56 * 2**20),
     )(early, late, out3, grad3, small)
-    return outs[: len(shapes)], [out[0] for out in outs[len(shapes) : -2]], outs[-2:]
+    return outs[: len(shapes)], [out if out.ndim == 1 else out[0] for out in outs[len(shapes) : -2]], outs[-2:]
 
 
 def fused_body(
@@ -1385,9 +1402,9 @@
     )
     vectors = dict(
         pool_b=pool_bias, ln1_g=ln1_gain, ln1_b=ln1_bias, content=content_bias, pos=pos_bias, ln2_g=ln2_gain,
-        ln2_b=ln2_bias, ffn_in_b=ffn_in_bias, ffn_out_b=ffn_out_bias, up_b=up_bias,
-    )
-    vectors = {name: vector[None] for name, vector in vectors.items()} | dict(sines=sines, cosines=cosines)
+        ln2_b=ln2_bias, ffn_in_b=ffn_in_bias, ffn_out_b=ffn_out_bias,
+    )
+    vectors = {name: vector[None] for name, vector in vectors.items()} | dict(up_flat=up_bias, sines=sines, cosines=cosines)
     vmem = pl.BlockSpec(memory_space=pltpu.VMEM)
     outs = dict(
         out3=((length, 3 * width), BF16), grad3=((length, 3 * width), BF16), small=((SMALL_ROWS, 512), F32),
@@ -1408,7 +1425,7 @@
     full = dict(
         mixing=(width // 128, 3 * length, 128), pooled=block, grad_final=block, grad_act=wide, score=(tokens // TILE, length, TILE), att=(rounds, length, PAIR),
         mixed=block, dkv=(tokens, PAIR), dhead=(width, HEAD), dbias=(8, HEAD), near=(length, PAIR), far=block,
-        small_in=(7, SMALL_ROWS, 512),
+        small_in=(7, SMALL_ROWS, 512), up_b=(1, 3 * width),
     )
     scratch |= {name: pltpu.VMEM(shape, BF16) for name, shape in low.items()}
     scratch |= {name: pltpu.VMEM(shape, F32) for name, shape in full.items()}

time: 178 us -> 176 us (0.989)
  no operation moved by 1% of the time
where the time goes in v6:
time: 176 us
  Pallas kernels  175 us (99%)
    pallas_call x1, Pallas kernels, fused_body(): pl.pallas_call(functools.partial(layer_kernel, n, length, layout), in_spe...  163 us
    pallas_call x1, Pallas kernels, finished(): pl.pallas_call(last_kernel, in_specs=[pl.BlockSpec(memory_space=pl.ANY)]...  12 us

profile of v6, /device:TPU:0, one launch (start us, length us, event | category | flops | bytes accessed | tf_op | source)
XLA Modules:
  0.0 175.9 jit_solution(8539548398490679639)
XLA Ops:
  0.7 163.1 %shard_map.400 = (bf16[192,1536]{1,0:T(8,128)(2,1)}, bf16[192,1536]{1,0:T(8,128)(2,1)}, f32[16,512]{1,0:T(8,128)}, bf16[6144,512]{1,0:T(8,128)(2,1)}, bf16[3584,512]{1,0:T(8,128)(2,1)}) custom-call(bf16[576,512]{1,0:T(8,128)(2,1)} %bitcast.22, bf16[1536,512]{1,0:T(8,128)(2,1)} %refs_1_.1, bf16[512,512]{1,0:T(8,128)(2,1)} %refs_2_.1, ...), custom_call_target="tpu_custom_call" | custom-call | tf_op jit(solution)/shard_map/pallas_call | solution.py:1440
  163.7 12.0 %shard_map.401 = (f32[512,2048]{1,0:T(8,128)}, f32[2048,512]{1,0:T(8,128)}, f32[512,1536]{1,0:T(8,128)}, f32[512,512]{1,0:T(8,128)}, f32[1536,512]{1,0:T(8,128)}...) custom-call(bf16[6144,512]{1,0:T(8,128)(2,1)} %get-tuple-element.47., ...), custom_call_target="tpu_custom_call" | custom-call | tf_op jit(solution)/shard_map/pallas_call | solution.py:1370

commit v7 on v6

--- a/solution.py
+++ b/solution.py
@@ -33,11 +33,11 @@
 
 def place_of(block, group):
     turn, spot = block // group, block % group
-    return turn, jnp.where(turn % 2 == 0, spot, group - 1 - spot)
+    return turn, jnp.where((turn + turn // 4) % 2 == 0, spot, group - 1 - spot)
 
 
 def block_of(turn, member, group):
-    return turn * group + jnp.where(turn % 2 == 0, member, group - 1 - member)
+    return turn * group + jnp.where((turn + turn // 4) % 2 == 0, member, group - 1 - member)
 
 
 def whereabouts(group):
@@ -601,7 +601,7 @@
 LATE_CHUNKS = ((3072, 512, False), (1536, 1024, False), (2560, 512, True), (0, 1024, False), (1024, 512, True))
 QKV_SUMS, POOL_SUMS = slice(4, 6), slice(6, None)
 SMALL_ROWS = 16
-TILE = 512
+TILE = 768
 OVER_ROWS = ((0,), (0,))
 OVER_COLUMNS = ((1,), (1,))
 
@@ -889,14 +889,15 @@
         to_chip, _ = chip_of(core, h, 0, group)
         sems = (r.send_sem.at[1], r.kv_sem.at[chip])
         kv_jobs.append((r.kv_out.at[h], r.kv.at[rows_in(chip)], sems, chip % 2, to_chip))
-    first_jobs = kv_jobs + q_jobs(r.q_out, r.q, r.send_sem.at[0], r.q_sem)
-    for job in first_jobs:
+    query_jobs = q_jobs(r.q_out, r.q, r.send_sem.at[0], r.q_sem)
+    for job in kv_jobs + query_jobs:
         send(*job)
 
     ready(r.ct_bytes, r.up_w, r.ffn_out)
     tokens_of(r.ct_bytes, r.ct3)
     grad_final = dot(r.ct3[...], r.up_w[...], OVER_COLUMNS)
     r.grad_final[...] = grad_final
+    first_jobs = kv_jobs + query_jobs
     grad_branch = grad_final.astype(BF16)
     r.grad_branch[...] = grad_branch
     for part in range(4):
@@ -946,21 +947,35 @@
         arrived(r.kv.at[rows_in(at)], r.kv_sem.at[at])
         forward(turn).start()
 
+    def met(turn):
+        other = turn * group + 1 - core
+        arrived(r.kv.at[rows_in(other)], r.kv_sem.at[other])
+
+    rising = row == 0
     pass_on(0)
     pass_on(1)
-    arrived(r.kv.at[rows_in(1 - core)], r.kv_sem.at[1 - core])
-
-    def attend(turn, carry):
+
+    @pl.when(jnp.logical_not(rising))
+    def _():
+        lax.fori_loop(2, rounds, lambda turn, carry: (pass_on(turn), carry)[1], 0)
+
+    met(0)
+
+    @pl.when(jnp.logical_not(rising))
+    def _():
+        lax.fori_loop(1, rounds, lambda turn, carry: (met(turn), carry)[1], 0)
+
+    def attend(index, carry):
+        turn = jnp.where(rising, index, rounds - 1 - index)
         block = block_of(turn, member, group)
 
-        @pl.when(turn < rounds - 2)
+        @pl.when(jnp.logical_and(rising, index < rounds - 2))
         def _():
-            pass_on(turn + 2)
-
-        @pl.when(turn < rounds - 1)
+            pass_on(index + 2)
+
+        @pl.when(jnp.logical_and(rising, index < rounds - 1))
         def _():
-            other = (turn + 1) * group + 1 - core
-            arrived(r.kv.at[rows_in(other)], r.kv_sem.at[other])
+            met(index + 1)
 
         arrived(r.q.at[turn], r.q_sem.at[turn])
         query_u, _, turned = query_parts(

time: 176 us -> 175 us (level)
  no operation moved by 1% of the time
where the time goes in v7:
time: 175 us
  Pallas kernels  174 us (99%)
    pallas_call x1, Pallas kernels, fused_body(): pl.pallas_call(functools.partial(layer_kernel, n, length, layout), in_spe...  162 us
    pallas_call x1, Pallas kernels, finished(): pl.pallas_call(last_kernel, in_specs=[pl.BlockSpec(memory_space=pl.ANY)]...  12 us

profile of v7, /device:TPU:0, one launch (start us, length us, event | category | flops | bytes accessed | tf_op | source)
XLA Modules:
  0.0 174.8 jit_solution(7832832488788809896)
XLA Ops:
  0.7 162.0 %shard_map.400 = (bf16[192,1536]{1,0:T(8,128)(2,1)}, bf16[192,1536]{1,0:T(8,128)(2,1)}, f32[16,512]{1,0:T(8,128)}, bf16[6144,512]{1,0:T(8,128)(2,1)}, bf16[3584,512]{1,0:T(8,128)(2,1)}) custom-call(bf16[576,512]{1,0:T(8,128)(2,1)} %bitcast.22, bf16[1536,512]{1,0:T(8,128)(2,1)} %refs_1_.1, bf16[512,512]{1,0:T(8,128)(2,1)} %refs_2_.1, ...), custom_call_target="tpu_custom_call" | custom-call | tf_op jit(solution)/shard_map/pallas_call | solution.py:1455
  162.6 12.0 %shard_map.401 = (f32[512,2048]{1,0:T(8,128)}, f32[2048,512]{1,0:T(8,128)}, f32[512,1536]{1,0:T(8,128)}, f32[512,512]{1,0:T(8,128)}, f32[1536,512]{1,0:T(8,128)}...) custom-call(bf16[6144,512]{1,0:T(8,128)(2,1)} %get-tuple-element.47., ...), custom_call_target="tpu_custom_call" | custom-call | tf_op jit(solution)/shard_map/pallas_call | solution.py:1385

commit v8 on v7

--- a/solution.py
+++ b/solution.py
@@ -1106,10 +1106,7 @@
         early[4096 + part * width : 4096 + (part + 1) * width] = dot(final_low, r.ct3[:, at], OVER_ROWS).astype(BF16)
     sums[2].step(0)
     steps_at(-2)
-    for part in range(3):
-        at = slice(part * width, (part + 1) * width)
-        lifted = dot(final_low, r.up_w[:, at]) + r.up_b[:, at]
-        r.out3[:, at] = (r.x3[:, at].astype(F32) + lifted).astype(BF16)
+    r.att_low[...] = final_low
 
     steps_at(-1)
 
@@ -1217,6 +1214,10 @@
     for turn in range(rounds):
         sent(r.dkv_out.at[turn * group + core], r.send_sem.at[4], row, turn * group + core)
         give_over(turn).wait_send()
+    for part in range(3):
+        at = slice(part * width, (part + 1) * width)
+        lifted = dot(r.att_low[...], r.up_w[:, at]) + r.up_b[:, at]
+        r.out3[:, at] = (r.x3[:, at].astype(F32) + lifted).astype(BF16)
     arrived(r.dq_in, r.dq_sem.at[0])
     arrived(r.dkv_in, r.dkv_sem.at[0])
     grad_query = joined(lambda h: r.dq_in[h].astype(F32)).astype(BF16)

time: 175 us -> 175 us (level)
  no operation moved by 1% of the time
where the time goes in v8:
time: 175 us
  Pallas kernels  174 us (99%)
    pallas_call x1, Pallas kernels, fused_body(): pl.pallas_call(functools.partial(layer_kernel, n, length, layout), in_spe...  162 us
    pallas_call x1, Pallas kernels, finished(): pl.pallas_call(last_kernel, in_specs=[pl.BlockSpec(memory_space=pl.ANY)]...  12 us

profile of v8, /device:TPU:0, one launch (start us, length us, event | category | flops | bytes accessed | tf_op | source)
XLA Modules:
  0.0 174.7 jit_solution(10050349985119362581)
XLA Ops:
  0.7 161.8 %shard_map.400 = (bf16[192,1536]{1,0:T(8,128)(2,1)}, bf16[192,1536]{1,0:T(8,128)(2,1)}, f32[16,512]{1,0:T(8,128)}, bf16[6144,512]{1,0:T(8,128)(2,1)}, bf16[3584,512]{1,0:T(8,128)(2,1)}) custom-call(bf16[576,512]{1,0:T(8,128)(2,1)} %bitcast.22, bf16[1536,512]{1,0:T(8,128)(2,1)} %refs_1_.1, bf16[512,512]{1,0:T(8,128)(2,1)} %refs_2_.1, ...), custom_call_target="tpu_custom_call" | custom-call | tf_op jit(solution)/shard_map/pallas_call | solution.py:1456
  162.5 12.0 %shard_map.401 = (f32[512,2048]{1,0:T(8,128)}, f32[2048,512]{1,0:T(8,128)}, f32[512,1536]{1,0:T(8,128)}, f32[512,512]{1,0:T(8,128)}, f32[1536,512]{1,0:T(8,128)}...) custom-call(bf16[6144,512]{1,0:T(8,128)(2,1)} %get-tuple-element.47., ...), custom_call_target="tpu_custom_call" | custom-call | tf_op jit(solution)/shard_map/pallas_call | solution.py:1386
